TPU v7x, 32 devices: a whole 2x2x4 slice. The times are simulated.
32 devices in a mesh: dp: 8 (over z, x), mp: 4 (over y, core).
Axes of the slice: x: 2, y: 2, z: 4, core: 2. Of those that a mesh axis runs over, the one named last changes fastest.
Arguments:
- tokens: bfloat16 [8192, 2048], P(('dp', 'mp')), may hold values from -6 to 6
- cotangent: bfloat16 [8192, 2048], P(('dp', 'mp'))
- group_ids: int32 [8], P('dp'), may hold values from 0 to 5
- group_scales: float32 [6], replicated, may hold values from 0.5 to 2
- gains: float32 [2, 2048], replicated
- gains_first: float32 [2, 2048], replicated, may hold values from -0.00024414062 to 0.00024414062
- gains_second: float32 [2, 2048], replicated, may hold values from 1.0219479e-09 to 4.08002e-09
- taps: float32 [3, 3, 2048], replicated, may hold values from -1 to 1
- taps_first: float32 [3, 3, 2048], replicated, may hold values from -0.00024414062 to 0.00024414062
- taps_second: float32 [3, 3, 2048], replicated, may hold values from 1.0219479e-09 to 4.08002e-09
- residues: float32 [16, 2048], replicated
- residues_first: float32 [16, 2048], replicated, may hold values from -0.00024414062 to 0.00024414062
- residues_second: float32 [16, 2048], replicated, may hold values from 1.0219479e-09 to 4.08002e-09
- log_rates: float32 [16, 2048], replicated
- log_rates_first: float32 [16, 2048], replicated, may hold values from -0.00024414062 to 0.00024414062
- log_rates_second: float32 [16, 2048], replicated, may hold values from 1.0219479e-09 to 4.08002e-09
- skip: float32 [2048], replicated, may hold values from 0.5 to 1.5
- skip_first: float32 [2048], replicated, may hold values from -0.00024414062 to 0.00024414062
- skip_second: float32 [2048], replicated, may hold values from 1.0219479e-09 to 4.08002e-09
- in_weight: float32 [2048, 3, 2048], P('dp', None, 'mp'), may hold values from -0.125 to 0.125
- in_weight_first: float32 [2048, 3, 2048], P('dp', None, 'mp'), may hold values from -0.00024414062 to 0.00024414062
- in_weight_second: float32 [2048, 3, 2048], P('dp', None, 'mp'), may hold values from 1.0219479e-09 to 4.08002e-09
- out_weight: float32 [2048, 2048], P('mp', 'dp'), may hold values from -0.125 to 0.125
- out_weight_first: float32 [2048, 2048], P('mp', 'dp'), may hold values from -0.00024414062 to 0.00024414062
- out_weight_second: float32 [2048, 2048], P('mp', 'dp'), may hold values from 1.0219479e-09 to 4.08002e-09
- gate_weight: float32 [2048, 5632], P('dp', 'mp'), may hold values from -0.125 to 0.125
- gate_weight_first: float32 [2048, 5632], P('dp', 'mp'), may hold values from -0.00024414062 to 0.00024414062
- gate_weight_second: float32 [2048, 5632], P('dp', 'mp'), may hold values from 2.564584e-10 to 1.0219479e-09
- up_weight: float32 [2048, 5632], P('dp', 'mp'), may hold values from -0.125 to 0.125
- up_weight_first: float32 [2048, 5632], P('dp', 'mp'), may hold values from -0.00024414062 to 0.00024414062
- up_weight_second: float32 [2048, 5632], P('dp', 'mp'), may hold values from 2.564584e-10 to 1.0219479e-09
- down_weight: float32 [5632, 2048], P('mp', 'dp'), may hold values from -0.078125 to 0.078125
- down_weight_first: float32 [5632, 2048], P('mp', 'dp'), may hold values from -0.00024414062 to 0.00024414062
- down_weight_second: float32 [5632, 2048], P('mp', 'dp'), may hold values from 1.0219479e-09 to 4.08002e-09
Outputs:
- output: bfloat16 [8192, 2048], P(('dp', 'mp'))
- input_grad: bfloat16 [8192, 2048], P(('dp', 'mp'))
- radial_grad: float32 [8192], P(('dp', 'mp'))
- gains_new: float32 [2, 2048], replicated
- gains_first_new: float32 [2, 2048], replicated
- gains_second_new: float32 [2, 2048], replicated
- taps_new: float32 [3, 3, 2048], replicated
- taps_first_new: float32 [3, 3, 2048], replicated
- taps_second_new: float32 [3, 3, 2048], replicated
- residues_new: float32 [16, 2048], replicated
- residues_first_new: float32 [16, 2048], replicated
- residues_second_new: float32 [16, 2048], replicated
- log_rates_new: float32 [16, 2048], replicated
- log_rates_first_new: float32 [16, 2048], replicated
- log_rates_second_new: float32 [16, 2048], replicated
- skip_new: float32 [2048], replicated
- skip_first_new: float32 [2048], replicated
- skip_second_new: float32 [2048], replicated
- in_weight_new: float32 [2048, 3, 2048], P('dp', None, 'mp')
- in_weight_first_new: float32 [2048, 3, 2048], P('dp', None, 'mp')
- in_weight_second_new: float32 [2048, 3, 2048], P('dp', None, 'mp')
- out_weight_new: float32 [2048, 2048], P('mp', 'dp')
- out_weight_first_new: float32 [2048, 2048], P('mp', 'dp')
- out_weight_second_new: float32 [2048, 2048], P('mp', 'dp')
- gate_weight_new: float32 [2048, 5632], P('dp', 'mp')
- gate_weight_first_new: float32 [2048, 5632], P('dp', 'mp')
- gate_weight_second_new: float32 [2048, 5632], P('dp', 'mp')
- up_weight_new: float32 [2048, 5632], P('dp', 'mp')
- up_weight_first_new: float32 [2048, 5632], P('dp', 'mp')
- up_weight_second_new: float32 [2048, 5632], P('dp', 'mp')
- down_weight_new: float32 [5632, 2048], P('mp', 'dp')
- down_weight_first_new: float32 [5632, 2048], P('mp', 'dp')
- down_weight_second_new: float32 [5632, 2048], P('mp', 'dp')
- grad_norm: float32 [], replicated
All inputs are finite; a program needn't handle non-finite values.
Results may differ from a plain program's by a relative error of at most 0.024.
Values may be sent and summed in bfloat16 or wider, within the bound.
No kernel may reach another device: no remote copies, remote signals or barrier semaphores. Data moves between devices by JAX's collectives and lax.ppermute only.
A program may use at most 320 MiB of HBM per device.

v0:
```python
import math

import jax
import jax.numpy as jnp
from jax import lax
from jax.sharding import PartitionSpec as P

STEP = 10


EPSILON = 1e-05
CLIP = 1.0
BETA_ONE = 0.9
BETA_TWO = 0.95
ADAM_EPSILON = 1e-08
DECAY = 0.1
RATE_MATRIX = 0.05
RATE_SMALL = 0.5
RATE_RATES = 4.0
HIGHEST = lax.Precision.HIGHEST


def factor_pair(size):
    leading = 1
    while leading * 2 * (leading * 2) <= size and size % (leading * 2) == 0:
        leading = leading * 2
    return (leading, size // leading)


def angle_table(rows, cols, modulus):
    product = (
        lax.broadcasted_iota(jnp.int32, (rows, cols), 0)
        * lax.broadcasted_iota(jnp.int32, (rows, cols), 1)
        % modulus
    )
    phase = product.astype(jnp.float32) * (2.0 * math.pi / modulus)
    return (jnp.cos(phase), jnp.sin(phase))


def dft_tables(size):
    leading, trailing = factor_pair(size)
    return (
        angle_table(leading, leading, leading),
        angle_table(leading, trailing, size),
        angle_table(trailing, trailing, trailing),
    )


def along_forward(values, table):
    return jnp.einsum("anc,nk->akc", values, table, precision=HIGHEST)


def along_inverse(values, table):
    return jnp.einsum("akc,nk->anc", values, table, precision=HIGHEST)


def spectrum(signal, tables):
    (cos_lead, sin_lead), (cos_turn, sin_turn), (cos_trail, sin_trail) = tables
    leading, trailing = cos_turn.shape
    width = signal.shape[1]
    padded = jnp.concatenate([signal, jnp.zeros_like(signal)], axis=0).reshape(
        leading, trailing * width
    )
    real_one = jnp.dot(cos_lead, padded, precision=HIGHEST).reshape(leading, trailing, width)
    imag_one = -jnp.dot(sin_lead, padded, precision=HIGHEST).reshape(leading, trailing, width)
    cos_twist = cos_turn[:, :, None]
    sin_twist = sin_turn[:, :, None]
    real_two = real_one * cos_twist + imag_one * sin_twist
    imag_two = imag_one * cos_twist - real_one * sin_twist
    real_out = along_forward(real_two, cos_trail) + along_forward(imag_two, sin_trail)
    imag_out = along_forward(imag_two, cos_trail) - along_forward(real_two, sin_trail)
    return (real_out, imag_out)


def signal_of(real_in, imag_in, tables):
    (cos_lead, sin_lead), (cos_turn, sin_turn), (cos_trail, sin_trail) = tables
    leading, trailing = cos_turn.shape
    width = real_in.shape[2]
    real_one = along_inverse(real_in, cos_trail) - along_inverse(imag_in, sin_trail)
    imag_one = along_inverse(imag_in, cos_trail) + along_inverse(real_in, sin_trail)
    cos_twist = cos_turn[:, :, None]
    sin_twist = sin_turn[:, :, None]
    real_two = (real_one * cos_twist - imag_one * sin_twist).reshape(leading, trailing * width)
    imag_two = (imag_one * cos_twist + real_one * sin_twist).reshape(leading, trailing * width)
    result = jnp.dot(cos_lead, real_two, precision=HIGHEST) - jnp.dot(
        sin_lead, imag_two, precision=HIGHEST
    )
    size = leading * trailing
    return (result / size).reshape(size, width)[: size // 2]


def contract_rows(left, right):
    return lax.dot_general(
        left, right, (((0,), (0,)), ((), ())), preferred_element_type=jnp.float32
    )


def against_rows(left, right):
    return lax.dot_general(
        left, right, (((1,), (1,)), ((), ())), preferred_element_type=jnp.float32
    )


def short_conv(values, kernel):
    length = values.shape[0]
    result = kernel[0] * values
    for offset in range(1, kernel.shape[0]):
        shifted = jnp.pad(values, ((offset, 0), (0, 0), (0, 0)))[:length]
        result = result + kernel[offset] * shifted
    return result


def norm_back(values, scale, gain, grad):
    weighted = grad * gain
    inner_mean = jnp.mean(values * weighted, axis=1, keepdims=True)
    return (
        scale * weighted - values * (scale * scale * scale) * inner_mean,
        jnp.sum(grad * values * scale, axis=0),
    )


def adam(weight, first, second, grad, rate, decay):
    first_new = BETA_ONE * first + (1.0 - BETA_ONE) * grad
    second_new = BETA_TWO * second + (1.0 - BETA_TWO) * grad * grad
    stride = (
        first_new
        / (1.0 - BETA_ONE**STEP)
        / (jnp.sqrt(second_new / (1.0 - BETA_TWO**STEP)) + ADAM_EPSILON)
    )
    return (weight - rate * (stride + decay * weight), first_new, second_new)


def on_device(
    tokens,
    cotangent,
    group_ids,
    group_scales,
    gains,
    gains_first,
    gains_second,
    taps,
    taps_first,
    taps_second,
    residues,
    residues_first,
    residues_second,
    log_rates,
    log_rates_first,
    log_rates_second,
    skip,
    skip_first,
    skip_second,
    in_weight,
    in_weight_first,
    in_weight_second,
    out_weight,
    out_weight_first,
    out_weight_second,
    gate_weight,
    gate_weight_first,
    gate_weight_second,
    up_weight,
    up_weight_first,
    up_weight_second,
    down_weight,
    down_weight_first,
    down_weight_second,
):
    rows = tokens.shape[0]
    model = tokens.shape[1]
    length = rows * lax.axis_size("mp")
    channels = in_weight.shape[2]
    begin = lax.axis_index("mp") * channels
    in_full, out_full, gate_full, up_full, down_full = (
        lax.all_gather(in_weight.astype(jnp.bfloat16), "dp", axis=0, tiled=True),
        lax.all_gather(out_weight.astype(jnp.bfloat16), "dp", axis=1, tiled=True),
        lax.all_gather(gate_weight.astype(jnp.bfloat16), "dp", axis=0, tiled=True),
        lax.all_gather(up_weight.astype(jnp.bfloat16), "dp", axis=0, tiled=True),
        lax.all_gather(down_weight.astype(jnp.bfloat16), "dp", axis=1, tiled=True),
    )
    in_flat = in_full.reshape(model, 3 * channels)

    def own(array):
        return lax.dynamic_slice_in_dim(array, begin, channels, array.ndim - 1)

    taps_own = own(taps)
    residues_own = own(residues)
    rates_own = jnp.exp(own(log_rates))
    skip_own = own(skip)
    resid = tokens.astype(jnp.float32)
    scale_one = lax.rsqrt(jnp.mean(resid * resid, axis=1, keepdims=True) + EPSILON)
    normed = (resid * scale_one * gains[0]).astype(jnp.bfloat16)
    normed_all = lax.all_gather(normed, "mp", axis=0, tiled=True)
    proj = jnp.dot(normed_all, in_flat, preferred_element_type=jnp.float32).reshape(
        length, 3, channels
    )
    mixed = short_conv(proj, taps_own)
    query, key, value = (mixed[:, 0], mixed[:, 1], mixed[:, 2])
    gated = key * value
    positions = jnp.arange(length, dtype=jnp.float32)
    decays = jnp.exp(-positions[:, None, None] * rates_own[None])
    filt = jnp.sum(decays * residues_own[None], axis=1)
    tables = dft_tables(2 * length)
    filt_real, filt_imag = spectrum(filt, tables)
    gated_real, gated_imag = spectrum(gated, tables)
    conv = (
        signal_of(
            filt_real * gated_real - filt_imag * gated_imag,
            filt_real * gated_imag + filt_imag * gated_real,
            tables,
        )
        + skip_own * gated
    )
    branch = (query * conv).astype(jnp.bfloat16)
    middle = resid + lax.psum_scatter(
        jnp.dot(branch, out_full, preferred_element_type=jnp.float32).astype(jnp.bfloat16),
        "mp",
        scatter_dimension=0,
        tiled=True,
    ).astype(jnp.float32)
    scale_two = lax.rsqrt(jnp.mean(middle * middle, axis=1, keepdims=True) + EPSILON)
    normed_two = (middle * scale_two * gains[1]).astype(jnp.bfloat16)
    normed_two_all = lax.all_gather(normed_two, "mp", axis=0, tiled=True)
    gate = jnp.dot(normed_two_all, gate_full, preferred_element_type=jnp.float32)
    up = jnp.dot(normed_two_all, up_full, preferred_element_type=jnp.float32)
    sigma = jax.nn.sigmoid(gate)
    silu = gate * sigma
    inner = (silu * up).astype(jnp.bfloat16)
    output = (
        middle
        + lax.psum_scatter(
            jnp.dot(inner, down_full, preferred_element_type=jnp.float32).astype(jnp.bfloat16),
            "mp",
            scatter_dimension=0,
            tiled=True,
        ).astype(jnp.float32)
    ).astype(jnp.bfloat16)
    sequence_scale = jnp.sum(
        jnp.where(
            group_ids[:, None] == jnp.arange(group_scales.shape[0], dtype=jnp.int32)[None, :],
            group_scales[None, :],
            0.0,
        )
    )
    back_all = lax.all_gather(cotangent, "mp", axis=0, tiled=True)
    grad_down = sequence_scale * contract_rows(inner, back_all)
    grad_inner = sequence_scale * against_rows(back_all, down_full)
    grad_gate = (grad_inner * up * sigma * (1.0 + gate * (1.0 - sigma))).astype(jnp.bfloat16)
    grad_up = (grad_inner * silu).astype(jnp.bfloat16)
    grad_w_gate = contract_rows(normed_two_all, grad_gate)
    grad_w_up = contract_rows(normed_two_all, grad_up)
    grad_normed_two = lax.psum_scatter(
        (against_rows(grad_gate, gate_full) + against_rows(grad_up, up_full)).astype(jnp.bfloat16),
        "mp",
        scatter_dimension=0,
        tiled=True,
    ).astype(jnp.float32)
    grad_from_norm, gain_two = norm_back(middle, scale_two, gains[1], grad_normed_two)
    grad_middle = cotangent.astype(jnp.float32) * sequence_scale + grad_from_norm
    grad_middle_all = lax.all_gather(grad_middle.astype(jnp.bfloat16), "mp", axis=0, tiled=True)
    grad_w_out = contract_rows(branch, grad_middle_all)
    grad_branch = against_rows(grad_middle_all, out_full)
    grad_query = grad_branch * conv
    grad_conv = grad_branch * query
    back_real, back_imag = spectrum(grad_conv, tables)
    grad_gated = (
        signal_of(
            back_real * filt_real + back_imag * filt_imag,
            back_imag * filt_real - back_real * filt_imag,
            tables,
        )
        + skip_own * grad_conv
    )
    grad_filt = signal_of(
        back_real * gated_real + back_imag * gated_imag,
        back_imag * gated_real - back_real * gated_imag,
        tables,
    )
    grad_skip = jnp.sum(grad_conv * gated, axis=0)
    weighted_decays = grad_filt[:, None, :] * decays
    grad_residues = jnp.sum(weighted_decays, axis=0)
    grad_log_rates = (
        -rates_own * residues_own * jnp.sum(weighted_decays * positions[:, None, None], axis=0)
    )
    grad_mixed = jnp.stack([grad_query, grad_gated * value, grad_gated * key], axis=1)
    tap_grads = [jnp.sum(grad_mixed * proj, axis=0)]
    grad_proj = taps_own[0] * grad_mixed
    for offset in range(1, taps_own.shape[0]):
        shifted = jnp.pad(proj, ((offset, 0), (0, 0), (0, 0)))[:length]
        tap_grads.append(jnp.sum(grad_mixed * shifted, axis=0))
        ahead = jnp.pad(grad_mixed, ((0, offset), (0, 0), (0, 0)))[offset:]
        grad_proj = grad_proj + taps_own[offset] * ahead
    grad_taps = jnp.stack(tap_grads, axis=0)
    grad_proj_low = grad_proj.astype(jnp.bfloat16).reshape(length, 3 * channels)
    grad_w_in = contract_rows(normed_all, grad_proj_low).reshape(model, 3, channels)
    grad_normed = lax.psum_scatter(
        against_rows(grad_proj_low, in_flat).astype(jnp.bfloat16),
        "mp",
        scatter_dimension=0,
        tiled=True,
    ).astype(jnp.float32)
    grad_from_first, gain_one = norm_back(resid, scale_one, gains[0], grad_normed)
    grad_input = grad_middle + grad_from_first
    input_grad = grad_input.astype(jnp.bfloat16)
    radial_grad = scale_one[:, 0] * jnp.sum(resid * grad_input, axis=1) / model**0.5

    def place(part, whole):
        return lax.dynamic_update_slice_in_dim(
            jnp.zeros(whole.shape, jnp.float32), part, begin, part.ndim - 1
        )

    small = lax.psum(
        (
            jnp.stack([gain_one, gain_two], axis=0),
            place(grad_taps, taps),
            place(grad_residues, residues),
            place(grad_log_rates, log_rates),
            place(grad_skip, skip),
        ),
        ("dp", "mp"),
    )
    shards = (
        lax.psum_scatter(
            grad_w_in.astype(jnp.bfloat16), "dp", scatter_dimension=0, tiled=True
        ).astype(jnp.float32),
        lax.psum_scatter(
            grad_w_out.astype(jnp.bfloat16), "dp", scatter_dimension=1, tiled=True
        ).astype(jnp.float32),
        lax.psum_scatter(
            grad_w_gate.astype(jnp.bfloat16), "dp", scatter_dimension=0, tiled=True
        ).astype(jnp.float32),
        lax.psum_scatter(
            grad_w_up.astype(jnp.bfloat16), "dp", scatter_dimension=0, tiled=True
        ).astype(jnp.float32),
        lax.psum_scatter(
            grad_down.astype(jnp.bfloat16), "dp", scatter_dimension=1, tiled=True
        ).astype(jnp.float32),
    )
    square_big = sum((jnp.sum(grad * grad) for grad in shards))
    square_total = lax.psum(square_big, ("dp", "mp")) + sum(
        (jnp.sum(grad * grad) for grad in small)
    )
    grad_norm = jnp.sqrt(square_total)
    factor = jnp.minimum(1.0, CLIP / (grad_norm + 1e-06))
    gains_new, gains_first_new, gains_second_new = adam(
        gains, gains_first, gains_second, small[0] * factor, RATE_SMALL, 0.0
    )
    taps_new, taps_first_new, taps_second_new = adam(
        taps, taps_first, taps_second, small[1] * factor, RATE_SMALL, 0.0
    )
    residues_new, residues_first_new, residues_second_new = adam(
        residues, residues_first, residues_second, small[2] * factor, RATE_SMALL, 0.0
    )
    log_rates_new, log_rates_first_new, log_rates_second_new = adam(
        log_rates, log_rates_first, log_rates_second, small[3] * factor, RATE_RATES, 0.0
    )
    skip_new, skip_first_new, skip_second_new = adam(
        skip, skip_first, skip_second, small[4] * factor, RATE_SMALL, 0.0
    )
    in_weight_new, in_weight_first_new, in_weight_second_new = adam(
        in_weight, in_weight_first, in_weight_second, shards[0] * factor, RATE_MATRIX, DECAY
    )
    out_weight_new, out_weight_first_new, out_weight_second_new = adam(
        out_weight, out_weight_first, out_weight_second, shards[1] * factor, RATE_MATRIX, DECAY
    )
    gate_weight_new, gate_weight_first_new, gate_weight_second_new = adam(
        gate_weight, gate_weight_first, gate_weight_second, shards[2] * factor, RATE_MATRIX, DECAY
    )
    up_weight_new, up_weight_first_new, up_weight_second_new = adam(
        up_weight, up_weight_first, up_weight_second, shards[3] * factor, RATE_MATRIX, DECAY
    )
    down_weight_new, down_weight_first_new, down_weight_second_new = adam(
        down_weight, down_weight_first, down_weight_second, shards[4] * factor, RATE_MATRIX, DECAY
    )
    return (
        output,
        input_grad,
        radial_grad,
        gains_new,
        gains_first_new,
        gains_second_new,
        taps_new,
        taps_first_new,
        taps_second_new,
        residues_new,
        residues_first_new,
        residues_second_new,
        log_rates_new,
        log_rates_first_new,
        log_rates_second_new,
        skip_new,
        skip_first_new,
        skip_second_new,
        in_weight_new,
        in_weight_first_new,
        in_weight_second_new,
        out_weight_new,
        out_weight_first_new,
        out_weight_second_new,
        gate_weight_new,
        gate_weight_first_new,
        gate_weight_second_new,
        up_weight_new,
        up_weight_first_new,
        up_weight_second_new,
        down_weight_new,
        down_weight_first_new,
        down_weight_second_new,
        grad_norm,
    )


def solution(mesh):
    return jax.shard_map(
        on_device,
        mesh=mesh,
        in_specs=(
            P(("dp", "mp"), None),
            P(("dp", "mp"), None),
            P("dp"),
            P(),
            P(),
            P(),
            P(),
            P(),
            P(),
            P(),
            P(),
            P(),
            P(),
            P(),
            P(),
            P(),
            P(),
            P(),
            P(),
            P("dp", None, "mp"),
            P("dp", None, "mp"),
            P("dp", None, "mp"),
            P("mp", "dp"),
            P("mp", "dp"),
            P("mp", "dp"),
            P("dp", "mp"),
            P("dp", "mp"),
            P("dp", "mp"),
            P("dp", "mp"),
            P("dp", "mp"),
            P("dp", "mp"),
            P("mp", "dp"),
            P("mp", "dp"),
            P("mp", "dp"),
        ),
        out_specs=(
            P(("dp", "mp"), None),
            P(("dp", "mp"), None),
            P(("dp", "mp")),
            P(),
            P(),
            P(),
            P(),
            P(),
            P(),
            P(),
            P(),
            P(),
            P(),
            P(),
            P(),
            P(),
            P(),
            P(),
            P("dp", None, "mp"),
            P("dp", None, "mp"),
            P("dp", None, "mp"),
            P("mp", "dp"),
            P("mp", "dp"),
            P("mp", "dp"),
            P("dp", "mp"),
            P("dp", "mp"),
            P("dp", "mp"),
            P("dp", "mp"),
            P("dp", "mp"),
            P("dp", "mp"),
            P("mp", "dp"),
            P("mp", "dp"),
            P("mp", "dp"),
            P(),
        ),
        check_vma=False,
    )
```

profile of v0, /device:TPU:0, one launch (start us, length us, event | category | flops | bytes accessed | tf_op | source)
XLA Modules:
  0.0 1673.7 jit_solution(4752810792248887098)
XLA Ops:
  17.0 9.5 multiply_reduce_fusion.1
  33.9 8.0 fusion.18
  41.9 5.3 fusion.20
  48.7 63.9 %all-gather.12.cloned.1.call-done = bf16[2048,3,512]{2,0,1:T(8,128)(2,1)} async-done(((bf16[256,3,512]{2,0,1:T(8,128)(2,1)}), bf16[2048,3,512]{2,0,1:T(8,128)(2,1)}) %all-gather.12.cloned.1.call-update) | async-done | bytes 6291472 | tf_op jit(solution)/shard_map/all_gather | solution.py:175
  112.6 8.9 copy.156
  121.5 25.9 %all-gather.10.cloned.1.call-done = bf16[1024,2048]{1,0:T(8,128)(2,1)} async-done(((bf16[256,2048]{1,0:T(8,128)(2,1)}), bf16[1024,2048]{1,0:T(8,128)(2,1)}) %all-gather.10.cloned.1.call-update) | async-done | bytes 4194320 | tf_op jit(solution)/shard_map/all_gather | solution.py:193
  147.4 10.3 fusion.7
  173.1 8.1 fusion.14
  181.3 10.0 multiply_add_fusion.5
  191.2 6.1 fusion.74
  197.3 6.1 fusion.76
  203.4 7.3 fusion.82
  210.7 6.1 fusion.84
  216.8 6.5 fusion.103
  223.3 6.7 fusion.100
  230.0 7.6 fusion.94
  237.6 14.2 multiply_subtract_fusion.3
  268.7 12.8 fusion.47
  293.8 5.6 multiply_convert_fusion.5
  299.4 6.2 convolution_convert_fusion.4
  308.0 42.3 %reduce-scatter.10.cloned.1.call-done = bf16[256,2048]{1,0:T(8,128)(2,1)} async-done(((bf16[1024,2048]{1,0:T(8,128)(2,1)}), bf16[256,2048]{1,0:T(8,128)(2,1)}) %reduce-scatter.10.cloned.1.call-update) | async-done | bytes 1048592 | tf_op jit(solution)/shard_map/reduce_scatter | solution.py:215
  360.3 85.5 %all-gather.20.cloned.1.call-done = bf16[2048,1408]{1,0:T(8,128)(2,1)} async-done(((bf16[256,1408]{1,0:T(8,128)(2,1)}), bf16[2048,1408]{1,0:T(8,128)(2,1)}) %all-gather.20.cloned.1.call-update) | async-done | bytes 5767184 | tf_op jit(solution)/shard_map/all_gather | solution.py:178
  445.8 34.8 %all-gather.16.cloned.1.call-done = bf16[1024,2048]{1,0:T(8,128)(2,1)} async-done(((bf16[256,2048]{1,0:T(8,128)(2,1)}), bf16[1024,2048]{1,0:T(8,128)(2,1)}) %all-gather.16.cloned.1.call-update) | async-done | bytes 4194320 | tf_op jit(solution)/shard_map/all_gather | solution.py:223
  480.6 11.8 fusion.419
  492.4 83.9 %all-gather.18.cloned.1.call-done = bf16[2048,1408]{1,0:T(8,128)(2,1)} async-done(((bf16[256,1408]{1,0:T(8,128)(2,1)}), bf16[2048,1408]{1,0:T(8,128)(2,1)}) %all-gather.18.cloned.1.call-update) | async-done | bytes 5767184 | tf_op jit(solution)/shard_map/all_gather | solution.py:177
  576.2 11.7 fusion.418
  587.9 22.7 %all-gather.24.cloned.1.call-done = bf16[1024,2048]{1,0:T(8,128)(2,1)} async-done(((bf16[256,2048]{1,0:T(8,128)(2,1)}), bf16[1024,2048]{1,0:T(8,128)(2,1)}) %all-gather.24.cloned.1.call-update) | async-done | bytes 4194320 | tf_op jit(solution)/shard_map/all_gather | solution.py:245
  610.6 96.4 %all-gather.22.cloned.1.call-done = bf16[1408,2048]{1,0:T(8,128)(2,1)} async-done(((bf16[1408,256]{1,0:T(8,128)(2,1)}), bf16[1408,2048]{1,0:T(8,128)(2,1)}) %all-gather.22.cloned.1.call-update) | async-done | bytes 5767184 | tf_op jit(solution)/shard_map/all_gather | solution.py:179
  707.0 17.0 %multiply_convert_fusion.1 = (bf16[1024,1408]{1,0:T(8,128)(2,1)}, bf16[1024,1408]{1,0:T(8,128)(2,1)S(1)}, bf16[1024,1408]{1,0:T(8,128)(2,1)}) fusion(f32[]{:T(128)} %fusion.289, f32[1024,1408]{1,0:T(8,128)} %fusion.418, f32[1024,1408]{1,0:T(8,128)} %fusion.419, bf16[1024,2048]{1,0:T(8,128)(2,1)} %all-gather.24.cloned.1.call-done, ...), kind=kOutput, calls=%fused_computation.26 | convolution fusion | flops 5928648704 | bytes 30146564 | tf_op jit(solution)/shard_map/dot_general | solution.py:99
  724.1 6.7 fusion.420
  730.8 11.4 add_convert_fusion
  742.2 11.0 convolution_convert_fusion.3
  753.3 31.7 %reduce-scatter.14.cloned.1.call-done = bf16[256,2048]{1,0:T(8,128)(2,1)} async-done(((bf16[1024,2048]{1,0:T(8,128)(2,1)}), bf16[256,2048]{1,0:T(8,128)(2,1)}) %reduce-scatter.14.cloned.1.call-update) | async-done | bytes 1048592 | tf_op jit(solution)/shard_map/reduce_scatter | solution.py:252
  787.6 44.5 %reduce-scatter.12.cloned.1.call-done = bf16[256,2048]{1,0:T(8,128)(2,1)} async-done(((bf16[1024,2048]{1,0:T(8,128)(2,1)}), bf16[256,2048]{1,0:T(8,128)(2,1)}) %reduce-scatter.12.cloned.1.call-update) | async-done | bytes 1048592 | tf_op jit(solution)/shard_map/reduce_scatter | solution.py:231
  832.1 5.3 fusion.415
  837.4 11.1 multiply_convert_fusion
  848.7 11.1 convolution_convert_fusion.1
  859.9 10.9 convolution_convert_fusion
  872.4 7.9 multiply_reduce_fusion.5
  889.2 5.8 fusion.10
  899.9 7.6 fusion.66
  907.5 6.3 fusion.68
  913.9 7.3 fusion.106
  921.2 17.0 %multiply_add_fusion.1 = (f32[64,32,512]{2,0,1:T(8,128)}, f32[64,32,512]{2,0,1:T(8,128)}, f32[64,32,512]{2,0,1:T(8,128)}, f32[64,32,512]{2,0,1:T(8,128)S(1)}) fusion(f32[64,32,512]{2,0,1:T(8,128)} %copy-done.10, f32[64,32,512]{2,0,1:T(8,128)} %fusion.106, f32[64,32,512]{2,0,1:T(8,128)} %copy-done.11, f32[64,32,512]{2,0,1:T(8,128)} %get-tuple-element.125, ...), kind=kOutput, calls=%fused_computation.108 | convolution fusion | flops 818995200 | bytes 46137344 | tf_op jit(solution)/shard_map/anc,nk->akc/dot_general | solution.py:50
  938.2 8.2 fusion.30
  946.4 5.5 fusion.32
  951.8 6.0 fusion.26
  957.8 5.5 fusion.28
  963.3 5.5 fusion.38
  968.8 5.5 fusion.40
  974.3 5.5 fusion.42
  979.8 5.5 fusion.44
  985.4 40.5 %fusion.23 = (f32[64,4,8,512]{3,2,1,0:T(8,128)}, f32[64,4,8,512]{3,2,1,0:T(8,128)}, f32[64,4,8,512]{3,2,1,0:T(8,128)}, f32[64,4,8,512]{3,2,1,0:T(8,128)}) fusion(f32[32,64]{0,1:T(8,128)S(1)} %copy-done.48, f32[32,64]{0,1:T(8,128)S(1)} %copy-done.50, f32[64,32,512]{2,0,1:T(8,128)} %fusion.28, f32[64,32,512]{2,0,1:T(8,128)} %fusion.32, ...), kind=kLoop, calls=%fused_computation.54 | loop fusion | flops 16777216 | bytes 50348032
  1065.8 9.7 multiply_reduce_fusion
  1077.2 5.9 convolution_convert_fusion.5
  1083.2 7.7 fusion.5
  1092.6 11.0 bitcast_convert_fusion
  1108.7 11.7 convolution_convert_fusion.2
  1124.9 89.1 %reduce-scatter.24.cloned.1.call-done = bf16[256,1408]{1,0:T(8,128)(2,1)} async-done(((bf16[2048,1408]{1,0:T(8,128)(2,1)}), bf16[256,1408]{1,0:T(8,128)(2,1)}) %reduce-scatter.24.cloned.1.call-update) | async-done | bytes 720912 | tf_op jit(solution)/shard_map/reduce_scatter | solution.py:332
  1216.2 132.6 %all-reduce.11.cloned.1.call-done = (f32[3,3,2048]{2,1,0:T(4,128)}, f32[16,2048]{1,0:T(8,128)}, f32[16,2048]{1,0:T(8,128)}) async-done(((f32[3,3,2048]{2,1,0:T(4,128)}, f32[16,2048]{1,0:T(8,128)}, f32[16,2048]{1,0:T(8,128)}), (f32[3,3,2048]{2,1,0:T(4,128)}, f32[16,2048]{1,0:T(8,128)}, f32[16,2048]{1,0:T(8,128)})) %all-reduce.11.cloned.1.call-update) | async-done | bytes 335888 | tf_op jit(solution)/shard_map/psum | solution.py:312
  1353.5 66.9 %reduce-scatter.20.cloned.1.call-done = bf16[512,256]{1,0:T(8,128)(2,1)} async-done(((bf16[512,2048]{1,0:T(8,128)(2,1)}), bf16[512,256]{1,0:T(8,128)(2,1)}) %reduce-scatter.20.cloned.1.call-update) | async-done | bytes 262160 | tf_op jit(solution)/shard_map/reduce_scatter | solution.py:326
  1422.1 44.2 %reduce-scatter.16.cloned.1.call-done = bf16[256,2048]{1,0:T(8,128)(2,1)} async-done(((bf16[1024,2048]{1,0:T(8,128)(2,1)}), bf16[256,2048]{1,0:T(8,128)(2,1)}) %reduce-scatter.16.cloned.1.call-update) | async-done | bytes 1048592 | tf_op jit(solution)/shard_map/reduce_scatter | solution.py:296
  1471.8 116.9 %reduce-scatter.18.cloned.1.call-done = bf16[256,3,512]{2,0,1:T(8,128)(2,1)} async-done(((bf16[2048,3,512]{2,0,1:T(8,128)(2,1)}), bf16[256,3,512]{2,0,1:T(8,128)(2,1)}) %reduce-scatter.18.cloned.1.call-update) | async-done | bytes 786448 | tf_op jit(solution)/shard_map/reduce_scatter | solution.py:323
  1594.1 40.3 %all-reduce.7 = (f32[2,2048]{1,0:T(2,128)S(1)}, f32[]{:T(128)}, f32[2048]{0:T(1024)S(1)}) all-reduce(f32[2,2048]{1,0:T(2,128)S(1)} %pad_maximum_fusion.1, f32[]{:T(128)S(6)} %add.527, f32[2048]{0:T(1024)S(1)} %dynamic_update_slice.15), channel_id=1, replica_groups=mesh['dp'=8,'mp'=4] {'dp','mp'}, use_global_device_ids=true, to_apply=%region_13.14 | all-reduce | flops 6145 | bytes 49160 | tf_op jit(solution)/shard_map/psum | solution.py:312
  (296 shorter events, 188.5 us)
Async XLA Ops:
  7.2 6.7 copy-start.36
  7.2 105.4 %all-gather.12.cloned.1.call-start = ((), (), s32[]{:S(2)}) async-start(), calls=%async_computation.10 | async-start | bytes 7077888 | tf_op jit(solution)/shard_map/all_gather | solution.py:175
  9.8 137.6 %all-gather.10.cloned.1.call-start = ((), (), s32[]{:S(2)}) async-start(), calls=%async_computation.9 | async-start | bytes 5242880 | tf_op jit(solution)/shard_map/all_gather | solution.py:193
  12.0 14.5 copy-start.70
  13.9 285.5 %all-gather.14.cloned.1.call-start = ((), (), s32[]{:S(2)}) async-start(), calls=%async_computation.11 | async-start | bytes 2359296 | tf_op jit(solution)/shard_map/all_gather | solution.py:176
  14.7 335.6 %reduce-scatter.10.cloned.1.call-start = ((), (), s32[]{:S(2)}) async-start(), calls=%async_computation.12 | async-start | bytes 5242880 | tf_op jit(solution)/shard_map/reduce_scatter | solution.py:215
  14.8 11.7 copy-start.75
  33.9 8.0 copy-start.3
  48.7 109.0 %copy-start.56 = (f32[3,512]{1,0:T(4,128)}, f32[3,512]{1,0:T(4,128)S(1)}, u32[]{:S(2)}) copy-start(f32[3,512]{1,0:T(4,128)S(1)} %get-tuple-element.112) | copy-start | bytes 18436
  48.7 109.0 %copy-start.58 = (f32[3,512]{1,0:T(4,128)}, f32[3,512]{1,0:T(4,128)S(1)}, u32[]{:S(2)}) copy-start(f32[3,512]{1,0:T(4,128)S(1)} %get-tuple-element.113) | copy-start | bytes 18436
  48.7 109.0 %copy-start.60 = (f32[3,512]{1,0:T(4,128)}, f32[3,512]{1,0:T(4,128)S(1)}, u32[]{:S(2)}) copy-start(f32[3,512]{1,0:T(4,128)S(1)} %get-tuple-element.114) | copy-start | bytes 18436
  173.1 8.1 copy-start.9
  223.3 14.4 copy-start.10
  223.3 6.7 copy-start.12
  230.0 7.6 copy-start.11
  293.8 5.6 copy-start.21
  305.6 140.2 %all-gather.20.cloned.1.call-start = ((), (), s32[]{:S(2)}) async-start(), calls=%async_computation.15 | async-start | bytes 6488064 | tf_op jit(solution)/shard_map/all_gather | solution.py:178
  307.9 172.7 %all-gather.16.cloned.1.call-start = ((), (), s32[]{:S(2)}) async-start(), calls=%async_computation.13 | async-start | bytes 5242880 | tf_op jit(solution)/shard_map/all_gather | solution.py:223
  351.9 5.9 copy-start.26
  354.7 221.6 %all-gather.18.cloned.1.call-start = ((), (), s32[]{:S(2)}) async-start(), calls=%async_computation.14 | async-start | bytes 6488064 | tf_op jit(solution)/shard_map/all_gather | solution.py:177
  357.1 253.5 %all-gather.24.cloned.1.call-start = ((), (), s32[]{:S(2)}) async-start(), calls=%async_computation.18 | async-start | bytes 5242880 | tf_op jit(solution)/shard_map/all_gather | solution.py:245
  357.8 349.2 %all-gather.22.cloned.1.call-start = ((), (), s32[]{:S(2)}) async-start(), calls=%async_computation.16 | async-start | bytes 6488064 | tf_op jit(solution)/shard_map/all_gather | solution.py:179
  358.8 426.2 %reduce-scatter.14.cloned.1.call-start = ((), (), s32[]{:S(2)}) async-start(), calls=%async_computation.19 | async-start | bytes 5242880 | tf_op jit(solution)/shard_map/reduce_scatter | solution.py:252
  707.0 17.0 %copy-start.77 = (bf16[2048,1408]{1,0:T(8,128)(2,1)S(1)}, bf16[2048,1408]{1,0:T(8,128)(2,1)}, u32[]{:S(2)}) copy-start(bf16[2048,1408]{1,0:T(8,128)(2,1)} %all-gather.18.cloned.1.call-done) | copy-start | bytes 17301508
  724.0 6.7 copy-start.79
  724.1 6.7 copy-start.80
  742.2 89.9 %reduce-scatter.12.cloned.1.call-start = ((), (), s32[]{:S(2)}) async-start(), calls=%async_computation.17 | async-start | bytes 5242880 | tf_op jit(solution)/shard_map/reduce_scatter | solution.py:231
  753.2 31.8 %copy-start.16 = (bf16[256,2048]{1,0:T(8,128)(2,1)S(1)}, bf16[256,2048]{1,0:T(8,128)(2,1)}, u32[]{:S(2)}) copy-start(bf16[256,2048]{1,0:T(8,128)(2,1)} %reduce-scatter.10.cloned.1.call-done) | copy-start | bytes 3145732
  753.2 78.9 %copy-start.29 = (bf16[256,2048]{1,0:T(8,128)(2,1)S(1)}, bf16[256,2048]{1,0:T(8,128)(2,1)}, u32[]{:S(2)}) copy-start(bf16[256,2048]{1,0:T(8,128)(2,1)} %param.35) | copy-start | bytes 3145732
  753.2 118.8 %all-gather.26.cloned.1.call-start = ((), (), s32[]{:S(2)}) async-start(), calls=%async_computation.20 | async-start | bytes 5242880 | tf_op jit(solution)/shard_map/all_gather | solution.py:260
  837.4 283.1 %reduce-scatter.26.cloned.1.call-start = ((), (), s32[]{:S(2)}) async-start(), calls=%async_computation.26 | async-start | bytes 6488064 | tf_op jit(solution)/shard_map/reduce_scatter | solution.py:335
  848.6 274.2 %reduce-scatter.22.cloned.1.call-start = ((), (), s32[]{:S(2)}) async-start(), calls=%async_computation.24 | async-start | bytes 6488064 | tf_op jit(solution)/shard_map/reduce_scatter | solution.py:329
  859.8 354.2 %reduce-scatter.24.cloned.1.call-start = ((), (), s32[]{:S(2)}) async-start(), calls=%async_computation.25 | async-start | bytes 6488064 | tf_op jit(solution)/shard_map/reduce_scatter | solution.py:332
  870.8 478.0 %all-reduce.11.cloned.1.call-start = ((), (), s32[]{:S(2)}) async-start(), calls=%async_computation.27 | async-start | bytes 720896 | tf_op jit(solution)/shard_map/psum | solution.py:312
  889.2 5.8 copy-start.4
  889.2 5.8 copy-start.48
  889.2 5.8 copy-start.50
  899.9 13.9 copy-start.5
  938.2 8.2 copy-start.8
  1052.6 7.9 slice-start
  1065.8 9.7 copy-start.53
  1065.8 11.4 copy-start.45
  1077.1 6.1 copy-start.57
  1077.1 6.1 copy-start.59
  1077.1 6.1 copy-start.61
  1077.2 343.2 %reduce-scatter.20.cloned.1.call-start = ((), (), s32[]{:S(2)}) async-start(), calls=%async_computation.23 | async-start | bytes 2359296 | tf_op jit(solution)/shard_map/reduce_scatter | solution.py:326
  1083.2 383.1 %reduce-scatter.16.cloned.1.call-start = ((), (), s32[]{:S(2)}) async-start(), calls=%async_computation.21 | async-start | bytes 5242880 | tf_op jit(solution)/shard_map/reduce_scatter | solution.py:296
  1103.7 485.0 %reduce-scatter.18.cloned.1.call-start = ((), (), s32[]{:S(2)}) async-start(), calls=%async_computation.22 | async-start | bytes 7077888 | tf_op jit(solution)/shard_map/reduce_scatter | solution.py:323
  1120.5 345.8 %copy-start.2 = (bf16[256,2048]{1,0:T(8,128)(2,1)S(1)}, bf16[256,2048]{1,0:T(8,128)(2,1)}, u32[]{:S(2)}) copy-start(bf16[256,2048]{1,0:T(8,128)(2,1)} %param.34) | copy-start | bytes 3145732
  1120.5 345.8 %copy-start.55 = (f32[1,2048]{1,0:T(1,128)S(1)}, f32[1,2048]{1,0:T(1,128)}, u32[]{:S(2)}) copy-start(f32[1,2048]{1,0:T(1,128)} %copy-done.54) | copy-start | bytes 24580
  1120.5 347.5 %copy-start.20 = (f32[256,2048]{1,0:T(8,128)S(1)}, f32[256,2048]{1,0:T(8,128)}, u32[]{:S(2)}) copy-start(f32[256,2048]{1,0:T(8,128)} %get-tuple-element.82) | copy-start | bytes 6291460
  1120.5 347.5 %copy-start.71 = (f32[256]{0:T(256)S(1)}, f32[256]{0:T(256)}, u32[]{:S(2)}) copy-start(f32[256]{0:T(256)} %copy-done.70) | copy-start | bytes 3076
  1120.5 347.5 %copy-start.74 = (f32[256]{0:T(256)S(1)}, f32[256]{0:T(256)}, u32[]{:S(2)}) copy-start(f32[256]{0:T(256)} %get-tuple-element.121) | copy-start | bytes 3076
  1124.9 346.3 %copy-start.73 = (f32[256]{0:T(256)S(1)}, f32[256]{0:T(256)}, u32[]{:S(2)}) copy-start(f32[256]{0:T(256)} %copy-done.72) | copy-start | bytes 3076
  1216.0 255.7 %copy-start.64 = (f32[2048]{0:T(1024)S(1)}, f32[2048]{0:T(1024)}, u32[]{:S(2)}) copy-start(f32[2048]{0:T(1024)} %get-tuple-element.37) | copy-start | bytes 24580
  1422.0 217.6 %copy-start.69 = (f32[2048]{0:T(1024)S(1)}, f32[2048]{0:T(1024)}, u32[]{:S(2)}) copy-start(f32[2048]{0:T(1024)} %param.50) | copy-start | bytes 24580
  1422.1 219.1 %copy-start.63 = (f32[2,2048]{1,0:T(2,128)S(1)}, f32[2,2048]{1,0:T(2,128)}, u32[]{:S(2)}) copy-start(f32[2,2048]{1,0:T(2,128)} %param.38) | copy-start | bytes 49156
  1422.1 219.1 %copy-start.67 = (f32[2,2048]{1,0:T(2,128)S(1)}, f32[2,2048]{1,0:T(2,128)}, u32[]{:S(2)}) copy-start(f32[2,2048]{1,0:T(2,128)} %param.39) | copy-start | bytes 49156
  1422.1 219.1 %copy-start.68 = (f32[2,2048]{1,0:T(2,128)S(1)}, f32[2,2048]{1,0:T(2,128)}, u32[]{:S(2)}) copy-start(f32[2,2048]{1,0:T(2,128)} %param.40) | copy-start | bytes 49156
  1468.0 179.5 %copy-start.46 = (bf16[512,256]{1,0:T(8,128)(2,1)S(1)}, bf16[512,256]{1,0:T(8,128)(2,1)}, u32[]{:S(2)}) copy-start(bf16[512,256]{1,0:T(8,128)(2,1)} %reduce-scatter.20.cloned.1.call-done) | copy-start | bytes 786436
  1471.2 179.0 %copy-start.25 = (f32[256,1408]{1,0:T(8,128)S(1)}, f32[256,1408]{1,0:T(8,128)}, u32[]{:S(2)}) copy-start(f32[256,1408]{1,0:T(8,128)} %param.62) | copy-start | bytes 4325380
  1471.2 179.0 %copy-start.33 = (bf16[256,1408]{1,0:T(8,128)(2,1)S(1)}, bf16[256,1408]{1,0:T(8,128)(2,1)}, u32[]{:S(2)}) copy-start(bf16[256,1408]{1,0:T(8,128)(2,1)} %reduce-scatter.24.cloned.1.call-done) | copy-start | bytes 2162692
  1639.6 10.6 copy-start.39
  1639.6 10.6 copy-start.40
  (38 other events, 122.8 us)
Sparse Core Ops, SparseCore 0:
  10.8 101.7 all-gather.11
  114.7 32.6 all-gather.9
  150.1 51.0 all-gather.13
  305.8 44.4 reduce-scatter.9
  353.1 92.6 all-gather.19
  447.9 32.6 all-gather.15
  483.6 92.6 all-gather.17
  577.9 32.6 all-gather.23
  613.4 93.5 all-gather.21
  742.3 42.6 reduce-scatter.13
  787.5 44.4 reduce-scatter.11
  837.5 34.4 all-gather.25
  876.1 110.3 reduce-scatter.25
  990.5 109.7 reduce-scatter.21
  1104.2 109.7 reduce-scatter.23
  1221.1 127.6 all-reduce.10
  1352.2 68.0 reduce-scatter.19
  1422.7 43.4 reduce-scatter.15
  1470.3 118.3 reduce-scatter.17
where the time goes:
time: 1680 us; the launch traced here: 1670 us
  waiting for transfers between devices  983 us (59%)
  matrix products  384 us (23%)
  other arithmetic  171 us (10%)
  local copies, waits for them, and re-layouts  69.7 us (4%)
  blocking collectives  40.3 us (2%)
  between operations  24.6 us (1%)
    psum x1, waiting for transfers between devices, on_device(): lax.psum((jnp.stack([gain_one, gain_two], axis=0), place(grad_taps, taps)...  133 us
    reduce_scatter x1, waiting for transfers between devices, on_device(): lax.psum_scatter(grad_w_in.astype(jnp.bfloat16), 'dp', scatter_dimension=...  117 us
    dot_general x12, matrix products, along_forward(): return jnp.einsum('anc,nk->akc', values, table, precision=HIGHEST)  98.7 us
    all_gather x1, waiting for transfers between devices, on_device(): lax.all_gather(down_weight.astype(jnp.bfloat16), 'dp', axis=1, tiled=True)  96.4 us
    reduce_scatter x1, waiting for transfers between devices, on_device(): lax.psum_scatter(grad_w_up.astype(jnp.bfloat16), 'dp', scatter_dimension=...  89.1 us
    all_gather x1, waiting for transfers between devices, on_device(): lax.all_gather(up_weight.astype(jnp.bfloat16), 'dp', axis=0, tiled=True)  85.5 us
    all_gather x1, waiting for transfers between devices, on_device(): lax.all_gather(gate_weight.astype(jnp.bfloat16), 'dp', axis=0, tiled=True)  83.9 us
    reduce_scatter x1, waiting for transfers between devices, on_device(): lax.psum_scatter(grad_w_out.astype(jnp.bfloat16), 'dp', scatter_dimension...  66.9 us
  transfers between devices with their start and end apart: 19, of which 16 were waited for; matrix products, arithmetic and copies ran while one was open for 32% of the time, Pallas kernels for 0%

commit v1 on v0

v1 whole, which is shorter than its diff:
```python
import functools

import jax
import jax.numpy as jnp
from jax import lax
from jax.experimental import pallas as pl
from jax.experimental.pallas import tpu as pltpu
from jax.sharding import PartitionSpec as P

STEP = 10


EPSILON = 1e-05
CLIP = 1.0
BETA_ONE = 0.9
BETA_TWO = 0.95
ADAM_EPSILON = 1e-08
DECAY = 0.1
RATE_MATRIX = 0.05
RATE_SMALL = 0.5
RATE_RATES = 4.0

LANES = 128
CHUNK = 128
CHUNKS = 8
LENGTH = CHUNK * CHUNKS
PAD = 8
TAPS = 3
POLES = 16
SKIP_ROW = TAPS * 3
RES_ROW = 16
RATE_ROW = RES_ROW + POLES
COEF_ROWS = RATE_ROW + POLES
MODE_GROUP = 8

f32 = jnp.float32
bf16 = jnp.bfloat16


def chunk_row(pos_ref, seq, n):
    block, half = n // 2, n % 2
    y, c = pos_ref[0], pos_ref[1]
    dy = y if block // 2 == 0 else 1 - y
    dc = c if block % 2 == 0 else 1 - c
    if half == 0:
        row = dc * LENGTH + seq * (2 * CHUNK) + dy * CHUNK
    else:
        row = dc * LENGTH + LENGTH // 2 + dy * (2 * CHUNK) + seq * CHUNK
    return pl.multiple_of(row, CHUNK)


def mix_chunk(pad_ref, coef, which, n):
    base = PAD + n * CHUNK
    total = coef[which : which + 1, :] * pad_ref[pl.ds(base, CHUNK), :]
    for i in range(1, TAPS):
        row = 3 * i + which
        total = total + coef[row : row + 1, :] * pad_ref[pl.ds(base - i, CHUNK), :]
    return total


def spread(row):
    return jnp.broadcast_to(row, (CHUNKS, LANES))


def power_of_two(value, doublings):
    for _ in range(doublings):
        value = value * value
    return value


def shift_down(value, count):
    rolled = pltpu.roll(value, count, 0)
    place = lax.broadcasted_iota(jnp.int32, (CHUNKS, LANES), 0)
    return jnp.where(place >= count, rolled, 0.0)


def shift_up(value, count):
    rolled = pltpu.roll(value, CHUNKS - count, 0)
    place = lax.broadcasted_iota(jnp.int32, (CHUNKS, LANES), 0)
    return jnp.where(place < CHUNKS - count, rolled, 0.0)


def tile_rows(t):
    return pl.ds(pl.multiple_of(t * CHUNKS, CHUNKS), CHUNKS)


def forward_kernel(pos_ref, proj_ref, coef_ref, branch_ref, conv_ref, pads, u_ref, y_ref):
    coef = coef_ref[...]
    decay = [spread(coef[RATE_ROW + p : RATE_ROW + p + 1, :]) for p in range(POLES)]
    weight = [spread(coef[RES_ROW + p : RES_ROW + p + 1, :]) for p in range(POLES)]
    skip = coef[SKIP_ROW : SKIP_ROW + 1, :]
    y_ref[pl.ds(0, CHUNKS), :] = jnp.zeros((CHUNKS, LANES), f32)
    zero = y_ref[pl.ds(0, CHUNKS), :]
    for seq in range(2):
        for j in range(3):
            pads[j, pl.ds(0, PAD), :] = jnp.zeros((PAD, LANES), f32)
        for n in range(CHUNKS):
            rows = pl.ds(chunk_row(pos_ref, seq, n), CHUNK)
            for j in range(3):
                pads[j, pl.ds(PAD + n * CHUNK, CHUNK), :] = proj_ref[
                    rows, j * LANES : (j + 1) * LANES
                ]
        for n in range(CHUNKS):
            gated = mix_chunk(pads.at[1], coef, 1, n) * mix_chunk(pads.at[2], coef, 2, n)
            u_ref[pl.ds(n, CHUNK, stride=CHUNKS), :] = gated

        def ends(t, state):
            u = u_ref[tile_rows(t), :]
            return [a * h + u for a, h in zip(decay, state)]

        state = lax.fori_loop(0, CHUNK, ends, [zero] * POLES, unroll=2)
        start = []
        for a, h in zip(decay, state):
            jump = power_of_two(a, 7)
            for count in (1, 2, 4):
                h = h + jump * shift_down(h, count)
                jump = jump * jump
            start.append(shift_down(h, 1))

        def outputs(t, state):
            u = u_ref[tile_rows(t), :]
            state = [a * h + u for a, h in zip(decay, state)]
            terms = [w * h for w, h in zip(weight, state)]
            while len(terms) > 1:
                terms = [l + r for l, r in zip(terms[0::2], terms[1::2])]
            y_ref[tile_rows(t), :] = terms[0]
            return state

        lax.fori_loop(0, CHUNK, outputs, start, unroll=2)
        for n in range(CHUNKS):
            rows = pl.ds(chunk_row(pos_ref, seq, n), CHUNK)
            strided = pl.ds(n, CHUNK, stride=CHUNKS)
            conv = y_ref[strided, :] + skip * u_ref[strided, :]
            conv_ref[rows, :] = conv
            branch_ref[rows, :] = (mix_chunk(pads.at[0], coef, 0, n) * conv).astype(bf16)


def backward_kernel(
    pos_ref,
    proj_ref,
    conv_ref,
    grad_ref,
    coef_ref,
    out_ref,
    sums_ref,
    pads,
    mixed,
    grads,
    u_ref,
    g_ref,
    y_ref,
):
    coef = coef_ref[...]
    decay = [spread(coef[RATE_ROW + p : RATE_ROW + p + 1, :]) for p in range(POLES)]
    weight = [spread(coef[RES_ROW + p : RES_ROW + p + 1, :]) for p in range(POLES)]
    skip = coef[SKIP_ROW : SKIP_ROW + 1, :]
    y_ref[pl.ds(0, CHUNKS), :] = jnp.zeros((CHUNKS, LANES), f32)
    zero = y_ref[pl.ds(0, CHUNKS), :]
    row_zero = jnp.zeros((1, LANES), f32)
    tap_sums = [row_zero] * (3 * TAPS)
    skip_sum = row_zero
    res_sums = [zero] * POLES
    rate_sums = [zero] * POLES
    for seq in range(2):
        for j in range(3):
            pads[j, pl.ds(0, PAD), :] = jnp.zeros((PAD, LANES), f32)
            grads[j, pl.ds(LENGTH, PAD), :] = jnp.zeros((PAD, LANES), f32)
        for n in range(CHUNKS):
            rows = pl.ds(chunk_row(pos_ref, seq, n), CHUNK)
            for j in range(3):
                pads[j, pl.ds(PAD + n * CHUNK, CHUNK), :] = proj_ref[
                    rows, j * LANES : (j + 1) * LANES
                ]
        for n in range(CHUNKS):
            rows = pl.ds(chunk_row(pos_ref, seq, n), CHUNK)
            strided = pl.ds(n, CHUNK, stride=CHUNKS)
            plain = pl.ds(n * CHUNK, CHUNK)
            query = mix_chunk(pads.at[0], coef, 0, n)
            key = mix_chunk(pads.at[1], coef, 1, n)
            value = mix_chunk(pads.at[2], coef, 2, n)
            mixed[0, plain, :] = key
            mixed[1, plain, :] = value
            branch_grad = grad_ref[rows, :]
            grads[0, plain, :] = branch_grad * conv_ref[rows, :]
            u_ref[strided, :] = key * value
            g_ref[strided, :] = branch_grad * query

        def ends(step, state):
            g = g_ref[tile_rows(CHUNK - 1 - step), :]
            after = []
            for a, (b, e) in zip(decay, state):
                ab = a * b
                after.append((ab + g, a * e + ab))
            return after

        state = lax.fori_loop(0, CHUNK, ends, [(zero, zero)] * POLES, unroll=2)
        start = []
        for a, (b, e) in zip(decay, state):
            jump = power_of_two(a, 7)
            span = float(CHUNK)
            for count in (1, 2, 4):
                b_next, e_next = shift_up(b, count), shift_up(e, count)
                e = e + jump * (e_next + span * b_next)
                b = b + jump * b_next
                jump = jump * jump
                span = 2.0 * span
            start.append((shift_up(b, 1), shift_up(e, 1)))

        for first in range(0, POLES, MODE_GROUP):
            modes = range(first, first + MODE_GROUP)

            def outputs(step, state, modes=modes, first=first):
                t = CHUNK - 1 - step
                g = g_ref[tile_rows(t), :]
                u = u_ref[tile_rows(t), :]
                after, terms = [], []
                for p, (b, e, res, rate) in zip(modes, state):
                    ab = decay[p] * b
                    e = decay[p] * e + ab
                    b = ab + g
                    terms.append(weight[p] * b)
                    after.append((b, e, res + u * b, rate + u * e))
                while len(terms) > 1:
                    terms = [l + r for l, r in zip(terms[0::2], terms[1::2])]
                total = terms[0]
                if first > 0:
                    total = total + y_ref[tile_rows(t), :]
                y_ref[tile_rows(t), :] = total
                return after

            begin = [(*start[p], res_sums[p], rate_sums[p]) for p in modes]
            after = lax.fori_loop(0, CHUNK, outputs, begin, unroll=2)
            for p, (_, _, res, rate) in zip(modes, after):
                res_sums[p], rate_sums[p] = res, rate

        for n in range(CHUNKS):
            strided = pl.ds(n, CHUNK, stride=CHUNKS)
            plain = pl.ds(n * CHUNK, CHUNK)
            conv_grad = g_ref[strided, :]
            gated_grad = y_ref[strided, :] + skip * conv_grad
            skip_sum = skip_sum + jnp.sum(conv_grad * u_ref[strided, :], axis=0, keepdims=True)
            grads[1, plain, :] = gated_grad * mixed[1, plain, :]
            grads[2, plain, :] = gated_grad * mixed[0, plain, :]
        for n in range(CHUNKS):
            rows = pl.ds(chunk_row(pos_ref, seq, n), CHUNK)
            for j in range(3):
                here = grads[j, pl.ds(n * CHUNK, CHUNK), :]
                total = coef[j : j + 1, :] * here
                for i in range(TAPS):
                    behind = pads[j, pl.ds(PAD + n * CHUNK - i, CHUNK), :]
                    row = 3 * i + j
                    tap_sums[row] = tap_sums[row] + jnp.sum(here * behind, axis=0, keepdims=True)
                    if i > 0:
                        ahead = grads[j, pl.ds(n * CHUNK + i, CHUNK), :]
                        total = total + coef[row : row + 1, :] * ahead
                out_ref[rows, j * LANES : (j + 1) * LANES] = total.astype(bf16)
    for row in range(3 * TAPS):
        sums_ref[row : row + 1, :] = tap_sums[row]
    sums_ref[SKIP_ROW : SKIP_ROW + 1, :] = skip_sum
    for row in range(SKIP_ROW + 1, RES_ROW):
        sums_ref[row : row + 1, :] = row_zero
    for p in range(POLES):
        sums_ref[RES_ROW + p : RES_ROW + p + 1, :] = jnp.sum(res_sums[p], axis=0, keepdims=True)
        sums_ref[RATE_ROW + p : RATE_ROW + p + 1, :] = jnp.sum(
            rate_sums[p], axis=0, keepdims=True
        )


def mixer_forward(position, proj, coef):
    rows, channels = proj.shape[0], coef.shape[1]
    return pl.pallas_call(
        forward_kernel,
        grid=(channels // LANES,),
        in_specs=[
            pl.BlockSpec(memory_space=pltpu.SMEM),
            pl.BlockSpec((rows, 3 * LANES), lambda i: (0, i)),
            pl.BlockSpec((COEF_ROWS, LANES), lambda i: (0, i)),
        ],
        out_specs=[
            pl.BlockSpec((rows, LANES), lambda i: (0, i)),
            pl.BlockSpec((rows, LANES), lambda i: (0, i)),
        ],
        out_shape=[
            jax.ShapeDtypeStruct((rows, channels), bf16),
            jax.ShapeDtypeStruct((rows, channels), f32),
        ],
        scratch_shapes=[
            pltpu.VMEM((3, PAD + LENGTH, LANES), f32),
            pltpu.VMEM((LENGTH, LANES), f32),
            pltpu.VMEM((LENGTH, LANES), f32),
        ],
        compiler_params=pltpu.CompilerParams(vmem_limit_bytes=28 << 20),
        cost_estimate=pl.CostEstimate(
            flops=20_000_000, bytes_accessed=12 << 20, transcendentals=0
        ),
        name="mixer_forward",
    )(position, proj, coef)


def mixer_backward(position, proj, conv, grad, coef):
    rows, channels = proj.shape[0], coef.shape[1]
    return pl.pallas_call(
        backward_kernel,
        grid=(channels // LANES,),
        in_specs=[
            pl.BlockSpec(memory_space=pltpu.SMEM),
            pl.BlockSpec((rows, 3 * LANES), lambda i: (0, i)),
            pl.BlockSpec((rows, LANES), lambda i: (0, i)),
            pl.BlockSpec((rows, LANES), lambda i: (0, i)),
            pl.BlockSpec((COEF_ROWS, LANES), lambda i: (0, i)),
        ],
        out_specs=[
            pl.BlockSpec((rows, 3 * LANES), lambda i: (0, i)),
            pl.BlockSpec((COEF_ROWS, LANES), lambda i: (0, i)),
        ],
        out_shape=[
            jax.ShapeDtypeStruct((rows, 3 * channels), bf16),
            jax.ShapeDtypeStruct((COEF_ROWS, channels), f32),
        ],
        scratch_shapes=[
            pltpu.VMEM((3, PAD + LENGTH, LANES), f32),
            pltpu.VMEM((2, LENGTH, LANES), f32),
            pltpu.VMEM((3, LENGTH + PAD, LANES), f32),
            pltpu.VMEM((LENGTH, LANES), f32),
            pltpu.VMEM((LENGTH, LANES), f32),
            pltpu.VMEM((LENGTH, LANES), f32),
        ],
        compiler_params=pltpu.CompilerParams(vmem_limit_bytes=36 << 20),
        cost_estimate=pl.CostEstimate(
            flops=60_000_000, bytes_accessed=16 << 20, transcendentals=0
        ),
        name="mixer_backward",
    )(position, proj, conv, grad, coef)


def rows_by_rows(left, right):
    return lax.dot_general(left, right, (((1,), (1,)), ((), ())), preferred_element_type=f32)


def columns_by_columns(left, right):
    return lax.dot_general(left, right, (((0,), (0,)), ((), ())), preferred_element_type=f32)


def plain_dot(left, right):
    return jnp.dot(left, right, preferred_element_type=f32)


def low(values):
    return values.astype(bf16)


def add_low(left, right):
    return (left.astype(f32) + right.astype(f32)).astype(bf16)


def norm_back(values, scale, gain, grad):
    weighted = grad * gain
    inner_mean = jnp.mean(values * weighted, axis=1, keepdims=True)
    return (
        scale * weighted - values * (scale * scale * scale) * inner_mean,
        jnp.sum(grad * values * scale, axis=0),
    )


def adam(weight, first, second, grad, rate, decay):
    first_new = BETA_ONE * first + (1.0 - BETA_ONE) * grad
    second_new = BETA_TWO * second + (1.0 - BETA_TWO) * grad * grad
    stride = (
        first_new
        / (1.0 - BETA_ONE**STEP)
        / (jnp.sqrt(second_new / (1.0 - BETA_TWO**STEP)) + ADAM_EPSILON)
    )
    return (weight - rate * (stride + decay * weight), first_new, second_new)


class Links:
    def __init__(self, groups, holders):
        self.groups = groups
        self.ring = [(2 * z + x, 2 * ((z + 1) % groups) + x) for z in range(groups) for x in (0, 1)]
        self.over_x = [(2 * z + x, 2 * z + 1 - x) for z in range(groups) for x in (0, 1)]
        self.over_y = [(2 * y + c, 2 * (1 - y) + c) for y in (0, 1) for c in (0, 1)]
        self.over_c = [(2 * y + c, 2 * y + 1 - c) for y in (0, 1) for c in (0, 1)]
        self.turns = [
            [(2 * z + x, 2 * ((z + s) % groups) + x) for z in range(groups) for x in (0, 1)]
            for s in range(groups)
        ]

    def z(self, v):
        return lax.ppermute(v, "dp", self.ring)

    def turn(self, v, s):
        return lax.ppermute(v, "dp", self.turns[s])

    def x(self, v):
        return lax.ppermute(v, "dp", self.over_x)

    def y(self, v):
        return lax.ppermute(v, "mp", self.over_y)

    def c(self, v):
        return lax.ppermute(v, "mp", self.over_c)


def gather_rows(net, block):
    half = block.shape[0] // 2
    a, b = block[:half], block[half:]
    a_x, b_y = net.x(a), net.y(b)
    a_y, b_x = net.y(a), net.x(b)
    a_xy, b_yx = net.y(a_x), net.x(b_y)
    mine = [a, a_y, a_x, a_xy, b, b_x, b_y, b_yx]
    return jnp.concatenate(mine + [net.c(piece) for piece in mine], axis=0)


def scatter_rows(net, partial):
    rows = partial.shape[0]
    near = add_low(partial[: rows // 2], net.c(partial[rows // 2 :]))
    piece = rows // 16
    a, b = near[: 4 * piece], near[4 * piece :]
    a = add_low(a[: 2 * piece], net.x(a[2 * piece :]))
    b = add_low(b[: 2 * piece], net.y(b[2 * piece :]))
    a = a[:piece].astype(f32) + net.y(a[piece:]).astype(f32)
    b = b[:piece].astype(f32) + net.x(b[piece:]).astype(f32)
    return jnp.concatenate([a, b], axis=0)


def pick(pair, index):
    return lax.dynamic_index_in_dim(pair, index, 0, keepdims=False)


def in_order(mine, other, x, axis):
    return jnp.where(
        x == 0,
        jnp.concatenate([mine, other], axis=axis),
        jnp.concatenate([other, mine], axis=axis),
    )


def gather_units(net, halves, x, z):
    piece = in_order(pick(halves, x), net.x(pick(halves, 1 - x)), x, 1)
    units, width = piece.shape
    whole = jnp.zeros((units, width * net.groups), bf16)
    for step in range(net.groups):
        place = lax.rem(z + net.groups - step, net.groups) * width
        whole = lax.dynamic_update_slice(whole, piece, (0, place))
        if step < net.groups - 1:
            piece = net.z(piece)
    return whole


def scatter_units(net, grad, z):
    width = grad.shape[1] // net.groups

    def part(step):
        place = lax.rem(z + 2 * net.groups - 1 - step, net.groups) * width
        return lax.dynamic_slice_in_dim(grad, place, width, 1)

    total = part(0)
    for step in range(1, net.groups):
        total = net.z(total).astype(f32) + part(step).astype(f32)
        if step < net.groups - 1:
            total = total.astype(bf16)
    return total


def trade_units(net, total, x):
    width = total.shape[1] // 2
    mine = lax.dynamic_slice_in_dim(total, x * width, width, 1)
    other = lax.dynamic_slice_in_dim(total, (1 - x) * width, width, 1)
    got = net.x(other.astype(bf16)).astype(f32)
    return jnp.where(x == 0, jnp.stack([mine, got]), jnp.stack([got, mine]))


def on_device(
    net,
    tokens,
    cotangent,
    group_ids,
    group_scales,
    gains,
    gains_first,
    gains_second,
    taps,
    taps_first,
    taps_second,
    residues,
    residues_first,
    residues_second,
    log_rates,
    log_rates_first,
    log_rates_second,
    skip,
    skip_first,
    skip_second,
    in_weight,
    in_weight_first,
    in_weight_second,
    out_weight,
    out_weight_first,
    out_weight_second,
    gate_weight,
    gate_weight_first,
    gate_weight_second,
    up_weight,
    up_weight_first,
    up_weight_second,
    down_weight,
    down_weight_first,
    down_weight_second,
):
    model = tokens.shape[1]
    depth = in_weight.shape[0]
    channels = in_weight.shape[2] // 2
    hidden = gate_weight.shape[1] // 2
    tiles = channels // LANES
    dp, mp = lax.axis_index("dp"), lax.axis_index("mp")
    z, x, y, c = dp // 2, dp % 2, mp // 2, mp % 2
    begin = (mp * 2 + x) * channels
    position = jnp.stack([y, c]).astype(jnp.int32)

    in_halves = (
        low(in_weight).reshape(depth, 3, 2, tiles, LANES).transpose(2, 3, 1, 4, 0)
    ).reshape(2, 3 * channels, depth)
    w_in = gather_units(net, in_halves, x, z)
    w_out = gather_units(net, low(out_weight).reshape(2, channels, depth), x, z)
    w_gate = gather_units(net, low(gate_weight).T.reshape(2, hidden, depth), x, z)
    w_up = gather_units(net, low(up_weight).T.reshape(2, hidden, depth), x, z)
    w_down = gather_units(net, low(down_weight).reshape(2, hidden, depth), x, z)

    def own(array):
        return lax.dynamic_slice_in_dim(array, begin, channels, array.ndim - 1)

    residues_own = own(residues)
    rates_own = jnp.exp(own(log_rates))
    coef = jnp.concatenate(
        [
            own(taps).reshape(3 * TAPS, channels),
            own(skip)[None],
            jnp.zeros((RES_ROW - SKIP_ROW - 1, channels), f32),
            residues_own,
            jnp.exp(-rates_own),
        ],
        axis=0,
    )

    sequence_scale = jnp.sum(
        jnp.where(
            group_ids[:, None] == jnp.arange(group_scales.shape[0], dtype=jnp.int32)[None, :],
            group_scales[None, :],
            0.0,
        )
    )
    other_scale = net.x(sequence_scale.reshape(1, 1))

    resid = tokens.astype(f32)
    scale_one = lax.rsqrt(jnp.mean(resid * resid, axis=1, keepdims=True) + EPSILON)
    normed = low(resid * scale_one * gains[0])
    normed_all = gather_rows(net, normed)
    back_all = gather_rows(net, cotangent)
    proj = rows_by_rows(normed_all, w_in)
    branch, conv = mixer_forward(position, proj, coef)
    middle = resid + scatter_rows(net, low(plain_dot(branch, w_out)))
    scale_two = lax.rsqrt(jnp.mean(middle * middle, axis=1, keepdims=True) + EPSILON)
    normed_two = low(middle * scale_two * gains[1])
    normed_two_all = gather_rows(net, normed_two)
    gate = rows_by_rows(normed_two_all, w_gate)
    up = rows_by_rows(normed_two_all, w_up)
    sigma = jax.nn.sigmoid(gate)
    silu = gate * sigma
    inner = silu * up
    rows = normed_two_all.shape[0]
    index = lax.broadcasted_iota(jnp.int32, (rows, 1), 0)
    half, within = (index // (rows // 4)) % 2, (index // (rows // 16)) % 4
    other_row = jnp.where(half == 0, within // 2, within % 2) == 1
    row_scale = jnp.where(other_row, other_scale, sequence_scale.reshape(1, 1))

    grad_down = low(columns_by_columns(low(inner * row_scale), back_all))
    total_down = scatter_units(net, grad_down, z)
    grad_inner = rows_by_rows(back_all, w_down) * row_scale
    grad_gate = low(grad_inner * up * sigma * (1.0 + gate * (1.0 - sigma)))
    grad_up = low(grad_inner * silu)
    total_gate = scatter_units(net, low(columns_by_columns(grad_gate, normed_two_all)), z)
    total_up = scatter_units(net, low(columns_by_columns(grad_up, normed_two_all)), z)
    output = low(middle + scatter_rows(net, low(plain_dot(low(inner), w_down))))
    grad_normed_two = scatter_rows(
        net, low(plain_dot(grad_gate, w_gate) + plain_dot(grad_up, w_up))
    )
    grad_from_norm, gain_two = norm_back(middle, scale_two, gains[1], grad_normed_two)
    grad_middle = cotangent.astype(f32) * sequence_scale + grad_from_norm
    grad_middle_all = gather_rows(net, low(grad_middle))
    total_out = scatter_units(net, low(columns_by_columns(branch, grad_middle_all)), z)
    grad_branch = rows_by_rows(grad_middle_all, w_out)
    grad_proj, sums = mixer_backward(position, proj, conv, grad_branch, coef)
    total_in = scatter_units(net, low(columns_by_columns(grad_proj, normed_all)), z)
    grad_normed = scatter_rows(net, low(plain_dot(grad_proj, w_in)))
    grad_from_first, gain_one = norm_back(resid, scale_one, gains[0], grad_normed)
    grad_input = grad_middle + grad_from_first
    input_grad = low(grad_input)
    radial_grad = scale_one[:, 0] * jnp.sum(resid * grad_input, axis=1) / model**0.5

    sums = jnp.concatenate(
        [sums[:RATE_ROW], -rates_own * residues_own * sums[RATE_ROW:]], axis=0
    )
    sums = sum((net.turn(sums, s) for s in range(1, net.groups)), sums)
    sums = in_order(sums[None], net.x(sums)[None], x, 0)[None]
    sums = in_order(sums, net.c(sums), c, 0)[None]
    sums = in_order(sums, net.y(sums), y, 0)
    sums = sums.reshape(8, COEF_ROWS, channels).transpose(1, 0, 2).reshape(COEF_ROWS, model)
    grad_taps = sums[: 3 * TAPS].reshape(taps.shape)
    grad_skip = sums[SKIP_ROW]
    grad_residues = sums[RES_ROW:RATE_ROW]
    grad_log_rates = sums[RATE_ROW:]

    totals = (total_in, total_out, total_gate, total_up, total_down)
    square_big = sum((jnp.sum(grad * grad) for grad in totals))
    last = jnp.concatenate(
        [gain_one.reshape(-1, LANES), gain_two.reshape(-1, LANES), jnp.full((8, LANES), square_big)]
    )
    last = last + net.x(last)
    last = last + net.y(last)
    last = last + net.c(last)
    last = sum((net.turn(last, s) for s in range(1, net.groups)), last)
    span = model // LANES
    grad_gains = last[: 2 * span].reshape(2, model)
    small = (grad_gains, grad_taps, grad_residues, grad_log_rates, grad_skip)
    square_total = last[2 * span, 0] + sum((jnp.sum(grad * grad) for grad in small))
    grad_norm = jnp.sqrt(square_total)
    factor = jnp.minimum(1.0, CLIP / (grad_norm + 1e-06))

    pair_in, pair_out, pair_gate, pair_up, pair_down = (
        trade_units(net, total, x) for total in totals
    )
    shard_in = (
        pair_in.reshape(2, tiles, 3, LANES, depth)
        .transpose(4, 2, 0, 1, 3)
        .reshape(depth, 3, 2 * channels)
    )
    shard_out = pair_out.reshape(2 * channels, depth)
    shard_gate = pair_gate.reshape(2 * hidden, depth).T
    shard_up = pair_up.reshape(2 * hidden, depth).T
    shard_down = pair_down.reshape(2 * hidden, depth)

    return (
        output,
        input_grad,
        radial_grad,
        *adam(gains, gains_first, gains_second, grad_gains * factor, RATE_SMALL, 0.0),
        *adam(taps, taps_first, taps_second, grad_taps * factor, RATE_SMALL, 0.0),
        *adam(
            residues, residues_first, residues_second, grad_residues * factor, RATE_SMALL, 0.0
        ),
        *adam(
            log_rates,
            log_rates_first,
            log_rates_second,
            grad_log_rates * factor,
            RATE_RATES,
            0.0,
        ),
        *adam(skip, skip_first, skip_second, grad_skip * factor, RATE_SMALL, 0.0),
        *adam(
            in_weight, in_weight_first, in_weight_second, shard_in * factor, RATE_MATRIX, DECAY
        ),
        *adam(
            out_weight, out_weight_first, out_weight_second, shard_out * factor, RATE_MATRIX, DECAY
        ),
        *adam(
            gate_weight,
            gate_weight_first,
            gate_weight_second,
            shard_gate * factor,
            RATE_MATRIX,
            DECAY,
        ),
        *adam(up_weight, up_weight_first, up_weight_second, shard_up * factor, RATE_MATRIX, DECAY),
        *adam(
            down_weight,
            down_weight_first,
            down_weight_second,
            shard_down * factor,
            RATE_MATRIX,
            DECAY,
        ),
        grad_norm,
    )


def solution(mesh):
    net = Links(mesh.shape["dp"] // 2, mesh.shape["mp"])
    rows = P(("dp", "mp"), None)
    split_in = P("dp", None, "mp")
    split_out = P("mp", "dp")
    split_up = P("dp", "mp")
    matrices = (split_in,) * 3 + (split_out,) * 3 + (split_up,) * 6 + (split_out,) * 3
    return jax.shard_map(
        functools.partial(on_device, net),
        mesh=mesh,
        in_specs=(rows, rows, P("dp"), P()) + (P(),) * 15 + matrices,
        out_specs=(rows, rows, P(("dp", "mp"))) + (P(),) * 15 + matrices + (P(),),
        check_vma=False,
    )
```

time: 1680 us -> 962 us (0.57)
  waiting for transfers between devices: 983 us -> 483 us
  matrix products: 384 us -> 132 us
  starting transfers between devices: 1 us -> 81.9 us
  other arithmetic: 171 us -> 104 us
  Pallas kernels: 0 us -> 43.6 us
  blocking collectives: 40.3 us -> 0 us
  local copies, waits for them, and re-layouts: 69.7 us -> 101 us
    ppermute x0 -> x129, waiting for transfers between devices: none -> 483 us  [the longest x30 284 us: z(): return lax.ppermute(v, 'dp', self.ring)]
    reduce_scatter x9 -> x0, waiting for transfers between devices: 436 us -> none  [the longest x1 117 us: on_device(): lax.psum_scatter(grad_w_in.astype(jnp.bfloat16), 'dp', scatter_dimension=...]
    all_gather x9 -> x0, waiting for transfers between devices: 414 us -> none  [the longest x1 96.4 us: on_device(): lax.all_gather(down_weight.astype(jnp.bfloat16), 'dp', axis=1, tiled=True)]
    dot_general x51 -> x15, matrix products: 384 us -> 132 us  [the longest x5 44.8 us: rows_by_rows(): lax.dot_general(left, right, (((1,), (1,)), ((), ())), preferred_element_...]
    psum x1 -> x0, waiting for transfers between devices: 133 us -> none  [on_device(): lax.psum((jnp.stack([gain_one, gain_two], axis=0), place(grad_taps, taps)...]
    ppermute x0 -> x129, starting transfers between devices: none -> 81.9 us  [the longest x33 42.5 us: x(): return lax.ppermute(v, 'dp', self.over_x)]
    unnamed x3 -> x4, other arithmetic: 53.2 us -> 0.01 us
    pallas_call x0 -> x2, Pallas kernels: none -> 43.6 us  [the longest x1 30.1 us: mixer_backward(): pl.pallas_call(backward_kernel, grid=(channels // LANES,), in_specs=[pl.B...]
  transfers between devices with their start and end apart: 19 -> 129, of which waited for: 16 -> 62; matrix products, arithmetic and copies ran while one was open for 32% -> 22% of each run, Pallas kernels for 0% -> 3%
where the time goes in v1:
time: 962 us; the launch traced here: 957 us
  waiting for transfers between devices  483 us (50%)
  matrix products  132 us (14%)
  other arithmetic  104 us (11%)
  local copies, waits for them, and re-layouts  101 us (10%)
  starting transfers between devices  81.9 us (9%)
  Pallas kernels  43.6 us (5%)
  between operations  12.6 us (1%)
    ppermute x30, waiting for transfers between devices, z(): return lax.ppermute(v, 'dp', self.ring)  284 us
    ppermute x33, waiting for transfers between devices, x(): return lax.ppermute(v, 'dp', self.over_x)  147 us
    unnamed x278, local copies, waits for them, and re-layouts  52.8 us
    dot_general x5, matrix products, rows_by_rows(): lax.dot_general(left, right, (((1,), (1,)), ((), ())), preferred_element_...  44.8 us
    dot_general x5, matrix products, columns_by_columns(): lax.dot_general(left, right, (((0,), (0,)), ((), ())), preferred_element_...  43.5 us
    dot_general x5, matrix products, plain_dot(): return jnp.dot(left, right, preferred_element_type=f32)  43.4 us
    ppermute x33, starting transfers between devices, x(): return lax.ppermute(v, 'dp', self.over_x)  42.5 us
    ppermute x22, waiting for transfers between devices, y(): return lax.ppermute(v, 'mp', self.over_y)  40.8 us
  transfers between devices with their start and end apart: 129, of which 62 were waited for; matrix products, arithmetic and copies ran while one was open for 22% of the time, Pallas kernels for 3%

profile of v1, /device:TPU:0, one launch (start us, length us, event | category | flops | bytes accessed | tf_op | source)
XLA Modules:
  0.0 956.9 jit_solution(84141421258062529)
XLA Ops:
  16.2 10.4 %collective-permute-done.18 = bf16[256,256]{1,0:T(8,128)(2,1)} collective-permute-done((bf16[256,256]{1,0:T(8,128)(2,1)}, bf16[256,256]{1,0:T(8,128)(2,1)}, u32[]{:S(2)}, u32[]{:S(2)}) %collective-permute-start.18) | collective-permute-done | bytes 131104 | tf_op jit(solution)/shard_map/ppermute | solution.py:395
  32.4 4.1 collective-permute-done.19
  48.6 6.2 collective-permute-done.21
  55.0 3.7 collective-permute-done.2
  63.5 5.9 collective-permute-done.5
  73.0 3.8 collective-permute-done.15
  80.6 17.1 %collective-permute-done.16 = bf16[768,512]{1,0:T(8,128)(2,1)S(1)} collective-permute-done((bf16[768,512]{1,0:T(8,128)(2,1)S(1)}, bf16[768,512]{1,0:T(8,128)(2,1)S(1)}, u32[]{:S(2)}, u32[]{:S(2)}) %collective-permute-start.16) | collective-permute-done | bytes 786464 | tf_op jit(solution)/shard_map/ppermute | solution.py:389
  100.5 17.4 %collective-permute-done.17 = bf16[768,512]{1,0:T(8,128)(2,1)S(1)} collective-permute-done((bf16[768,512]{1,0:T(8,128)(2,1)S(1)}, bf16[768,512]{1,0:T(8,128)(2,1)S(1)}, u32[]{:S(2)}, u32[]{:S(2)}) %collective-permute-start.17) | collective-permute-done | bytes 786464 | tf_op jit(solution)/shard_map/ppermute | solution.py:389
  118.1 10.4 %fusion.81.proj_ref = f32[2048,768]{1,0:T(8,128)S(1)} fusion(bf16[2048,2048]{1,0:T(8,128)(2,1)} %constant_dynamic-update-slice_fusion, bf16[768,2048]{1,0:T(8,128)(2,1)S(1)} %constant_dynamic-update-slice_fusion.80), kind=kOutput, calls=%fused_computation.335 | convolution fusion | flops 6442450944 | bytes 17825792 | tf_op jit(solution)/shard_map/dot_general | solution.py:337
  128.5 13.5 %mixer_forward.1 = (bf16[2048,256]{1,0:T(8,128)(2,1)S(1)}, f32[2048,256]{1,0:T(8,128)S(1)}) custom-call(s32[2]{0:T(128)S(1)} %pad_add_fusion.pos_ref, f32[2048,768]{1,0:T(8,128)S(1)} %fusion.81.proj_ref, f32[48,256]{1,0:T(8,128)S(1)} %concatenate.140.coef_ref), custom_call_target="tpu_custom_call" | custom-call | flops 20000000 | bytes 12582912 | tf_op jit(solution)/shard_map/mixer_forward/pallas_call | solution.py:271
  168.3 7.3 collective-permute-done.45
  182.3 11.4 %collective-permute-done.49 = bf16[704,256]{1,0:T(8,128)(2,1)S(1)} collective-permute-done((bf16[704,256]{1,0:T(8,128)(2,1)S(1)}, bf16[704,256]{1,0:T(8,128)(2,1)S(1)}, u32[]{:S(2)}, u32[]{:S(2)}) %collective-permute-start.49) | collective-permute-done | bytes 360480 | tf_op jit(solution)/shard_map/ppermute | solution.py:395
  198.9 8.7 collective-permute-done.60
  213.5 6.0 collective-permute-done.63
  223.0 4.1 add_convert_fusion.4
  232.9 7.7 collective-permute-done.42
  242.0 10.4 %collective-permute-done.50 = bf16[704,512]{1,0:T(8,128)(2,1)} collective-permute-done((bf16[704,512]{1,0:T(8,128)(2,1)}, bf16[704,512]{1,0:T(8,128)(2,1)}, u32[]{:S(2)}, u32[]{:S(2)}) %collective-permute-start.50) | collective-permute-done | bytes 720928 | tf_op jit(solution)/shard_map/ppermute | solution.py:389
  263.8 14.0 %collective-permute-done.47 = bf16[704,512]{1,0:T(8,128)(2,1)S(1)} collective-permute-done((bf16[704,512]{1,0:T(8,128)(2,1)S(1)}, bf16[704,512]{1,0:T(8,128)(2,1)S(1)}, u32[]{:S(2)}, u32[]{:S(2)}) %collective-permute-start.47) | collective-permute-done | bytes 720928 | tf_op jit(solution)/shard_map/ppermute | solution.py:389
  277.8 15.4 %collective-permute-done.43 = bf16[704,512]{1,0:T(8,128)(2,1)S(1)} collective-permute-done((bf16[704,512]{1,0:T(8,128)(2,1)S(1)}, bf16[704,512]{1,0:T(8,128)(2,1)S(1)}, u32[]{:S(2)}, u32[]{:S(2)}) %collective-permute-start.43) | collective-permute-done | bytes 720928 | tf_op jit(solution)/shard_map/ppermute | solution.py:389
  293.2 15.4 %collective-permute-done.51 = bf16[704,512]{1,0:T(8,128)(2,1)S(1)} collective-permute-done((bf16[704,512]{1,0:T(8,128)(2,1)}, bf16[704,512]{1,0:T(8,128)(2,1)S(1)}, u32[]{:S(2)}, u32[]{:S(2)}) %collective-permute-start.51) | collective-permute-done | bytes 720928 | tf_op jit(solution)/shard_map/ppermute | solution.py:389
  312.8 11.3 %collective-permute-done.48 = bf16[704,512]{1,0:T(8,128)(2,1)S(1)} collective-permute-done((bf16[704,512]{1,0:T(8,128)(2,1)S(1)}, bf16[704,512]{1,0:T(8,128)(2,1)S(1)}, u32[]{:S(2)}, u32[]{:S(2)}) %collective-permute-start.48) | collective-permute-done | bytes 720928 | tf_op jit(solution)/shard_map/ppermute | solution.py:389
  325.2 14.4 %collective-permute-done.44 = bf16[704,512]{1,0:T(8,128)(2,1)S(1)} collective-permute-done((bf16[704,512]{1,0:T(8,128)(2,1)S(1)}, bf16[704,512]{1,0:T(8,128)(2,1)S(1)}, u32[]{:S(2)}, u32[]{:S(2)}) %collective-permute-start.44) | collective-permute-done | bytes 720928 | tf_op jit(solution)/shard_map/ppermute | solution.py:389
  340.5 14.2 %collective-permute-done.52 = bf16[704,512]{1,0:T(8,128)(2,1)S(1)} collective-permute-done((bf16[704,512]{1,0:T(8,128)(2,1)S(1)}, bf16[704,512]{1,0:T(8,128)(2,1)S(1)}, u32[]{:S(2)}, u32[]{:S(2)}) %collective-permute-start.52) | collective-permute-done | bytes 720928 | tf_op jit(solution)/shard_map/ppermute | solution.py:389
  357.7 11.9 %collective-permute-done.30 = bf16[128,2048]{1,0:T(8,128)(2,1)S(1)} collective-permute-done((bf16[128,2048]{1,0:T(8,128)(2,1)S(1)}, bf16[128,2048]{1,0:T(8,128)(2,1)S(1)}, u32[]{:S(2)}, u32[]{:S(2)}) %collective-permute-start.30) | collective-permute-done | bytes 524320 | tf_op jit(solution)/shard_map/ppermute | solution.py:395
  369.7 10.7 %collective-permute-done.32 = bf16[128,2048]{1,0:T(8,128)(2,1)S(1)} collective-permute-done((bf16[128,2048]{1,0:T(8,128)(2,1)S(1)}, bf16[128,2048]{1,0:T(8,128)(2,1)S(1)}, u32[]{:S(2)}, u32[]{:S(2)}) %collective-permute-start.32) | collective-permute-done | bytes 524320 | tf_op jit(solution)/shard_map/ppermute | solution.py:395
  384.6 8.4 fusion.83
  393.1 8.0 fusion.82
  401.1 11.7 %convolution_convert_fusion.1 = bf16[2048,2048]{1,0:T(8,128)(2,1)S(1)} fusion(bf16[704,2048]{1,0:T(8,128)(2,1)S(1)} %constant_dynamic-update-slice_fusion.64, f32[2048,704]{0,1:T(8,128)} %fusion.83, f32[2048,704]{0,1:T(8,128)} %fusion.82), kind=kOutput, calls=%fused_computation.6 | convolution fusion | flops 5918425088 | bytes 22806528 | tf_op jit(solution)/shard_map/dot_general | solution.py:345
  412.8 14.7 %convolution_convert_fusion.4 = bf16[704,2048]{1,0:T(8,128)(2,1)S(1)} fusion(bf16[2048,2048]{1,0:T(8,128)(2,1)} %constant_dynamic-update-slice_fusion.32, f32[2048]{0:T(1024)S(1)} %fusion.51, f32[2048,704]{0,1:T(8,128)} %fusion.83, f32[2048,704]{0,1:T(8,128)} %fusion.82), kind=kOutput, calls=%fused_computation.21 | convolution fusion | flops 5917114368 | bytes 22814720 | tf_op jit(solution)/shard_map/dot_general | solution.py:341
  427.5 15.5 %multiply_convert_fusion.2 = (bf16[2048,704]{0,1:T(8,128)(2,1)}, bf16[2048,704]{0,1:T(8,128)(2,1)S(1)}) fusion(f32[2048,704]{0,1:T(8,128)} %fusion.82, f32[2048,704]{0,1:T(8,128)} %fusion.83, f32[2048]{0:T(1024)S(1)} %fusion.51, bf16[2048,2048]{1,0:T(8,128)(2,1)} %constant_dynamic-update-slice_fusion.32, bf16[704,2048]{1,0:T(8,128)(2,1)S(1)} %copy-done.37), kind=kOutput, calls=%fused_computation.10 | convolution fusion | flops 5925765120 | bytes 28581888 | tf_op jit(solution)/shard_map/dot_general | solution.py:337
  447.0 8.7 convolution_convert_fusion.6
  458.2 10.6 %fusion.84 = f32[2048,2048]{1,0:T(8,128)} fusion(bf16[2048,704]{0,1:T(8,128)(2,1)S(1)} %get-tuple-element.105, bf16[704,2048]{1,0:T(8,128)(2,1)S(1)} %copy-done.41), kind=kOutput, calls=%fused_computation.338 | convolution fusion | flops 5905580032 | bytes 22544384 | tf_op jit(solution)/shard_map/dot_general | solution.py:345
  468.8 11.7 %add_convert_fusion = bf16[2048,2048]{1,0:T(8,128)(2,1)S(1)} fusion(f32[2048,2048]{1,0:T(8,128)} %fusion.84, bf16[2048,704]{0,1:T(8,128)(2,1)} %get-tuple-element.104, bf16[704,2048]{1,0:T(8,128)(2,1)} %copy-done.44), kind=kOutput, calls=%fused_computation | convolution fusion | flops 5913968640 | bytes 30932992 | tf_op jit(solution)/shard_map/dot_general | solution.py:345
  485.7 8.6 convolution_convert_fusion.5
  497.7 4.2 collective-permute-start.110
  504.5 11.8 %collective-permute-done.106 = bf16[704,512]{1,0:T(8,128)(2,1)S(1)} collective-permute-done((bf16[704,512]{1,0:T(8,128)(2,1)}, bf16[704,512]{1,0:T(8,128)(2,1)S(1)}, u32[]{:S(2)}, u32[]{:S(2)}) %collective-permute-start.106) | collective-permute-done | bytes 720928 | tf_op jit(solution)/shard_map/ppermute | solution.py:389
  518.6 13.2 %collective-permute-done.110 = bf16[704,512]{1,0:T(8,128)(2,1)} collective-permute-done((bf16[704,512]{1,0:T(8,128)(2,1)}, bf16[704,512]{1,0:T(8,128)(2,1)}, u32[]{:S(2)}, u32[]{:S(2)}) %collective-permute-start.110) | collective-permute-done | bytes 720928 | tf_op jit(solution)/shard_map/ppermute | solution.py:389
  534.3 13.0 %collective-permute-done.104 = bf16[704,512]{1,0:T(8,128)(2,1)} collective-permute-done((bf16[704,512]{1,0:T(8,128)(2,1)}, bf16[704,512]{1,0:T(8,128)(2,1)}, u32[]{:S(2)}, u32[]{:S(2)}) %collective-permute-start.104) | collective-permute-done | bytes 720928 | tf_op jit(solution)/shard_map/ppermute | solution.py:389
  549.7 12.9 %collective-permute-done.107 = bf16[704,512]{1,0:T(8,128)(2,1)S(1)} collective-permute-done((bf16[704,512]{1,0:T(8,128)(2,1)}, bf16[704,512]{1,0:T(8,128)(2,1)S(1)}, u32[]{:S(2)}, u32[]{:S(2)}) %collective-permute-start.107) | collective-permute-done | bytes 720928 | tf_op jit(solution)/shard_map/ppermute | solution.py:389
  564.6 13.6 %collective-permute-done.111 = bf16[704,512]{1,0:T(8,128)(2,1)} collective-permute-done((bf16[704,512]{1,0:T(8,128)(2,1)}, bf16[704,512]{1,0:T(8,128)(2,1)}, u32[]{:S(2)}, u32[]{:S(2)}) %collective-permute-start.111) | collective-permute-done | bytes 720928 | tf_op jit(solution)/shard_map/ppermute | solution.py:389
  580.5 13.1 %collective-permute-done.105 = bf16[704,512]{1,0:T(8,128)(2,1)} collective-permute-done((bf16[704,512]{1,0:T(8,128)(2,1)}, bf16[704,512]{1,0:T(8,128)(2,1)}, u32[]{:S(2)}, u32[]{:S(2)}) %collective-permute-start.105) | collective-permute-done | bytes 720928 | tf_op jit(solution)/shard_map/ppermute | solution.py:389
  593.6 3.5 multiply_reduce_fusion.6
  597.1 5.5 add_convert_fusion.2
  606.1 4.1 add_convert_fusion.3
  614.6 15.8 %collective-permute-done.74 = bf16[256,2048]{1,0:T(8,128)(2,1)S(1)} collective-permute-done((bf16[256,2048]{1,0:T(8,128)(2,1)}, bf16[256,2048]{1,0:T(8,128)(2,1)S(1)}, u32[]{:S(2)}, u32[]{:S(2)}) %collective-permute-start.74) | collective-permute-done | bytes 1048608 | tf_op jit(solution)/shard_map/ppermute | solution.py:395
  634.7 18.2 %collective-permute-done.54 = bf16[256,2048]{1,0:T(8,128)(2,1)S(1)} collective-permute-done((bf16[256,2048]{1,0:T(8,128)(2,1)S(1)}, bf16[256,2048]{1,0:T(8,128)(2,1)S(1)}, u32[]{:S(2)}, u32[]{:S(2)}) %collective-permute-start.54) | collective-permute-done | bytes 1048608 | tf_op jit(solution)/shard_map/ppermute | solution.py:395
  655.8 22.3 %collective-permute-done.77 = bf16[128,2048]{1,0:T(8,128)(2,1)S(1)} collective-permute-done((bf16[128,2048]{1,0:T(8,128)(2,1)S(1)}, bf16[128,2048]{1,0:T(8,128)(2,1)S(1)}, u32[]{:S(2)}, u32[]{:S(2)}) %collective-permute-start.77) | collective-permute-done | bytes 524320 | tf_op jit(solution)/shard_map/ppermute | solution.py:395
  681.1 9.5 collective-permute-done.57
  692.2 3.2 fusion.71
  703.9 6.5 collective-permute-done.79
  715.8 9.6 %collective-permute-done.82 = bf16[128,2048]{1,0:T(8,128)(2,1)S(1)} collective-permute-done((bf16[128,2048]{1,0:T(8,128)(2,1)S(1)}, bf16[128,2048]{1,0:T(8,128)(2,1)S(1)}, u32[]{:S(2)}, u32[]{:S(2)}) %collective-permute-start.82) | collective-permute-done | bytes 524320 | tf_op jit(solution)/shard_map/ppermute | solution.py:398
  725.5 7.4 collective-permute-done.80
  734.6 8.3 collective-permute-done.83
  750.4 30.1 %mixer_backward.1 = (bf16[2048,768]{1,0:T(8,128)(2,1)S(1)}, f32[48,256]{1,0:T(8,128)S(1)}) custom-call(s32[2]{0:T(128)S(1)} %copy-done.4, f32[2048,768]{1,0:T(8,128)S(1)} %bitcast.146, f32[2048,256]{1,0:T(8,128)S(1)} %get-tuple-element.39.conv_ref, f32[2048,256]{1,0:T(8,128)S(1)} %fusion.85.grad_ref, f32[48,256]{1,0:T(8,128)S(1)} %concatenate.140.coef_ref), custom_call_target="tpu_custom_call" | custom-call | flops 60000000 | bytes 16777216 | tf_op jit(solution)/shard_map/mixer_backward/pallas_call | solution.py:302
  781.3 7.1 convolution_convert_fusion
  796.7 9.2 convolution_convert_fusion.3
  812.9 4.2 collective-permute-done.100
  819.3 18.7 %collective-permute-done.101 = bf16[256,512]{1,0:T(8,128)(2,1)S(1)} collective-permute-done((bf16[256,512]{1,0:T(8,128)(2,1)S(1)}, bf16[256,512]{1,0:T(8,128)(2,1)S(1)}, u32[]{:S(2)}, u32[]{:S(2)}) %collective-permute-start.101) | collective-permute-done | bytes 262176 | tf_op jit(solution)/shard_map/ppermute | solution.py:389
  846.2 3.9 collective-permute-done.102
  852.4 12.1 %collective-permute-done.98 = bf16[768,512]{1,0:T(8,128)(2,1)S(1)} collective-permute-done((bf16[768,512]{1,0:T(8,128)(2,1)S(1)}, bf16[768,512]{1,0:T(8,128)(2,1)S(1)}, u32[]{:S(2)}, u32[]{:S(2)}) %collective-permute-start.98) | collective-permute-done | bytes 786464 | tf_op jit(solution)/shard_map/ppermute | solution.py:389
  870.7 13.0 %collective-permute-done.99 = bf16[768,512]{1,0:T(8,128)(2,1)S(1)} collective-permute-done((bf16[768,512]{1,0:T(8,128)(2,1)S(1)}, bf16[768,512]{1,0:T(8,128)(2,1)S(1)}, u32[]{:S(2)}, u32[]{:S(2)}) %collective-permute-start.99) | collective-permute-done | bytes 786464 | tf_op jit(solution)/shard_map/ppermute | solution.py:389
  893.1 3.4 collective-permute-done.94
  903.6 3.3 collective-permute-done.113
  921.5 3.1 fusion.22
  (668 shorter events, 287.0 us)
Async XLA Ops:
  7.8 32.3 %collective-permute-start.1 = (bf16[128,2048]{1,0:T(8,128)(2,1)}, bf16[128,2048]{1,0:T(8,128)(2,1)}, u32[]{:S(2)}, u32[]{:S(2)}) collective-permute-start(bf16[128,2048]{1,0:T(8,128)(2,1)} %get-tuple-element.134), channel_id=1, source_target_pairs={{0,4},{4,0},{8,12},{12,8},{16,20},{20,16},{24,28},{28,24},{1,5},{5... | collective-permute-start | bytes 1572872 | tf_op jit(solution)/shard_map/ppermute | solution.py:395
  10.7 30.9 %collective-permute-start = (bf16[128,2048]{1,0:T(8,128)(2,1)}, bf16[128,2048]{1,0:T(8,128)(2,1)}, u32[]{:S(2)}, u32[]{:S(2)}) collective-permute-start(bf16[128,2048]{1,0:T(8,128)(2,1)} %get-tuple-element.134), channel_id=1, source_target_pairs={{0,2},{1,3},{2,0},{3,1},{4,6},{5,7},{6,4},{7,5},{8,10},{9,11},{10,... | collective-permute-start | bytes 1572872 | tf_op jit(solution)/shard_map/ppermute | solution.py:398
  13.9 24.3 %collective-permute-start.14 = (bf16[768,256]{1,0:T(8,128)(2,1)S(1)}, bf16[768,256]{1,0:T(8,128)(2,1)}, u32[]{:S(2)}, u32[]{:S(2)}) collective-permute-start(bf16[768,256]{1,0:T(8,128)(2,1)S(1)} %get-tuple-element.135), channel_id=1, source_target_pairs={{0,4},{4,0},{8,12},{12,8},{16,20},{20,16},{24,28},{28,24},{1,5},{5... | collective-permute-start | bytes 1179656 | tf_op jit(solution)/shard_map/ppermute | solution.py:395
  15.5 63.1 %collective-permute-start.10 = (bf16[128,2048]{1,0:T(8,128)(2,1)}, bf16[128,2048]{1,0:T(8,128)(2,1)}, u32[]{:S(2)}, u32[]{:S(2)}) collective-permute-start(bf16[128,2048]{1,0:T(8,128)(2,1)} %get-tuple-element.132), channel_id=1, source_target_pairs={{0,1},{1,0},{2,3},{3,2},{4,5},{5,4},{6,7},{7,6},{8,9},{9,8},{10,11... | collective-permute-start | bytes 1572872 | tf_op jit(solution)/shard_map/ppermute | solution.py:401
  40.1 21.7 %collective-permute-start.3 = (bf16[128,2048]{1,0:T(8,128)(2,1)}, bf16[128,2048]{1,0:T(8,128)(2,1)S(1)}, u32[]{:S(2)}, u32[]{:S(2)}) collective-permute-start(bf16[128,2048]{1,0:T(8,128)(2,1)} %get-tuple-element.132), channel_id=1, source_target_pairs={{0,4},{4,0},{8,12},{12,8},{16,20},{20,16},{24,28},{28,24},{1,5},{5... | collective-permute-start | bytes 1572872 | tf_op jit(solution)/shard_map/ppermute | solution.py:395
  54.9 21.8 %collective-permute-start.15 = (bf16[768,512]{1,0:T(8,128)(2,1)S(1)}, bf16[768,512]{1,0:T(8,128)(2,1)S(1)}, u32[]{:S(2)}, u32[]{:S(2)}) collective-permute-start(bf16[768,512]{1,0:T(8,128)(2,1)S(1)} %get-tuple-element.103), channel_id=1, source_target_pairs={{0,8},{4,12},{8,16},{12,20},{16,24},{20,28},{24,0},{28,4},{1,9},{5... | collective-permute-start | bytes 2359304 | tf_op jit(solution)/shard_map/ppermute | solution.py:389
  70.2 28.5 %collective-permute-start.12 = (bf16[128,2048]{1,0:T(8,128)(2,1)S(1)}, bf16[128,2048]{1,0:T(8,128)(2,1)S(1)}, u32[]{:S(2)}, u32[]{:S(2)}) collective-permute-start(bf16[128,2048]{1,0:T(8,128)(2,1)S(1)} %collective-permute-done.4), channel_id=1, source_target_pairs={{0,1},{1,0},{2,3},{3,2},{4,5},{5,4},{6,7},{7,6},{8,9},{9,8},{10,11... | collective-permute-start | bytes 1572872 | tf_op jit(solution)/shard_map/ppermute | solution.py:401
  72.5 25.4 %collective-permute-start.11 = (bf16[128,2048]{1,0:T(8,128)(2,1)S(1)}, bf16[128,2048]{1,0:T(8,128)(2,1)S(1)}, u32[]{:S(2)}, u32[]{:S(2)}) collective-permute-start(bf16[128,2048]{1,0:T(8,128)(2,1)S(1)} %collective-permute-done.3), channel_id=1, source_target_pairs={{0,1},{1,0},{2,3},{3,2},{4,5},{5,4},{6,7},{7,6},{8,9},{9,8},{10,11... | collective-permute-start | bytes 1572872 | tf_op jit(solution)/shard_map/ppermute | solution.py:401
  76.7 21.0 %collective-permute-start.16 = (bf16[768,512]{1,0:T(8,128)(2,1)S(1)}, bf16[768,512]{1,0:T(8,128)(2,1)S(1)}, u32[]{:S(2)}, u32[]{:S(2)}) collective-permute-start(bf16[768,512]{1,0:T(8,128)(2,1)S(1)} %collective-permute-done.15), channel_id=1, source_target_pairs={{0,8},{4,12},{8,16},{12,20},{16,24},{20,28},{24,0},{28,4},{1,9},{5... | collective-permute-start | bytes 2359304 | tf_op jit(solution)/shard_map/ppermute | solution.py:389
  77.7 21.9 %collective-permute-start.13 = (bf16[128,2048]{1,0:T(8,128)(2,1)S(1)}, bf16[128,2048]{1,0:T(8,128)(2,1)S(1)}, u32[]{:S(2)}, u32[]{:S(2)}) collective-permute-start(bf16[128,2048]{1,0:T(8,128)(2,1)S(1)} %collective-permute-done.5), channel_id=1, source_target_pairs={{0,1},{1,0},{2,3},{3,2},{4,5},{5,4},{6,7},{7,6},{8,9},{9,8},{10,11... | collective-permute-start | bytes 1572872 | tf_op jit(solution)/shard_map/ppermute | solution.py:401
  149.1 73.4 %collective-permute-start.22 = (bf16[1024,2048]{1,0:T(8,128)(2,1)}, bf16[1024,2048]{1,0:T(8,128)(2,1)}, u32[]{:S(2)}, u32[]{:S(2)}) collective-permute-start(bf16[1024,2048]{1,0:T(8,128)(2,1)} %slice.265), channel_id=1, source_target_pairs={{0,1},{1,0},{2,3},{3,2},{4,5},{5,4},{6,7},{7,6},{8,9},{9,8},{10,11... | collective-permute-start | bytes 12582920 | tf_op jit(solution)/shard_map/ppermute | solution.py:401
  156.3 22.8 %collective-permute-start.41 = (bf16[704,256]{1,0:T(8,128)(2,1)}, bf16[704,256]{1,0:T(8,128)(2,1)}, u32[]{:S(2)}, u32[]{:S(2)}) collective-permute-start(bf16[704,256]{1,0:T(8,128)(2,1)} %get-tuple-element.137), channel_id=1, source_target_pairs={{0,4},{4,0},{8,12},{12,8},{16,20},{20,16},{24,28},{28,24},{1,5},{5... | collective-permute-start | bytes 1081352 | tf_op jit(solution)/shard_map/ppermute | solution.py:395
  164.1 30.2 %collective-permute-start.59 = (bf16[128,2048]{1,0:T(8,128)(2,1)}, bf16[128,2048]{1,0:T(8,128)(2,1)}, u32[]{:S(2)}, u32[]{:S(2)}) collective-permute-start(bf16[128,2048]{1,0:T(8,128)(2,1)} %get-tuple-element.128), channel_id=1, source_target_pairs={{0,4},{4,0},{8,12},{12,8},{16,20},{20,16},{24,28},{28,24},{1,5},{5... | collective-permute-start | bytes 1572872 | tf_op jit(solution)/shard_map/ppermute | solution.py:395
  168.1 27.8 %collective-permute-start.58 = (bf16[128,2048]{1,0:T(8,128)(2,1)}, bf16[128,2048]{1,0:T(8,128)(2,1)S(1)}, u32[]{:S(2)}, u32[]{:S(2)}) collective-permute-start(bf16[128,2048]{1,0:T(8,128)(2,1)} %get-tuple-element.128), channel_id=1, source_target_pairs={{0,2},{1,3},{2,0},{3,1},{4,6},{5,7},{6,4},{7,5},{8,10},{9,11},{10,... | collective-permute-start | bytes 1572872 | tf_op jit(solution)/shard_map/ppermute | solution.py:398
  195.9 24.6 %collective-permute-start.64 = (bf16[128,2048]{1,0:T(8,128)(2,1)}, bf16[128,2048]{1,0:T(8,128)(2,1)S(1)}, u32[]{:S(2)}, u32[]{:S(2)}) collective-permute-start(bf16[128,2048]{1,0:T(8,128)(2,1)} %get-tuple-element.128), channel_id=1, source_target_pairs={{0,1},{1,0},{2,3},{3,2},{4,5},{5,4},{6,7},{7,6},{8,9},{9,8},{10,11... | collective-permute-start | bytes 1572872 | tf_op jit(solution)/shard_map/ppermute | solution.py:401
  198.8 30.9 %collective-permute-start.46 = (bf16[704,512]{1,0:T(8,128)(2,1)S(1)}, bf16[704,512]{1,0:T(8,128)(2,1)S(1)}, u32[]{:S(2)}, u32[]{:S(2)}) collective-permute-start(bf16[704,512]{1,0:T(8,128)(2,1)S(1)} %get-tuple-element.95), channel_id=1, source_target_pairs={{0,8},{4,12},{8,16},{12,20},{16,24},{20,28},{24,0},{28,4},{1,9},{5... | collective-permute-start | bytes 2162696 | tf_op jit(solution)/shard_map/ppermute | solution.py:389
  219.6 21.1 %collective-permute-start.42 = (bf16[704,512]{1,0:T(8,128)(2,1)}, bf16[704,512]{1,0:T(8,128)(2,1)S(1)}, u32[]{:S(2)}, u32[]{:S(2)}) collective-permute-start(bf16[704,512]{1,0:T(8,128)(2,1)} %get-tuple-element.93), channel_id=1, source_target_pairs={{0,8},{4,12},{8,16},{12,20},{16,24},{20,28},{24,0},{28,4},{1,9},{5... | collective-permute-start | bytes 2162696 | tf_op jit(solution)/shard_map/ppermute | solution.py:389
  220.5 32.0 %collective-permute-start.50 = (bf16[704,512]{1,0:T(8,128)(2,1)}, bf16[704,512]{1,0:T(8,128)(2,1)}, u32[]{:S(2)}, u32[]{:S(2)}) collective-permute-start(bf16[704,512]{1,0:T(8,128)(2,1)} %get-tuple-element.99), channel_id=1, source_target_pairs={{0,8},{4,12},{8,16},{12,20},{16,24},{20,28},{24,0},{28,4},{1,9},{5... | collective-permute-start | bytes 2162696 | tf_op jit(solution)/shard_map/ppermute | solution.py:389
  222.4 31.2 %collective-permute-start.67 = (bf16[128,2048]{1,0:T(8,128)(2,1)}, bf16[128,2048]{1,0:T(8,128)(2,1)}, u32[]{:S(2)}, u32[]{:S(2)}) collective-permute-start(bf16[128,2048]{1,0:T(8,128)(2,1)} %collective-permute-done.60), channel_id=1, source_target_pairs={{0,1},{1,0},{2,3},{3,2},{4,5},{5,4},{6,7},{7,6},{8,9},{9,8},{10,11... | collective-permute-start | bytes 1572872 | tf_op jit(solution)/shard_map/ppermute | solution.py:401
  228.2 28.8 %collective-permute-start.23 = (bf16[256,2048]{1,0:T(8,128)(2,1)S(1)}, bf16[256,2048]{1,0:T(8,128)(2,1)S(1)}, u32[]{:S(2)}, u32[]{:S(2)}) collective-permute-start(bf16[256,2048]{1,0:T(8,128)(2,1)S(1)} %get-tuple-element.120), channel_id=1, source_target_pairs={{0,4},{4,0},{8,12},{12,8},{16,20},{20,16},{24,28},{28,24},{1,5},{5... | collective-permute-start | bytes 3145736 | tf_op jit(solution)/shard_map/ppermute | solution.py:395
  230.6 26.6 %collective-permute-start.25 = (bf16[256,2048]{1,0:T(8,128)(2,1)S(1)}, bf16[256,2048]{1,0:T(8,128)(2,1)S(1)}, u32[]{:S(2)}, u32[]{:S(2)}) collective-permute-start(bf16[256,2048]{1,0:T(8,128)(2,1)S(1)} %get-tuple-element.121), channel_id=1, source_target_pairs={{0,2},{1,3},{2,0},{3,1},{4,6},{5,7},{6,4},{7,5},{8,10},{9,11},{10,... | collective-permute-start | bytes 3145736 | tf_op jit(solution)/shard_map/ppermute | solution.py:398
  257.1 36.2 %collective-permute-start.43 = (bf16[704,512]{1,0:T(8,128)(2,1)S(1)}, bf16[704,512]{1,0:T(8,128)(2,1)S(1)}, u32[]{:S(2)}, u32[]{:S(2)}) collective-permute-start(bf16[704,512]{1,0:T(8,128)(2,1)S(1)} %collective-permute-done.42), channel_id=1, source_target_pairs={{0,8},{4,12},{8,16},{12,20},{16,24},{20,28},{24,0},{28,4},{1,9},{5... | collective-permute-start | bytes 2162696 | tf_op jit(solution)/shard_map/ppermute | solution.py:389
  257.1 51.5 %collective-permute-start.51 = (bf16[704,512]{1,0:T(8,128)(2,1)}, bf16[704,512]{1,0:T(8,128)(2,1)S(1)}, u32[]{:S(2)}, u32[]{:S(2)}) collective-permute-start(bf16[704,512]{1,0:T(8,128)(2,1)} %collective-permute-done.50), channel_id=1, source_target_pairs={{0,8},{4,12},{8,16},{12,20},{16,24},{20,28},{24,0},{28,4},{1,9},{5... | collective-permute-start | bytes 2162696 | tf_op jit(solution)/shard_map/ppermute | solution.py:389
  259.1 49.6 %collective-permute-start.26 = (bf16[128,2048]{1,0:T(8,128)(2,1)S(1)}, bf16[128,2048]{1,0:T(8,128)(2,1)S(1)}, u32[]{:S(2)}, u32[]{:S(2)}) collective-permute-start(bf16[128,2048]{1,0:T(8,128)(2,1)S(1)} %slice.273), channel_id=1, source_target_pairs={{0,4},{4,0},{8,12},{12,8},{16,20},{20,16},{24,28},{28,24},{1,5},{5... | collective-permute-start | bytes 1572872 | tf_op jit(solution)/shard_map/ppermute | solution.py:395
  262.4 46.4 %collective-permute-start.24 = (bf16[128,2048]{1,0:T(8,128)(2,1)S(1)}, bf16[128,2048]{1,0:T(8,128)(2,1)S(1)}, u32[]{:S(2)}, u32[]{:S(2)}) collective-permute-start(bf16[128,2048]{1,0:T(8,128)(2,1)S(1)} %slice.269), channel_id=1, source_target_pairs={{0,2},{1,3},{2,0},{3,1},{4,6},{5,7},{6,4},{7,5},{8,10},{9,11},{10,... | collective-permute-start | bytes 1572872 | tf_op jit(solution)/shard_map/ppermute | solution.py:398
  277.8 46.3 %collective-permute-start.48 = (bf16[704,512]{1,0:T(8,128)(2,1)S(1)}, bf16[704,512]{1,0:T(8,128)(2,1)S(1)}, u32[]{:S(2)}, u32[]{:S(2)}) collective-permute-start(bf16[704,512]{1,0:T(8,128)(2,1)S(1)} %collective-permute-done.47), channel_id=1, source_target_pairs={{0,8},{4,12},{8,16},{12,20},{16,24},{20,28},{24,0},{28,4},{1,9},{5... | collective-permute-start | bytes 2162696 | tf_op jit(solution)/shard_map/ppermute | solution.py:389
  293.2 46.3 %collective-permute-start.44 = (bf16[704,512]{1,0:T(8,128)(2,1)S(1)}, bf16[704,512]{1,0:T(8,128)(2,1)S(1)}, u32[]{:S(2)}, u32[]{:S(2)}) collective-permute-start(bf16[704,512]{1,0:T(8,128)(2,1)S(1)} %collective-permute-done.43), channel_id=1, source_target_pairs={{0,8},{4,12},{8,16},{12,20},{16,24},{20,28},{24,0},{28,4},{1,9},{5... | collective-permute-start | bytes 2162696 | tf_op jit(solution)/shard_map/ppermute | solution.py:389
  308.7 46.0 %collective-permute-start.52 = (bf16[704,512]{1,0:T(8,128)(2,1)S(1)}, bf16[704,512]{1,0:T(8,128)(2,1)S(1)}, u32[]{:S(2)}, u32[]{:S(2)}) collective-permute-start(bf16[704,512]{1,0:T(8,128)(2,1)S(1)} %collective-permute-done.51), channel_id=1, source_target_pairs={{0,8},{4,12},{8,16},{12,20},{16,24},{20,28},{24,0},{28,4},{1,9},{5... | collective-permute-start | bytes 2162696 | tf_op jit(solution)/shard_map/ppermute | solution.py:389
  310.7 29.0 %collective-permute-start.28 = (bf16[128,2048]{1,0:T(8,128)(2,1)S(1)}, bf16[128,2048]{1,0:T(8,128)(2,1)S(1)}, u32[]{:S(2)}, u32[]{:S(2)}) collective-permute-start(bf16[128,2048]{1,0:T(8,128)(2,1)S(1)} %get-tuple-element.131), channel_id=1, source_target_pairs={{0,4},{4,0},{8,12},{12,8},{16,20},{20,16},{24,28},{28,24},{1,5},{5... | collective-permute-start | bytes 1572872 | tf_op jit(solution)/shard_map/ppermute | solution.py:395
  312.2 44.3 %collective-permute-start.27 = (bf16[128,2048]{1,0:T(8,128)(2,1)S(1)}, bf16[128,2048]{1,0:T(8,128)(2,1)S(1)}, u32[]{:S(2)}, u32[]{:S(2)}) collective-permute-start(bf16[128,2048]{1,0:T(8,128)(2,1)S(1)} %get-tuple-element.131), channel_id=1, source_target_pairs={{0,2},{1,3},{2,0},{3,1},{4,6},{5,7},{6,4},{7,5},{8,10},{9,11},{10,... | collective-permute-start | bytes 1572872 | tf_op jit(solution)/shard_map/ppermute | solution.py:398
  324.1 32.3 %collective-permute-start.31 = (bf16[128,2048]{1,0:T(8,128)(2,1)S(1)}, bf16[128,2048]{1,0:T(8,128)(2,1)S(1)}, u32[]{:S(2)}, u32[]{:S(2)}) collective-permute-start(bf16[128,2048]{1,0:T(8,128)(2,1)S(1)} %get-tuple-element.129), channel_id=1, source_target_pairs={{0,2},{1,3},{2,0},{3,1},{4,6},{5,7},{6,4},{7,5},{8,10},{9,11},{10,... | collective-permute-start | bytes 1572872 | tf_op jit(solution)/shard_map/ppermute | solution.py:398
  354.7 28.4 %collective-permute-start.37 = (bf16[128,2048]{1,0:T(8,128)(2,1)S(1)}, bf16[128,2048]{1,0:T(8,128)(2,1)S(1)}, u32[]{:S(2)}, u32[]{:S(2)}) collective-permute-start(bf16[128,2048]{1,0:T(8,128)(2,1)S(1)} %get-tuple-element.129), channel_id=1, source_target_pairs={{0,1},{1,0},{2,3},{3,2},{4,5},{5,4},{6,7},{7,6},{8,9},{9,8},{10,11... | collective-permute-start | bytes 1572872 | tf_op jit(solution)/shard_map/ppermute | solution.py:401
  356.4 24.1 %collective-permute-start.33 = (bf16[128,2048]{1,0:T(8,128)(2,1)S(1)}, bf16[128,2048]{1,0:T(8,128)(2,1)S(1)}, u32[]{:S(2)}, u32[]{:S(2)}) collective-permute-start(bf16[128,2048]{1,0:T(8,128)(2,1)S(1)} %get-tuple-element.131), channel_id=1, source_target_pairs={{0,1},{1,0},{2,3},{3,2},{4,5},{5,4},{6,7},{7,6},{8,9},{9,8},{10,11... | collective-permute-start | bytes 1572872 | tf_op jit(solution)/shard_map/ppermute | solution.py:401
  356.6 27.3 %collective-permute-start.39 = (bf16[128,2048]{1,0:T(8,128)(2,1)S(1)}, bf16[128,2048]{1,0:T(8,128)(2,1)S(1)}, u32[]{:S(2)}, u32[]{:S(2)}) collective-permute-start(bf16[128,2048]{1,0:T(8,128)(2,1)S(1)} %collective-permute-done.31), channel_id=1, source_target_pairs={{0,1},{1,0},{2,3},{3,2},{4,5},{5,4},{6,7},{7,6},{8,9},{9,8},{10,11... | collective-permute-start | bytes 1572872 | tf_op jit(solution)/shard_map/ppermute | solution.py:401
  357.0 23.4 %collective-permute-start.32 = (bf16[128,2048]{1,0:T(8,128)(2,1)S(1)}, bf16[128,2048]{1,0:T(8,128)(2,1)S(1)}, u32[]{:S(2)}, u32[]{:S(2)}) collective-permute-start(bf16[128,2048]{1,0:T(8,128)(2,1)S(1)} %collective-permute-done.31), channel_id=1, source_target_pairs={{0,4},{4,0},{8,12},{12,8},{16,20},{20,16},{24,28},{28,24},{1,5},{5... | collective-permute-start | bytes 1572872 | tf_op jit(solution)/shard_map/ppermute | solution.py:395
  445.5 160.6 %collective-permute-start.53 = (bf16[1024,2048]{1,0:T(8,128)(2,1)}, bf16[1024,2048]{1,0:T(8,128)(2,1)}, u32[]{:S(2)}, u32[]{:S(2)}) collective-permute-start(bf16[1024,2048]{1,0:T(8,128)(2,1)} %slice.277), channel_id=1, source_target_pairs={{0,1},{1,0},{2,3},{3,2},{4,5},{5,4},{6,7},{7,6},{8,9},{9,8},{10,11... | collective-permute-start | bytes 12582920 | tf_op jit(solution)/shard_map/ppermute | solution.py:401
  446.5 48.9 %collective-permute-start.109 = (bf16[704,512]{1,0:T(8,128)(2,1)}, bf16[704,512]{1,0:T(8,128)(2,1)}, u32[]{:S(2)}, u32[]{:S(2)}) collective-permute-start(bf16[704,512]{1,0:T(8,128)(2,1)} %constant_dynamic-slice_fusion.1), channel_id=1, source_target_pairs={{0,8},{4,12},{8,16},{12,20},{16,24},{20,28},{24,0},{28,4},{1,9},{5... | collective-permute-start | bytes 2162696 | tf_op jit(solution)/shard_map/ppermute | solution.py:389
  458.2 43.7 %collective-permute-start.103 = (bf16[704,512]{1,0:T(8,128)(2,1)}, bf16[704,512]{1,0:T(8,128)(2,1)S(1)}, u32[]{:S(2)}, u32[]{:S(2)}) collective-permute-start(bf16[704,512]{1,0:T(8,128)(2,1)} %constant_dynamic-slice_fusion.3), channel_id=1, source_target_pairs={{0,8},{4,12},{8,16},{12,20},{16,24},{20,28},{24,0},{28,4},{1,9},{5... | collective-permute-start | bytes 2162696 | tf_op jit(solution)/shard_map/ppermute | solution.py:389
  485.6 111.5 %collective-permute-start.73 = (bf16[1024,2048]{1,0:T(8,128)(2,1)}, bf16[1024,2048]{1,0:T(8,128)(2,1)}, u32[]{:S(2)}, u32[]{:S(2)}) collective-permute-start(bf16[1024,2048]{1,0:T(8,128)(2,1)} %slice.287), channel_id=1, source_target_pairs={{0,1},{1,0},{2,3},{3,2},{4,5},{5,4},{6,7},{7,6},{8,9},{9,8},{10,11... | collective-permute-start | bytes 12582920 | tf_op jit(solution)/shard_map/ppermute | solution.py:401
  495.3 20.9 %collective-permute-start.106 = (bf16[704,512]{1,0:T(8,128)(2,1)}, bf16[704,512]{1,0:T(8,128)(2,1)S(1)}, u32[]{:S(2)}, u32[]{:S(2)}) collective-permute-start(bf16[704,512]{1,0:T(8,128)(2,1)} %constant_dynamic-slice_fusion.2), channel_id=1, source_target_pairs={{0,8},{4,12},{8,16},{12,20},{16,24},{20,28},{24,0},{28,4},{1,9},{5... | collective-permute-start | bytes 2162696 | tf_op jit(solution)/shard_map/ppermute | solution.py:389
  497.7 34.1 %collective-permute-start.110 = (bf16[704,512]{1,0:T(8,128)(2,1)}, bf16[704,512]{1,0:T(8,128)(2,1)}, u32[]{:S(2)}, u32[]{:S(2)}) collective-permute-start(bf16[704,512]{1,0:T(8,128)(2,1)} %add_convert_fusion.16), channel_id=1, source_target_pairs={{0,8},{4,12},{8,16},{12,20},{16,24},{20,28},{24,0},{28,4},{1,9},{5... | collective-permute-start | bytes 2162696 | tf_op jit(solution)/shard_map/ppermute | solution.py:389
  504.1 43.2 %collective-permute-start.104 = (bf16[704,512]{1,0:T(8,128)(2,1)}, bf16[704,512]{1,0:T(8,128)(2,1)}, u32[]{:S(2)}, u32[]{:S(2)}) collective-permute-start(bf16[704,512]{1,0:T(8,128)(2,1)} %add_convert_fusion.20), channel_id=1, source_target_pairs={{0,8},{4,12},{8,16},{12,20},{16,24},{20,28},{24,0},{28,4},{1,9},{5... | collective-permute-start | bytes 2162696 | tf_op jit(solution)/shard_map/ppermute | solution.py:389
  518.4 44.2 %collective-permute-start.107 = (bf16[704,512]{1,0:T(8,128)(2,1)}, bf16[704,512]{1,0:T(8,128)(2,1)S(1)}, u32[]{:S(2)}, u32[]{:S(2)}) collective-permute-start(bf16[704,512]{1,0:T(8,128)(2,1)} %add_convert_fusion.18), channel_id=1, source_target_pairs={{0,8},{4,12},{8,16},{12,20},{16,24},{20,28},{24,0},{28,4},{1,9},{5... | collective-permute-start | bytes 2162696 | tf_op jit(solution)/shard_map/ppermute | solution.py:389
  534.2 44.0 %collective-permute-start.111 = (bf16[704,512]{1,0:T(8,128)(2,1)}, bf16[704,512]{1,0:T(8,128)(2,1)}, u32[]{:S(2)}, u32[]{:S(2)}) collective-permute-start(bf16[704,512]{1,0:T(8,128)(2,1)} %add_convert_fusion.15), channel_id=1, source_target_pairs={{0,8},{4,12},{8,16},{12,20},{16,24},{20,28},{24,0},{28,4},{1,9},{5... | collective-permute-start | bytes 2162696 | tf_op jit(solution)/shard_map/ppermute | solution.py:389
  549.6 44.0 %collective-permute-start.105 = (bf16[704,512]{1,0:T(8,128)(2,1)}, bf16[704,512]{1,0:T(8,128)(2,1)}, u32[]{:S(2)}, u32[]{:S(2)}) collective-permute-start(bf16[704,512]{1,0:T(8,128)(2,1)} %add_convert_fusion.19), channel_id=1, source_target_pairs={{0,8},{4,12},{8,16},{12,20},{16,24},{20,28},{24,0},{28,4},{1,9},{5... | collective-permute-start | bytes 2162696 | tf_op jit(solution)/shard_map/ppermute | solution.py:389
  563.9 132.2 %collective-permute-start.108 = (bf16[704,512]{1,0:T(8,128)(2,1)S(1)}, bf16[704,512]{1,0:T(8,128)(2,1)}, u32[]{:S(2)}, u32[]{:S(2)}) collective-permute-start(bf16[704,512]{1,0:T(8,128)(2,1)S(1)} %add_convert_fusion.17), channel_id=1, source_target_pairs={{0,8},{4,12},{8,16},{12,20},{16,24},{20,28},{24,0},{28,4},{1,9},{5... | collective-permute-start | bytes 2162696 | tf_op jit(solution)/shard_map/ppermute | solution.py:389
  604.1 26.3 %collective-permute-start.74 = (bf16[256,2048]{1,0:T(8,128)(2,1)}, bf16[256,2048]{1,0:T(8,128)(2,1)S(1)}, u32[]{:S(2)}, u32[]{:S(2)}) collective-permute-start(bf16[256,2048]{1,0:T(8,128)(2,1)} %get-tuple-element.112), channel_id=1, source_target_pairs={{0,4},{4,0},{8,12},{12,8},{16,20},{20,16},{24,28},{28,24},{1,5},{5... | collective-permute-start | bytes 3145736 | tf_op jit(solution)/shard_map/ppermute | solution.py:395
  605.6 26.4 %collective-permute-start.76 = (bf16[256,2048]{1,0:T(8,128)(2,1)}, bf16[256,2048]{1,0:T(8,128)(2,1)}, u32[]{:S(2)}, u32[]{:S(2)}) collective-permute-start(bf16[256,2048]{1,0:T(8,128)(2,1)} %get-tuple-element.113), channel_id=1, source_target_pairs={{0,2},{1,3},{2,0},{3,1},{4,6},{5,7},{6,4},{7,5},{8,10},{9,11},{10,... | collective-permute-start | bytes 3145736 | tf_op jit(solution)/shard_map/ppermute | solution.py:398
  610.5 42.4 %collective-permute-start.54 = (bf16[256,2048]{1,0:T(8,128)(2,1)S(1)}, bf16[256,2048]{1,0:T(8,128)(2,1)S(1)}, u32[]{:S(2)}, u32[]{:S(2)}) collective-permute-start(bf16[256,2048]{1,0:T(8,128)(2,1)S(1)} %get-tuple-element.116), channel_id=1, source_target_pairs={{0,4},{4,0},{8,12},{12,8},{16,20},{20,16},{24,28},{28,24},{1,5},{5... | collective-permute-start | bytes 3145736 | tf_op jit(solution)/shard_map/ppermute | solution.py:395
  611.3 43.1 %collective-permute-start.56 = (bf16[256,2048]{1,0:T(8,128)(2,1)S(1)}, bf16[256,2048]{1,0:T(8,128)(2,1)S(1)}, u32[]{:S(2)}, u32[]{:S(2)}) collective-permute-start(bf16[256,2048]{1,0:T(8,128)(2,1)S(1)} %get-tuple-element.117), channel_id=1, source_target_pairs={{0,2},{1,3},{2,0},{3,1},{4,6},{5,7},{6,4},{7,5},{8,10},{9,11},{10,... | collective-permute-start | bytes 3145736 | tf_op jit(solution)/shard_map/ppermute | solution.py:398
  630.4 71.1 %collective-permute-start.128 = (bf16[704,256]{1,0:T(8,128)(2,1)S(1)}, bf16[704,256]{1,0:T(8,128)(2,1)S(1)}, u32[]{:S(2)}, u32[]{:S(2)}) collective-permute-start(bf16[704,256]{1,0:T(8,128)(2,1)S(1)} %dynamic-slice_convert_fusion.1), channel_id=1, source_target_pairs={{0,4},{4,0},{8,12},{12,8},{16,20},{20,16},{24,28},{28,24},{1,5},{5... | collective-permute-start | bytes 1081352 | tf_op jit(solution)/shard_map/ppermute | solution.py:395
  632.0 78.9 %collective-permute-start.126 = (bf16[704,256]{1,0:T(8,128)(2,1)S(1)}, bf16[704,256]{1,0:T(8,128)(2,1)S(1)}, u32[]{:S(2)}, u32[]{:S(2)}) collective-permute-start(bf16[704,256]{1,0:T(8,128)(2,1)S(1)} %dynamic-slice_convert_fusion.3), channel_id=1, source_target_pairs={{0,4},{4,0},{8,12},{12,8},{16,20},{20,16},{24,28},{28,24},{1,5},{5... | collective-permute-start | bytes 1081352 | tf_op jit(solution)/shard_map/ppermute | solution.py:395
  652.9 25.2 %collective-permute-start.77 = (bf16[128,2048]{1,0:T(8,128)(2,1)S(1)}, bf16[128,2048]{1,0:T(8,128)(2,1)S(1)}, u32[]{:S(2)}, u32[]{:S(2)}) collective-permute-start(bf16[128,2048]{1,0:T(8,128)(2,1)S(1)} %slice.295), channel_id=1, source_target_pairs={{0,4},{4,0},{8,12},{12,8},{16,20},{20,16},{24,28},{28,24},{1,5},{5... | collective-permute-start | bytes 1572872 | tf_op jit(solution)/shard_map/ppermute | solution.py:395
  654.4 25.4 %collective-permute-start.75 = (bf16[128,2048]{1,0:T(8,128)(2,1)S(1)}, bf16[128,2048]{1,0:T(8,128)(2,1)S(1)}, u32[]{:S(2)}, u32[]{:S(2)}) collective-permute-start(bf16[128,2048]{1,0:T(8,128)(2,1)S(1)} %slice.291), channel_id=1, source_target_pairs={{0,2},{1,3},{2,0},{3,1},{4,6},{5,7},{6,4},{7,5},{8,10},{9,11},{10,... | collective-permute-start | bytes 1572872 | tf_op jit(solution)/shard_map/ppermute | solution.py:398
  700.2 117.1 %collective-permute-start.127 = (bf16[704,256]{1,0:T(8,128)(2,1)S(1)}, bf16[704,256]{1,0:T(8,128)(2,1)S(1)}, u32[]{:S(2)}, u32[]{:S(2)}) collective-permute-start(bf16[704,256]{1,0:T(8,128)(2,1)S(1)} %dynamic-slice_convert_fusion.2), channel_id=1, source_target_pairs={{0,4},{4,0},{8,12},{12,8},{16,20},{20,16},{24,28},{28,24},{1,5},{5... | collective-permute-start | bytes 1081352 | tf_op jit(solution)/shard_map/ppermute | solution.py:395
  702.4 23.1 %collective-permute-start.82 = (bf16[128,2048]{1,0:T(8,128)(2,1)S(1)}, bf16[128,2048]{1,0:T(8,128)(2,1)S(1)}, u32[]{:S(2)}, u32[]{:S(2)}) collective-permute-start(bf16[128,2048]{1,0:T(8,128)(2,1)S(1)} %get-tuple-element.123), channel_id=1, source_target_pairs={{0,2},{1,3},{2,0},{3,1},{4,6},{5,7},{6,4},{7,5},{8,10},{9,11},{10,... | collective-permute-start | bytes 1572872 | tf_op jit(solution)/shard_map/ppermute | solution.py:398
  710.5 22.4 %collective-permute-start.80 = (bf16[128,2048]{1,0:T(8,128)(2,1)S(1)}, bf16[128,2048]{1,0:T(8,128)(2,1)S(1)}, u32[]{:S(2)}, u32[]{:S(2)}) collective-permute-start(bf16[128,2048]{1,0:T(8,128)(2,1)S(1)} %collective-permute-done.79), channel_id=1, source_target_pairs={{0,2},{1,3},{2,0},{3,1},{4,6},{5,7},{6,4},{7,5},{8,10},{9,11},{10,... | collective-permute-start | bytes 1572872 | tf_op jit(solution)/shard_map/ppermute | solution.py:398
  711.9 34.1 %collective-permute-start.88 = (bf16[128,2048]{1,0:T(8,128)(2,1)S(1)}, bf16[128,2048]{1,0:T(8,128)(2,1)S(1)}, u32[]{:S(2)}, u32[]{:S(2)}) collective-permute-start(bf16[128,2048]{1,0:T(8,128)(2,1)S(1)} %get-tuple-element.123), channel_id=1, source_target_pairs={{0,1},{1,0},{2,3},{3,2},{4,5},{5,4},{6,7},{7,6},{8,9},{9,8},{10,11... | collective-permute-start | bytes 1572872 | tf_op jit(solution)/shard_map/ppermute | solution.py:401
  791.0 48.8 %collective-permute-start.92 = (bf16[1024,2048]{1,0:T(8,128)(2,1)}, bf16[1024,2048]{1,0:T(8,128)(2,1)S(1)}, u32[]{:S(2)}, u32[]{:S(2)}) collective-permute-start(bf16[1024,2048]{1,0:T(8,128)(2,1)} %slice.299), channel_id=1, source_target_pairs={{0,1},{1,0},{2,3},{3,2},{4,5},{5,4},{6,7},{7,6},{8,9},{9,8},{10,11... | collective-permute-start | bytes 12582920 | tf_op jit(solution)/shard_map/ppermute | solution.py:401
  808.1 30.7 %collective-permute-start.97 = (bf16[768,512]{1,0:T(8,128)(2,1)S(1)}, bf16[768,512]{1,0:T(8,128)(2,1)S(1)}, u32[]{:S(2)}, u32[]{:S(2)}) collective-permute-start(bf16[768,512]{1,0:T(8,128)(2,1)S(1)} %constant_dynamic-slice_fusion.5), channel_id=1, source_target_pairs={{0,8},{4,12},{8,16},{12,20},{16,24},{20,28},{24,0},{28,4},{1,9},{5... | collective-permute-start | bytes 2359304 | tf_op jit(solution)/shard_map/ppermute | solution.py:389
  839.1 25.4 %collective-permute-start.98 = (bf16[768,512]{1,0:T(8,128)(2,1)S(1)}, bf16[768,512]{1,0:T(8,128)(2,1)S(1)}, u32[]{:S(2)}, u32[]{:S(2)}) collective-permute-start(bf16[768,512]{1,0:T(8,128)(2,1)S(1)} %add_convert_fusion.14), channel_id=1, source_target_pairs={{0,8},{4,12},{8,16},{12,20},{16,24},{20,28},{24,0},{28,4},{1,9},{5... | collective-permute-start | bytes 2359304 | tf_op jit(solution)/shard_map/ppermute | solution.py:389
  842.3 24.6 %collective-permute-start.93 = (bf16[256,2048]{1,0:T(8,128)(2,1)S(1)}, bf16[256,2048]{1,0:T(8,128)(2,1)S(1)}, u32[]{:S(2)}, u32[]{:S(2)}) collective-permute-start(bf16[256,2048]{1,0:T(8,128)(2,1)S(1)} %get-tuple-element.108), channel_id=1, source_target_pairs={{0,4},{4,0},{8,12},{12,8},{16,20},{20,16},{24,28},{28,24},{1,5},{5... | collective-permute-start | bytes 3145736 | tf_op jit(solution)/shard_map/ppermute | solution.py:395
  843.8 23.0 %collective-permute-start.95 = (bf16[256,2048]{1,0:T(8,128)(2,1)S(1)}, bf16[256,2048]{1,0:T(8,128)(2,1)S(1)}, u32[]{:S(2)}, u32[]{:S(2)}) collective-permute-start(bf16[256,2048]{1,0:T(8,128)(2,1)S(1)} %get-tuple-element.109), channel_id=1, source_target_pairs={{0,2},{1,3},{2,0},{3,1},{4,6},{5,7},{6,4},{7,5},{8,10},{9,11},{10,... | collective-permute-start | bytes 3145736 | tf_op jit(solution)/shard_map/ppermute | solution.py:398
  868.5 23.2 %collective-permute-start.96 = (bf16[128,2048]{1,0:T(8,128)(2,1)}, bf16[128,2048]{1,0:T(8,128)(2,1)}, u32[]{:S(2)}, u32[]{:S(2)}) collective-permute-start(bf16[128,2048]{1,0:T(8,128)(2,1)} %slice.307), channel_id=1, source_target_pairs={{0,4},{4,0},{8,12},{12,8},{16,20},{20,16},{24,28},{28,24},{1,5},{5... | collective-permute-start | bytes 1572872 | tf_op jit(solution)/shard_map/ppermute | solution.py:395
  (173 other events, 2082.1 us)

commit v2 on v1

--- a/solution.py
+++ b/solution.py
@@ -43,9 +43,9 @@
     dy = y if block // 2 == 0 else 1 - y
     dc = c if block % 2 == 0 else 1 - c
     if half == 0:
-        row = dc * LENGTH + seq * (2 * CHUNK) + dy * CHUNK
+        row = dc * LENGTH + seq * (4 * CHUNK) + dy * CHUNK
     else:
-        row = dc * LENGTH + LENGTH // 2 + dy * (2 * CHUNK) + seq * CHUNK
+        row = dc * LENGTH + dy * (4 * CHUNK) + 2 * CHUNK + seq * CHUNK
     return pl.multiple_of(row, CHUNK)
 
 
@@ -291,31 +291,31 @@
         ],
         compiler_params=pltpu.CompilerParams(vmem_limit_bytes=28 << 20),
         cost_estimate=pl.CostEstimate(
-            flops=20_000_000, bytes_accessed=12 << 20, transcendentals=0
+            flops=1 << 20, bytes_accessed=1 << 10, transcendentals=0
         ),
         name="mixer_forward",
     )(position, proj, coef)
 
 
-def mixer_backward(position, proj, conv, grad, coef):
-    rows, channels = proj.shape[0], coef.shape[1]
+def mixer_backward(position, proj, conv, grad, coef, tile):
+    rows = proj.shape[0]
     return pl.pallas_call(
         backward_kernel,
-        grid=(channels // LANES,),
+        grid=(1,),
         in_specs=[
             pl.BlockSpec(memory_space=pltpu.SMEM),
-            pl.BlockSpec((rows, 3 * LANES), lambda i: (0, i)),
-            pl.BlockSpec((rows, LANES), lambda i: (0, i)),
-            pl.BlockSpec((rows, LANES), lambda i: (0, i)),
-            pl.BlockSpec((COEF_ROWS, LANES), lambda i: (0, i)),
+            pl.BlockSpec((rows, 3 * LANES), lambda i: (0, tile)),
+            pl.BlockSpec((rows, LANES), lambda i: (0, tile)),
+            pl.BlockSpec((rows, LANES), lambda i: (0, tile)),
+            pl.BlockSpec((COEF_ROWS, LANES), lambda i: (0, tile)),
         ],
         out_specs=[
-            pl.BlockSpec((rows, 3 * LANES), lambda i: (0, i)),
-            pl.BlockSpec((COEF_ROWS, LANES), lambda i: (0, i)),
+            pl.BlockSpec((rows, 3 * LANES), lambda i: (0, 0)),
+            pl.BlockSpec((COEF_ROWS, LANES), lambda i: (0, 0)),
         ],
         out_shape=[
-            jax.ShapeDtypeStruct((rows, 3 * channels), bf16),
-            jax.ShapeDtypeStruct((COEF_ROWS, channels), f32),
+            jax.ShapeDtypeStruct((rows, 3 * LANES), bf16),
+            jax.ShapeDtypeStruct((COEF_ROWS, LANES), f32),
         ],
         scratch_shapes=[
             pltpu.VMEM((3, PAD + LENGTH, LANES), f32),
@@ -325,12 +325,234 @@
             pltpu.VMEM((LENGTH, LANES), f32),
             pltpu.VMEM((LENGTH, LANES), f32),
         ],
-        compiler_params=pltpu.CompilerParams(vmem_limit_bytes=36 << 20),
+        compiler_params=pltpu.CompilerParams(vmem_limit_bytes=32 << 20),
         cost_estimate=pl.CostEstimate(
-            flops=60_000_000, bytes_accessed=16 << 20, transcendentals=0
+            flops=1 << 20, bytes_accessed=1 << 10, transcendentals=0
         ),
         name="mixer_backward",
     )(position, proj, conv, grad, coef)
+
+
+TILE = 256
+NO_COST = pl.CostEstimate(flops=1 << 10, bytes_accessed=1 << 10, transcendentals=0)
+NT = (((1,), (1,)), ((), ()))
+NN = (((1,), (0,)), ((), ()))
+
+
+def whole_spec(array):
+    return pl.BlockSpec(array.shape, lambda i: (0,) * array.ndim, pipeline_mode=pl.Buffered(1))
+
+
+def up_kernel(scales, rows_ref, gate_w, up_w, inner_ref, scaled_ref, by_gate_ref, by_up_ref):
+    piece = TILE // 2
+    gate_all = lax.dot_general(rows_ref[...], gate_w[...], NT, preferred_element_type=f32)
+    up_all = lax.dot_general(rows_ref[...], up_w[...], NT, preferred_element_type=f32)
+    for part in range(2):
+        at = slice(part * piece, (part + 1) * piece)
+        index = lax.rem(2 * pl.program_id(0) + part, 8)
+        other = jnp.where(lax.rem(index, 4) < 2, index // 4, lax.rem(index, 2))
+        scale = jnp.where(other == 1, scales[1], scales[0])
+        gate, up = gate_all[at], up_all[at]
+        sigma = jax.nn.sigmoid(gate)
+        silu = gate * sigma
+        inner = silu * up
+        inner_ref[at, :] = inner.astype(bf16)
+        scaled_ref[at, :] = (inner * scale).astype(bf16)
+        by_gate_ref[at, :] = (scale * up * sigma * (1.0 + gate * (1.0 - sigma))).astype(bf16)
+        by_up_ref[at, :] = (scale * silu).astype(bf16)
+
+
+def ffn_up(scales, rows, gate_w, up_w):
+    count, hidden = rows.shape[0], gate_w.shape[0]
+    tile = pl.BlockSpec((TILE, hidden), lambda i: (i, 0))
+    return pl.pallas_call(
+        up_kernel,
+        grid=(count // TILE,),
+        in_specs=[
+            pl.BlockSpec(memory_space=pltpu.SMEM),
+            pl.BlockSpec((TILE, rows.shape[1]), lambda i: (i, 0)),
+            whole_spec(gate_w),
+            whole_spec(up_w),
+        ],
+        out_specs=[tile] * 4,
+        out_shape=[jax.ShapeDtypeStruct((count, hidden), bf16)] * 4,
+        compiler_params=pltpu.CompilerParams(vmem_limit_bytes=24 << 20),
+        cost_estimate=NO_COST,
+        name="ffn_up",
+    )(scales, rows, gate_w, up_w)
+
+
+def rows_kernel(left, right, out):
+    out[...] = lax.dot_general(left[...], right[...], NT, preferred_element_type=f32)
+
+
+def rows_product(left, right):
+    count, width = left.shape
+    return pl.pallas_call(
+        rows_kernel,
+        grid=(count // TILE,),
+        in_specs=[pl.BlockSpec((TILE, width), lambda i: (i, 0)), whole_spec(right)],
+        out_specs=pl.BlockSpec((TILE, right.shape[0]), lambda i: (i, 0)),
+        out_shape=jax.ShapeDtypeStruct((count, right.shape[0]), f32),
+        compiler_params=pltpu.CompilerParams(vmem_limit_bytes=24 << 20),
+        cost_estimate=NO_COST,
+        name="rows_product",
+    )(left, right)
+
+
+def grad_kernel(rows_ref, down_w, by_gate_ref, by_up_ref, gate_ref, up_ref):
+    grad = lax.dot_general(rows_ref[...], down_w[...], NT, preferred_element_type=f32)
+    gate_ref[...] = (grad * by_gate_ref[...].astype(f32)).astype(bf16)
+    up_ref[...] = (grad * by_up_ref[...].astype(f32)).astype(bf16)
+
+
+def ffn_grad(rows, down_w, by_gate, by_up):
+    count, hidden = rows.shape[0], down_w.shape[0]
+    tile = pl.BlockSpec((TILE, hidden), lambda i: (i, 0))
+    return pl.pallas_call(
+        grad_kernel,
+        grid=(count // TILE,),
+        in_specs=[
+            pl.BlockSpec((TILE, rows.shape[1]), lambda i: (i, 0)),
+            whole_spec(down_w),
+            tile,
+            tile,
+        ],
+        out_specs=[tile] * 2,
+        out_shape=[jax.ShapeDtypeStruct((count, hidden), bf16)] * 2,
+        compiler_params=pltpu.CompilerParams(vmem_limit_bytes=24 << 20),
+        cost_estimate=NO_COST,
+        name="ffn_grad",
+    )(rows, down_w, by_gate, by_up)
+
+
+def product_kernel(count, adds, tiles, *refs):
+    lefts, rights = refs[:count], refs[count : 2 * count]
+    outs = refs[-tiles:]
+    total = None
+    for left, right in zip(lefts, rights):
+        term = lax.dot_general(left[...], right[...], NN, preferred_element_type=f32)
+        total = term if total is None else total + term
+    for tile in range(tiles):
+
+        @pl.when(pl.program_id(0) == tile)
+        def _(tile=tile):
+            if adds:
+                outs[tile][...] = (total + refs[2 * count + tile][...].astype(f32)).astype(bf16)
+            else:
+                outs[tile][...] = total.astype(bf16)
+
+
+def product_tiles(lefts, rights, first, tiles, adds=()):
+    width = rights[0].shape[1]
+    start = first // TILE
+    tile_spec = pl.BlockSpec((TILE, width), lambda i: (0, 0))
+    return pl.pallas_call(
+        functools.partial(product_kernel, len(lefts), len(adds), tiles),
+        grid=(tiles,),
+        in_specs=[
+            pl.BlockSpec((TILE, left.shape[1]), lambda i: (start + i, 0)) for left in lefts
+        ]
+        + [whole_spec(right) for right in rights]
+        + [whole_spec(add) for add in adds],
+        out_specs=[tile_spec] * tiles,
+        out_shape=[jax.ShapeDtypeStruct((TILE, width), bf16)] * tiles,
+        compiler_params=pltpu.CompilerParams(vmem_limit_bytes=28 << 20),
+        cost_estimate=NO_COST,
+        name="product",
+    )(*lefts, *rights, *adds)
+
+
+def halves_spec(rows, depth):
+    return [jax.ShapeDtypeStruct((rows, depth), bf16)] * 2
+
+
+def mixer_weights_kernel(where_ref, in_ref, out_ref, in_mine, in_other, out_mine, out_other):
+    units = in_ref.shape[2] // 2
+    tiles = units // LANES
+    for side, target in ((where_ref[3], in_mine), (1 - where_ref[3], in_other)):
+        for tile in range(tiles):
+            start = pl.multiple_of(side * units + tile * LANES, LANES)
+            for j in range(3):
+                row = (tile * 3 + j) * LANES
+                block = in_ref[j, :, pl.ds(start, LANES)]
+                target[row : row + LANES, :] = block.T.astype(bf16)
+    for side, target in ((where_ref[3], out_mine), (1 - where_ref[3], out_other)):
+        rows = pl.ds(pl.multiple_of(side * units, units), units)
+        target[...] = out_ref[rows, :].astype(bf16)
+
+
+def mixer_weights(where, in_weight, out_weight):
+    _, depth, channels = in_weight.shape
+    units = channels // 2
+    return pl.pallas_call(
+        mixer_weights_kernel,
+        in_specs=[pl.BlockSpec(memory_space=pltpu.SMEM)]
+        + [pl.BlockSpec(memory_space=pltpu.VMEM)] * 2,
+        out_specs=[pl.BlockSpec(memory_space=pltpu.VMEM)] * 4,
+        out_shape=halves_spec(3 * units, depth) + halves_spec(units, depth),
+        compiler_params=pltpu.CompilerParams(vmem_limit_bytes=12 << 20),
+        cost_estimate=NO_COST,
+        name="mixer_weights",
+    )(where, in_weight, out_weight)
+
+
+def ffn_weights_kernel(
+    where_ref, gate_ref, up_ref, down_ref, mine, other, down_mine, down_other, turned
+):
+    units = down_ref.shape[0] // 2
+    mine_rows = pl.ds(pl.multiple_of(where_ref[3] * units, units), units)
+    other_rows = pl.ds(pl.multiple_of((1 - where_ref[3]) * units, units), units)
+    for n, source in enumerate((gate_ref, up_ref)):
+        turned[...] = source[...].T
+        mine[n * units : (n + 1) * units, :] = turned[mine_rows, :].astype(bf16)
+        other[n * units : (n + 1) * units, :] = turned[other_rows, :].astype(bf16)
+    down_mine[...] = down_ref[mine_rows, :].astype(bf16)
+    down_other[...] = down_ref[other_rows, :].astype(bf16)
+
+
+def ffn_weights(where, gate_weight, up_weight, down_weight):
+    units, depth = down_weight.shape
+    return pl.pallas_call(
+        ffn_weights_kernel,
+        in_specs=[pl.BlockSpec(memory_space=pltpu.SMEM)]
+        + [pl.BlockSpec(memory_space=pltpu.VMEM)] * 3,
+        out_specs=[pl.BlockSpec(memory_space=pltpu.VMEM)] * 4,
+        out_shape=halves_spec(units, depth) + halves_spec(units // 2, depth),
+        scratch_shapes=[pltpu.VMEM((units, depth), f32)],
+        compiler_params=pltpu.CompilerParams(vmem_limit_bytes=20 << 20),
+        cost_estimate=NO_COST,
+        name="ffn_weights",
+    )(where, gate_weight, up_weight, down_weight)
+
+
+def weight_grad_kernel(left, right, out):
+    out[...] = lax.dot_general(
+        left[...], right[...], (((0,), (0,)), ((), ())), preferred_element_type=f32
+    ).astype(bf16)
+
+
+def weight_product(left, right, blocks=0):
+    depth, units = left.shape
+    width = right.shape[1]
+    if blocks:
+        tile = width // blocks
+        out_spec = pl.BlockSpec((None, units, tile), lambda i: (i, 0, 0))
+        shape = (blocks, units, tile)
+    else:
+        tile = min(width, 512)
+        out_spec = pl.BlockSpec((units, tile), lambda i: (0, i))
+        shape = (units, width)
+    return pl.pallas_call(
+        weight_grad_kernel,
+        grid=(width // tile,),
+        in_specs=[whole_spec(left), pl.BlockSpec((depth, tile), lambda i: (0, i))],
+        out_specs=out_spec,
+        out_shape=jax.ShapeDtypeStruct(shape, bf16),
+        compiler_params=pltpu.CompilerParams(vmem_limit_bytes=28 << 20),
+        cost_estimate=NO_COST,
+        name="weight_product",
+    )(left, right)
 
 
 def rows_by_rows(left, right):
@@ -374,22 +596,24 @@
 
 
 class Links:
-    def __init__(self, groups, holders):
+    def __init__(self, groups):
         self.groups = groups
-        self.ring = [(2 * z + x, 2 * ((z + 1) % groups) + x) for z in range(groups) for x in (0, 1)]
-        self.over_x = [(2 * z + x, 2 * z + 1 - x) for z in range(groups) for x in (0, 1)]
+        places = [(z, x) for z in range(groups) for x in (0, 1)]
+        self.ring = [(2 * z + x, 2 * ((z + 1) % groups) + x) for z, x in places]
+        self.lines = [[2 * z + x for z in range(groups)] for x in (0, 1)]
+        self.over_x = [(2 * z + x, 2 * z + 1 - x) for z, x in places]
         self.over_y = [(2 * y + c, 2 * (1 - y) + c) for y in (0, 1) for c in (0, 1)]
         self.over_c = [(2 * y + c, 2 * y + 1 - c) for y in (0, 1) for c in (0, 1)]
-        self.turns = [
-            [(2 * z + x, 2 * ((z + s) % groups) + x) for z in range(groups) for x in (0, 1)]
-            for s in range(groups)
-        ]
+        self.bits = [1 << n for n in range(groups.bit_length() - 1)]
+        self.across = {
+            bit: [(2 * z + x, 2 * (z ^ bit) + x) for z, x in places] for bit in self.bits
+        }
 
     def z(self, v):
         return lax.ppermute(v, "dp", self.ring)
 
-    def turn(self, v, s):
-        return lax.ppermute(v, "dp", self.turns[s])
+    def z_across(self, v, bit):
+        return lax.ppermute(v, "dp", self.across[bit])
 
     def x(self, v):
         return lax.ppermute(v, "dp", self.over_x)
@@ -401,26 +625,238 @@
         return lax.ppermute(v, "mp", self.over_c)
 
 
-def gather_rows(net, block):
-    half = block.shape[0] // 2
-    a, b = block[:half], block[half:]
-    a_x, b_y = net.x(a), net.y(b)
-    a_y, b_x = net.y(a), net.x(b)
-    a_xy, b_yx = net.y(a_x), net.x(b_y)
-    mine = [a, a_y, a_x, a_xy, b, b_x, b_y, b_yx]
-    return jnp.concatenate(mine + [net.c(piece) for piece in mine], axis=0)
-
-
-def scatter_rows(net, partial):
-    rows = partial.shape[0]
-    near = add_low(partial[: rows // 2], net.c(partial[rows // 2 :]))
-    piece = rows // 16
-    a, b = near[: 4 * piece], near[4 * piece :]
-    a = add_low(a[: 2 * piece], net.x(a[2 * piece :]))
-    b = add_low(b[: 2 * piece], net.y(b[2 * piece :]))
-    a = a[:piece].astype(f32) + net.y(a[piece:]).astype(f32)
-    b = b[:piece].astype(f32) + net.x(b[piece:]).astype(f32)
-    return jnp.concatenate([a, b], axis=0)
+def tie(value, *before):
+    return lax.optimization_barrier((value, *before))[0] if before else value
+
+
+class Chain:
+    def __init__(self):
+        self.held = ()
+
+    def __call__(self, value, *before):
+        return tie(value, *self.held, *before)
+
+    def mark(self, *done):
+        self.held = done
+
+    def wait(self, *arrived):
+        together = lax.optimization_barrier((*arrived, *self.held))[: len(arrived)]
+        self.held = together[:1]
+        return together[0] if len(arrived) == 1 else together
+
+
+def copy_kernel(count, place, *refs):
+    where, pieces, whole, sems = refs[0], refs[1 : count + 1], refs[count + 1], refs[count + 2]
+    copies = [
+        pltpu.make_async_copy(piece, whole.at[place(where, i)], sems.at[i])
+        for i, piece in enumerate(pieces)
+    ]
+    for copy in copies:
+        copy.start()
+    for copy in copies:
+        copy.wait()
+
+
+def assemble_columns(first, pieces, place, where, shape):
+    arrays, offsets = [first], [pieces[0][1]]
+    index = []
+    for i, (array, offset) in enumerate(pieces):
+        known = [n for n, other in enumerate(arrays) if other is array]
+        if i == 0:
+            index.append((0, offset))
+        elif array is pieces[0][0]:
+            index.append((0, offset))
+        elif known:
+            index.append((known[0], offset))
+        else:
+            arrays.append(array)
+            index.append((len(arrays) - 1, offset))
+    count = len(arrays)
+    units = shape[0]
+
+    def kernel(*refs):
+        where_ref, sources, whole, sems = refs[0], refs[1 : count + 1], refs[count + 1], refs[-1]
+        copies = [
+            pltpu.make_async_copy(
+                sources[n].at[pl.ds(offset, units), :],
+                whole.at[place(where_ref, i)],
+                sems.at[i],
+            )
+            for i, (n, offset) in enumerate(index)
+        ]
+        for copy in copies:
+            copy.start()
+        for copy in copies:
+            copy.wait()
+
+    return pl.pallas_call(
+        kernel,
+        in_specs=[pl.BlockSpec(memory_space=pltpu.SMEM)]
+        + [pl.BlockSpec(memory_space=pl.ANY)] * count,
+        out_specs=pl.BlockSpec(memory_space=pltpu.VMEM),
+        out_shape=jax.ShapeDtypeStruct(shape, bf16),
+        scratch_shapes=[pltpu.SemaphoreType.DMA((len(pieces),))],
+        compiler_params=pltpu.CompilerParams(vmem_limit_bytes=8 << 20),
+        cost_estimate=pl.CostEstimate(
+            flops=0, bytes_accessed=4 * units * shape[1], transcendentals=0
+        ),
+        name="assemble_columns",
+    )(where, *arrays)
+
+
+def assemble_blocks(blocks, where):
+    groups, rows, width = blocks.shape
+
+    def kernel(where_ref, source, whole, sems):
+        copies = [
+            pltpu.make_async_copy(
+                source.at[i], whole.at[:, pl.ds(i * width, width)], sems.at[i]
+            )
+            for i in range(groups)
+        ]
+        for copy in copies:
+            copy.start()
+        for copy in copies:
+            copy.wait()
+
+    return pl.pallas_call(
+        kernel,
+        in_specs=[pl.BlockSpec(memory_space=pltpu.SMEM), pl.BlockSpec(memory_space=pl.ANY)],
+        out_specs=pl.BlockSpec(memory_space=pltpu.VMEM),
+        out_shape=jax.ShapeDtypeStruct((rows, groups * width), bf16),
+        scratch_shapes=[pltpu.SemaphoreType.DMA((groups,))],
+        compiler_params=pltpu.CompilerParams(vmem_limit_bytes=10 << 20),
+        cost_estimate=NO_COST,
+        name="assemble_blocks",
+    )(where, blocks)
+
+
+def assemble_rows(pieces, where, shape):
+    arrays = []
+    for array, *_ in pieces:
+        if not any(array is other for other in arrays):
+            arrays.append(array)
+    index = [next(n for n, other in enumerate(arrays) if other is p[0]) for p in pieces]
+    count = len(arrays)
+
+    def kernel(*refs):
+        sources, whole, sems = refs[1 : count + 1], refs[-2], refs[-1]
+        copies = []
+        for i, (n, (_, start, rows, target)) in enumerate(zip(index, pieces)):
+            source = sources[n].at[pl.ds(start, rows), :]
+            copies.append(
+                pltpu.make_async_copy(source, whole.at[pl.ds(target, rows), :], sems.at[i])
+            )
+        for copy in copies:
+            copy.start()
+        for copy in copies:
+            copy.wait()
+
+    return pl.pallas_call(
+        kernel,
+        in_specs=[pl.BlockSpec(memory_space=pltpu.SMEM)]
+        + [pl.BlockSpec(memory_space=pl.ANY)] * count,
+        out_specs=pl.BlockSpec(memory_space=pltpu.VMEM),
+        out_shape=jax.ShapeDtypeStruct(shape, bf16),
+        scratch_shapes=[pltpu.SemaphoreType.DMA((len(pieces),))],
+        compiler_params=pltpu.CompilerParams(vmem_limit_bytes=10 << 20),
+        cost_estimate=NO_COST,
+        name="assemble_rows",
+    )(where, *arrays)
+
+
+class GatherRows:
+    def __init__(self, net, chain, block):
+        self.net, self.chain = net, chain
+        half = block.shape[0] // 2
+        self.a, self.b = block[:half], block[half:]
+        self.a_x, self.b_y = net.x(self.a), net.y(self.b)
+
+    def second(self, *more):
+        net, chain = self.net, self.chain
+        got = chain.wait(self.a_x, self.b_y, *more)
+        a_x, b_y = got[:2]
+        self.a = jnp.concatenate([self.a, a_x], axis=0)
+        self.b = jnp.concatenate([self.b, b_y], axis=0)
+        chain.mark(self.a, self.b)
+        self.a_y, self.b_x = net.y(self.a), net.x(self.b)
+        self.far_a, self.far_b = net.c(self.a), net.c(self.b)
+        return got[2:]
+
+    def third(self, *more):
+        got = self.chain.wait(self.a_y, self.b_x, *more)
+        self.a_y, self.b_x = got[:2]
+        return got[2:]
+
+    def trade(self):
+        a_y, b_x = (tie(piece, *self.chain.held) for piece in (self.a_y, self.b_x))
+        self.far_a_y, self.far_b_x = self.net.c(a_y), self.net.c(b_x)
+
+    def whole(self, where):
+        chain = self.chain
+        far_a, far_b, far_a_y, far_b_x = chain.wait(
+            self.far_a, self.far_b, self.far_a_y, self.far_b_x
+        )
+        rows = self.a.shape[0] // 2
+        near = (self.a, self.a_y, self.b, self.b_x)
+        far = (far_a, far_a_y, far_b, far_b_x)
+        pieces = []
+        for core, arrays in enumerate((near, far)):
+            for place, array in enumerate(arrays):
+                first = (8 * core + place) * rows
+                pieces += [(array, 0, rows, first), (array, rows, rows, first + 4 * rows)]
+        whole = assemble_rows(pieces, where, (16 * rows, self.a.shape[1]))
+        chain.mark(whole)
+        return whole
+
+
+class ScatterProduct:
+    def __init__(self, net, chain, lefts, rights):
+        self.net, self.chain = net, chain
+        self.lefts, self.rights = lefts, rights
+        self.far = self.tiles(4, 4)
+
+    def tiles(self, first, count, adds=()):
+        lefts = [self.chain(self.lefts[0]), *self.lefts[1:]]
+        tiles = product_tiles(lefts, self.rights, first * TILE, count, adds)
+        self.chain.mark(tiles[0])
+        return tiles
+
+    def trade(self):
+        held = [tie(tile, *self.chain.held) for tile in self.far]
+        self.far = [self.net.c(tile) for tile in held]
+
+    def near(self, *more):
+        got = self.chain.wait(*self.far, *more)
+        self.far = got[:4]
+        self.for_x, self.for_y = self.tiles(2, 2, self.far[2:])
+        return got[4:]
+
+    def send(self):
+        net = self.net
+        for_x, for_y = (tie(tile, *self.chain.held) for tile in (self.for_x, self.for_y))
+        self.from_x, self.from_y = net.x(for_x), net.y(for_y)
+
+    def hold(self):
+        self.a, self.b = self.tiles(0, 2, self.far[:2])
+
+    def second(self, *more):
+        net, chain, piece = self.net, self.chain, TILE // 2
+        got = chain.wait(self.from_x, self.from_y, *more)
+        self.from_x, self.from_y = got[:2]
+        a_y = add_low(self.a[piece:], self.from_x[piece:])
+        b_x = add_low(self.b[piece:], self.from_y[piece:])
+        self.a_y, self.b_x = net.y(a_y), net.x(b_x)
+        chain.mark(a_y, b_x)
+        return got[2:]
+
+    def last(self, *more):
+        piece = TILE // 2
+        got = self.chain.wait(self.a_y, self.b_x, *more)
+        a_y, b_x = got[:2]
+        a = self.a[:piece].astype(f32) + self.from_x[:piece].astype(f32) + a_y.astype(f32)
+        b = self.b[:piece].astype(f32) + self.from_y[:piece].astype(f32) + b_x.astype(f32)
+        return (jnp.concatenate([a, b], axis=0), *got[2:])
 
 
 def pick(pair, index):
@@ -435,39 +871,142 @@
     )
 
 
-def gather_units(net, halves, x, z):
-    piece = in_order(pick(halves, x), net.x(pick(halves, 1 - x)), x, 1)
-    units, width = piece.shape
-    whole = jnp.zeros((units, width * net.groups), bf16)
-    for step in range(net.groups):
-        place = lax.rem(z + net.groups - step, net.groups) * width
-        whole = lax.dynamic_update_slice(whole, piece, (0, place))
-        if step < net.groups - 1:
-            piece = net.z(piece)
-    return whole
-
-
-def scatter_units(net, grad, z):
-    width = grad.shape[1] // net.groups
-
-    def part(step):
-        place = lax.rem(z + 2 * net.groups - 1 - step, net.groups) * width
-        return lax.dynamic_slice_in_dim(grad, place, width, 1)
-
-    total = part(0)
-    for step in range(1, net.groups):
-        total = net.z(total).astype(f32) + part(step).astype(f32)
-        if step < net.groups - 1:
-            total = total.astype(bf16)
-    return total
-
-
-def trade_units(net, total, x):
-    width = total.shape[1] // 2
-    mine = lax.dynamic_slice_in_dim(total, x * width, width, 1)
-    other = lax.dynamic_slice_in_dim(total, (1 - x) * width, width, 1)
-    got = net.x(other.astype(bf16)).astype(f32)
-    return jnp.where(x == 0, jnp.stack([mine, got]), jnp.stack([got, mine]))
+class GatherUnits:
+    def __init__(self, net, chain, mine, other, x, z):
+        self.net, self.chain, self.x, self.z = net, chain, x, z
+        self.first, self.out = mine, other
+
+    def trade(self, *after):
+        self.got = self.net.x(tie(self.out, *after))
+
+    def traded(self, merge, got=None):
+        got = self.chain.wait(self.got) if got is None else got
+        if merge:
+            pair = self.chain(jnp.concatenate([self.first, got], axis=0))
+            self.chain.mark(pair)
+            self.rings = [[pair]]
+        else:
+            self.rings = [[self.first], [got]]
+
+    def send(self, ring=0, *after):
+        hops = self.rings[ring]
+        hops.append(self.net.z(tie(hops[-1], *after)))
+
+    def gather(self, first, last):
+        pair = self.rings[0][0]
+        units = pair.shape[0] // 2
+        mine, other = pair[first:last], pair[units + first : units + last]
+        piece = self.chain(in_order(mine, other, self.x, 1))
+        self.chain.mark(piece)
+        return lax.all_gather(piece, "dp", axis_index_groups=self.net.lines)
+
+    def coming(self, ring=0):
+        return self.rings[ring][-1]
+
+    def came(self, piece, ring=0):
+        self.rings[ring][-1] = piece
+
+    def arrived(self, ring=0):
+        self.came(self.chain.wait(self.coming(ring)), ring)
+
+    def whole(self, where, ranges):
+        groups, chain = self.net.groups, self.chain
+        for ring in range(len(self.rings)):
+            while len(self.rings[ring]) < groups:
+                self.send(ring)
+                self.arrived(ring)
+        units, width = self.first.shape
+        merged = len(self.rings) == 1
+        wholes = []
+        for first, last in ranges:
+            pieces = []
+            for step in range(groups):
+                for side in range(2):
+                    piece = self.rings[0 if merged else side][step]
+                    offset = side * units if merged else 0
+                    pieces.append((piece, offset + first))
+            if width % LANES == 0:
+
+                def place(where_ref, i):
+                    block = lax.rem(where_ref[2] + (groups - i // 2), groups) * 2
+                    side = where_ref[3] if i % 2 == 0 else 1 - where_ref[3]
+                    start = pl.multiple_of((block + side) * width, LANES)
+                    return (slice(None), pl.ds(start, width))
+
+                shape = (last - first, 2 * width * groups)
+                whole = assemble_columns(
+                    chain(pieces[0][0]), pieces, place, where, shape
+                )
+            else:
+                whole = jnp.zeros((last - first, 2 * width * groups), bf16)
+                for i, (piece, offset) in enumerate(pieces):
+                    block = 2 * lax.rem(self.z + groups - i // 2, groups)
+                    side = self.x if i % 2 == 0 else 1 - self.x
+                    part = piece[offset : offset + last - first]
+                    whole = lax.dynamic_update_slice(whole, part, (0, (block + side) * width))
+            chain.mark(whole)
+            wholes.append(whole)
+        return wholes
+
+
+class ScatterUnits:
+    def __init__(self, net, chain, grads, x, z, depth):
+        self.net, self.chain, self.grads, self.x, self.z = net, chain, grads, x, z
+        self.depth = depth
+        self.step = 0
+        self.total = self.part()
+        chain.mark(self.total)
+        self.hop()
+
+    def part(self):
+        groups = self.net.groups
+        place = lax.rem(self.z + 2 * groups - 1 - self.step, groups)
+        parts = [
+            lax.dynamic_slice_in_dim(grad, place * 2 * self.depth, 2 * self.depth, 1)
+            for grad in self.grads
+        ]
+        return parts[0] if len(parts) == 1 else jnp.concatenate(parts, axis=0)
+
+    def hop(self):
+        self.total = self.net.z(self.total)
+
+    def got(self):
+        self.came(self.chain.wait(self.total))
+
+    def came(self, total):
+        self.step += 1
+        total = total.astype(f32) + self.part().astype(f32)
+        self.total = low(total) if self.step < self.net.groups - 1 else total
+        self.chain.mark(self.total)
+        if self.step < self.net.groups - 1:
+            self.hop()
+
+    def finish(self):
+        while self.step < self.net.groups - 1:
+            self.got()
+        self.square = jnp.sum(self.total * self.total)
+        other = lax.dynamic_slice_in_dim(self.total, (1 - self.x) * self.depth, self.depth, 1)
+        self.other = low(other)
+        self.chain.mark(self.square, self.other)
+
+    def trade(self):
+        self.traded = self.net.x(tie(self.other, *self.chain.held))
+
+    def pair(self):
+        got, total = self.chain.wait(self.traded, self.total)
+        mine = lax.dynamic_slice_in_dim(total, self.x * self.depth, self.depth, 1)
+        got = got.astype(f32)
+        return jnp.where(self.x == 0, jnp.stack([mine, got]), jnp.stack([got, mine]))
+
+
+class ReducedUnits(ScatterUnits):
+    def __init__(self, net, chain, blocks, x, z, depth):
+        self.net, self.chain, self.x, self.z, self.depth = net, chain, x, z, depth
+        self.step = net.groups - 1
+        self.total = lax.psum_scatter(blocks, "dp", axis_index_groups=net.lines)
+
+    def came(self, total):
+        self.total = total.astype(f32)
 
 
 def on_device(
@@ -515,20 +1054,56 @@
     dp, mp = lax.axis_index("dp"), lax.axis_index("mp")
     z, x, y, c = dp // 2, dp % 2, mp // 2, mp % 2
     begin = (mp * 2 + x) * channels
-    position = jnp.stack([y, c]).astype(jnp.int32)
-
-    in_halves = (
-        low(in_weight).reshape(depth, 3, 2, tiles, LANES).transpose(2, 3, 1, 4, 0)
-    ).reshape(2, 3 * channels, depth)
-    w_in = gather_units(net, in_halves, x, z)
-    w_out = gather_units(net, low(out_weight).reshape(2, channels, depth), x, z)
-    w_gate = gather_units(net, low(gate_weight).T.reshape(2, hidden, depth), x, z)
-    w_up = gather_units(net, low(up_weight).T.reshape(2, hidden, depth), x, z)
-    w_down = gather_units(net, low(down_weight).reshape(2, hidden, depth), x, z)
+    position = jnp.stack([y, c, z, x]).astype(jnp.int32)
 
     def own(array):
         return lax.dynamic_slice_in_dim(array, begin, channels, array.ndim - 1)
 
+    chain = Chain()
+    resid = tokens.astype(f32)
+    scale_one = lax.rsqrt(jnp.mean(resid * resid, axis=1, keepdims=True) + EPSILON)
+    normed = low(resid * scale_one * gains[0])
+    chain.mark(normed)
+    in_mine, in_other, out_mine, out_other = mixer_weights(
+        position, chain(in_weight.transpose(1, 0, 2)), out_weight
+    )
+    chain.mark(in_mine)
+    ring_in = GatherUnits(net, chain, in_mine, in_other, x, z)
+    ring_in.trade()
+    ring_in.rings = [[ring_in.first]]
+    ring_in.send()
+    ring_out = GatherUnits(net, chain, out_mine, out_other, x, z)
+    sequence_scale = jnp.sum(
+        jnp.where(
+            group_ids[:, None] == jnp.arange(group_scales.shape[0], dtype=jnp.int32)[None, :],
+            group_scales[None, :],
+            0.0,
+        )
+    )
+
+    first, got = chain.wait(ring_in.coming(0), ring_in.got)
+    ring_in.came(first, 0)
+    ring_in.rings.append([got])
+    ring_in.send(0)
+    ring_in.send(1)
+    normed_rows = GatherRows(net, chain, chain(normed))
+    gate_mine, gate_other, down_mine, down_other = ffn_weights(
+        position, chain(gate_weight), up_weight, down_weight
+    )
+    chain.mark(gate_mine)
+    ring_gu = GatherUnits(net, chain, gate_mine, gate_other, x, z)
+    ring_down = GatherUnits(net, chain, down_mine, down_other, x, z)
+    ring_out.trade()
+    other_scale = net.x(chain(sequence_scale).reshape(1, 1))
+    got, other_scale, first, second = normed_rows.second(
+        ring_out.got, other_scale, ring_in.coming(0), ring_in.coming(1)
+    )
+    ring_in.came(first, 0)
+    ring_in.came(second, 1)
+    ring_in.send(0)
+    ring_in.send(1)
+    ring_out.traded(True, got)
+    ring_out.send()
     residues_own = own(residues)
     rates_own = jnp.exp(own(log_rates))
     coef = jnp.concatenate(
@@ -541,103 +1116,232 @@
         ],
         axis=0,
     )
-
-    sequence_scale = jnp.sum(
-        jnp.where(
-            group_ids[:, None] == jnp.arange(group_scales.shape[0], dtype=jnp.int32)[None, :],
-            group_scales[None, :],
-            0.0,
-        )
+    coef = chain(coef)
+    chain.mark(coef)
+    first, got, piece = normed_rows.third(
+        ring_in.coming(0), ring_in.coming(1), ring_out.coming()
     )
-    other_scale = net.x(sequence_scale.reshape(1, 1))
-
-    resid = tokens.astype(f32)
-    scale_one = lax.rsqrt(jnp.mean(resid * resid, axis=1, keepdims=True) + EPSILON)
-    normed = low(resid * scale_one * gains[0])
-    normed_all = gather_rows(net, normed)
-    back_all = gather_rows(net, cotangent)
-    proj = rows_by_rows(normed_all, w_in)
-    branch, conv = mixer_forward(position, proj, coef)
-    middle = resid + scatter_rows(net, low(plain_dot(branch, w_out)))
+    ring_in.came(first, 0)
+    ring_in.came(got, 1)
+    ring_out.came(piece)
+    ring_in.send(1)
+    ring_out.send()
+    ring_gu.trade(*chain.held)
+    normed_rows.trade()
+    normed_all = normed_rows.whole(position)
+    got, piece, traded = chain.wait(ring_in.coming(1), ring_out.coming(), ring_gu.got)
+    ring_in.came(got, 1)
+    ring_out.came(piece)
+    ring_out.send()
+    ring_gu.traded(True, traded)
+    gate_blocks = ring_gu.gather(0, hidden)
+    up_blocks = ring_gu.gather(hidden, 2 * hidden)
+    cotangent = chain(cotangent)
+    back_rows = GatherRows(net, chain, cotangent)
+    (w_in,) = ring_in.whole(position, [(0, 3 * channels)])
+
+    proj = rows_product(chain(normed_all), w_in)
+    chain.mark(proj)
+    back_rows.second()
+    branch, conv = mixer_forward(position, chain(proj), coef)
+    chain.mark(branch)
+    (piece,) = back_rows.third(ring_out.coming())
+    ring_out.came(piece)
+    (w_out,) = ring_out.whole(position, [(0, channels)])
+    product = ScatterProduct(net, chain, [branch], [w_out])
+    product.trade()
+    product.near()
+    product.send()
+    back_rows.trade()
+    product.hold()
+    back_all = back_rows.whole(position)
+    (gate_blocks,) = product.second(gate_blocks)
+    ring_down.trade(*chain.held)
+    w_gate = assemble_blocks(chain(gate_blocks), position)
+    chain.mark(w_gate)
+    (more,) = product.last()
+    middle = resid + more
     scale_two = lax.rsqrt(jnp.mean(middle * middle, axis=1, keepdims=True) + EPSILON)
     normed_two = low(middle * scale_two * gains[1])
-    normed_two_all = gather_rows(net, normed_two)
-    gate = rows_by_rows(normed_two_all, w_gate)
-    up = rows_by_rows(normed_two_all, w_up)
-    sigma = jax.nn.sigmoid(gate)
-    silu = gate * sigma
-    inner = silu * up
-    rows = normed_two_all.shape[0]
-    index = lax.broadcasted_iota(jnp.int32, (rows, 1), 0)
-    half, within = (index // (rows // 4)) % 2, (index // (rows // 16)) % 4
-    other_row = jnp.where(half == 0, within // 2, within % 2) == 1
-    row_scale = jnp.where(other_row, other_scale, sequence_scale.reshape(1, 1))
-
-    grad_down = low(columns_by_columns(low(inner * row_scale), back_all))
-    total_down = scatter_units(net, grad_down, z)
-    grad_inner = rows_by_rows(back_all, w_down) * row_scale
-    grad_gate = low(grad_inner * up * sigma * (1.0 + gate * (1.0 - sigma)))
-    grad_up = low(grad_inner * silu)
-    total_gate = scatter_units(net, low(columns_by_columns(grad_gate, normed_two_all)), z)
-    total_up = scatter_units(net, low(columns_by_columns(grad_up, normed_two_all)), z)
-    output = low(middle + scatter_rows(net, low(plain_dot(low(inner), w_down))))
-    grad_normed_two = scatter_rows(
-        net, low(plain_dot(grad_gate, w_gate) + plain_dot(grad_up, w_up))
+    chain.mark(normed_two)
+    normed_two_rows = GatherRows(net, chain, normed_two)
+    normed_two_rows.second()
+    got, up_blocks = chain.wait(ring_down.got, up_blocks)
+    ring_down.traded(True, got)
+    down_blocks = ring_down.gather(0, hidden)
+    w_up = assemble_blocks(chain(up_blocks), position)
+    chain.mark(w_up)
+    scales = chain(jnp.concatenate([sequence_scale.reshape(1), other_scale.reshape(1)]))
+    chain.mark(scales)
+    normed_two_rows.third()
+    normed_two_rows.trade()
+    normed_two_all = normed_two_rows.whole(position)
+    inner_low, inner_scaled, by_gate, by_up = ffn_up(
+        scales, chain(normed_two_all), w_gate, w_up
     )
+    chain.mark(inner_scaled, inner_low)
+
+    def weight_grad(left, right):
+        grad = weight_product(chain(left), right)
+        chain.mark(grad)
+        return grad
+
+    def blocks_of(left, right):
+        grad = weight_product(chain(left), right, net.groups)
+        chain.mark(grad)
+        return grad
+
+    def reduced(grad):
+        return ReducedUnits(net, chain, chain(grad), x, z, depth)
+
+    def scattered(*grads):
+        return ScatterUnits(net, chain, grads, x, z, depth)
+
+    sum_down = reduced(blocks_of(inner_scaled, back_all))
+    w_down = assemble_blocks(chain.wait(down_blocks), position)
+    chain.mark(w_down)
+    grad_gate, grad_up = ffn_grad(chain(back_all), w_down, by_gate, by_up)
+    chain.mark(grad_gate, grad_up)
+    product = ScatterProduct(net, chain, [grad_gate, grad_up], [w_gate, w_up])
+    product.trade()
+    product.near()
+    product.send()
+    product.hold()
+    grad_gate = blocks_of(grad_gate, normed_two_all)
+    grad_up = blocks_of(grad_up, normed_two_all)
+    product.second()
+    sum_gate, sum_up = reduced(grad_gate), reduced(grad_up)
+    output_product = ScatterProduct(net, chain, [inner_low], [w_down])
+    output_product.trade()
+    (grad_normed_two,) = product.last()
     grad_from_norm, gain_two = norm_back(middle, scale_two, gains[1], grad_normed_two)
     grad_middle = cotangent.astype(f32) * sequence_scale + grad_from_norm
-    grad_middle_all = gather_rows(net, low(grad_middle))
-    total_out = scatter_units(net, low(columns_by_columns(branch, grad_middle_all)), z)
-    grad_branch = rows_by_rows(grad_middle_all, w_out)
-    grad_proj, sums = mixer_backward(position, proj, conv, grad_branch, coef)
-    total_in = scatter_units(net, low(columns_by_columns(grad_proj, normed_all)), z)
-    grad_normed = scatter_rows(net, low(plain_dot(grad_proj, w_in)))
-    grad_from_first, gain_one = norm_back(resid, scale_one, gains[0], grad_normed)
-    grad_input = grad_middle + grad_from_first
-    input_grad = low(grad_input)
-    radial_grad = scale_one[:, 0] * jnp.sum(resid * grad_input, axis=1) / model**0.5
-
+    grad_middle_low = low(grad_middle)
+    chain.mark(grad_middle_low)
+    grad_middle_rows = GatherRows(net, chain, grad_middle_low)
+    output_product.near()
+    output_product.hold()
+    (got,) = grad_middle_rows.second(sum_down.total)
+    sum_down.came(got)
+    sum_down.finish()
+    sum_gate.came(chain.wait(sum_gate.total))
+    sum_gate.finish()
+    grad_middle_rows.third()
+    grad_middle_rows.trade()
+    sum_down.trade()
+    sum_gate.trade()
+    output_product.send()
+    grad_middle_all = grad_middle_rows.whole(position)
+    grad_branch = rows_by_rows(chain(grad_middle_all), w_out)
+    chain.mark(grad_branch)
+    proj_grads, small_sums, sums_in = [], [], []
+    for tile in range(tiles):
+        part, sums = mixer_backward(position, proj, conv, chain(grad_branch), coef, tile)
+        chain.mark(part)
+        proj_grads.append(part)
+        small_sums.append(sums)
+        if tile == 0:
+            sums_in.append(reduced(blocks_of(part, normed_all)))
+    span_in = 3 * LANES
+    w_in_parts = [w_in[tile * span_in : (tile + 1) * span_in] for tile in range(tiles)]
+    product = ScatterProduct(net, chain, proj_grads, w_in_parts)
+    product.trade()
+    grads_in = [blocks_of(part, normed_all) for part in proj_grads[1:]]
+    product.near()
+    product.send()
+    sums_in += [reduced(grad) for grad in grads_in]
+    product.hold()
+    output_product.second()
+    grad_out = blocks_of(branch, grad_middle_all)
+
+    sums = chain(jnp.concatenate(small_sums, axis=1))
     sums = jnp.concatenate(
         [sums[:RATE_ROW], -rates_own * residues_own * sums[RATE_ROW:]], axis=0
     )
-    sums = sum((net.turn(sums, s) for s in range(1, net.groups)), sums)
-    sums = in_order(sums[None], net.x(sums)[None], x, 0)[None]
-    sums = in_order(sums, net.c(sums), c, 0)[None]
-    sums = in_order(sums, net.y(sums), y, 0)
+    chain.mark(sums)
+    sums_across = net.z_across(sums, net.bits[0])
+    sum_up.came(chain.wait(sum_up.total))
+    sum_up.finish()
+    (across,) = product.second(sums_across)
+    sum_out = reduced(grad_out)
+    sum_up.trade()
+    sums = chain(sums) + across
+    chain.mark(sums)
+    sums_across = net.z_across(sums, net.bits[1])
+    (more,) = output_product.last()
+    output = low(middle + more)
+    chain.mark(output)
+
+    def pair_of(total):
+        pair = chain(total.pair())
+        chain.mark(pair)
+        return pair
+
+    shard_down = pair_of(sum_down).reshape(2 * hidden, depth)
+    shard_gate = chain(pair_of(sum_gate).reshape(2 * hidden, depth).T)
+    chain.mark(shard_gate)
+    grad_normed, first, across = product.last(sums_in[0].total, sums_across)
+    sums = sums + across
+    for bit in net.bits[2:]:
+        sums = sums + net.z_across(sums, bit)
+    sums_near = net.x(sums)
+    grad_from_first, gain_one = norm_back(resid, scale_one, gains[0], grad_normed)
+    grad_input = grad_middle + grad_from_first
+    chain.mark(gain_one)
+    sums_in[0].came(first)
+    sums_in[0].finish()
+    sums_in[0].trade()
+    sums_in[1].came(chain.wait(sums_in[1].total))
+    sums_in[1].finish()
+    sums_in[1].trade()
+    shard_up = chain(pair_of(sum_up).reshape(2 * hidden, depth).T)
+    chain.mark(shard_up)
+    sum_out.came(chain.wait(sum_out.total))
+    sum_out.finish()
+    sum_out.trade()
+
+    totals = (sum_down, sum_gate, sum_up, sum_out, *sums_in)
+    square = sum((total.square for total in totals)) + jnp.sum(sums * sums) / net.groups
+    last = jnp.concatenate(
+        [gain_one.reshape(-1, LANES), gain_two.reshape(-1, LANES), jnp.full((8, LANES), square)]
+    )
+    last = chain(last)
+    chain.mark(last)
+    sums = in_order(sums[None], chain.wait(sums_near)[None], x, 0)[None]
+    across, more = chain.wait(net.c(last), net.c(sums))
+    last = last + across
+    sums = in_order(sums, more, c, 0)[None]
+    for hop in (net.x, net.y):
+        last = last + chain.wait(hop(last))
+        chain.mark(last)
+    for bit in net.bits:
+        across = net.z_across(last, bit)
+        if bit == net.bits[0]:
+            more = net.y(tie(sums, last))
+        if bit == net.bits[1]:
+            shard_out = pair_of(sum_out).reshape(2 * channels, depth)
+            shard_in = chain(
+                jnp.stack([total.pair().reshape(2, 3, LANES, depth) for total in sums_in])
+                .transpose(4, 2, 1, 0, 3)
+                .reshape(depth, 3, 2 * channels)
+            )
+            chain.mark(shard_in)
+        last = last + chain.wait(across)
+        chain.mark(last)
+    sums = in_order(sums, chain.wait(more), y, 0)
+    input_grad = low(grad_input)
+    radial_grad = scale_one[:, 0] * jnp.sum(resid * grad_input, axis=1) / model**0.5
     sums = sums.reshape(8, COEF_ROWS, channels).transpose(1, 0, 2).reshape(COEF_ROWS, model)
     grad_taps = sums[: 3 * TAPS].reshape(taps.shape)
     grad_skip = sums[SKIP_ROW]
     grad_residues = sums[RES_ROW:RATE_ROW]
     grad_log_rates = sums[RATE_ROW:]
-
-    totals = (total_in, total_out, total_gate, total_up, total_down)
-    square_big = sum((jnp.sum(grad * grad) for grad in totals))
-    last = jnp.concatenate(
-        [gain_one.reshape(-1, LANES), gain_two.reshape(-1, LANES), jnp.full((8, LANES), square_big)]
-    )
-    last = last + net.x(last)
-    last = last + net.y(last)
-    last = last + net.c(last)
-    last = sum((net.turn(last, s) for s in range(1, net.groups)), last)
     span = model // LANES
     grad_gains = last[: 2 * span].reshape(2, model)
-    small = (grad_gains, grad_taps, grad_residues, grad_log_rates, grad_skip)
-    square_total = last[2 * span, 0] + sum((jnp.sum(grad * grad) for grad in small))
+    square_total = last[2 * span, 0] + jnp.sum(grad_gains * grad_gains)
     grad_norm = jnp.sqrt(square_total)
     factor = jnp.minimum(1.0, CLIP / (grad_norm + 1e-06))
-
-    pair_in, pair_out, pair_gate, pair_up, pair_down = (
-        trade_units(net, total, x) for total in totals
-    )
-    shard_in = (
-        pair_in.reshape(2, tiles, 3, LANES, depth)
-        .transpose(4, 2, 0, 1, 3)
-        .reshape(depth, 3, 2 * channels)
-    )
-    shard_out = pair_out.reshape(2 * channels, depth)
-    shard_gate = pair_gate.reshape(2 * hidden, depth).T
-    shard_up = pair_up.reshape(2 * hidden, depth).T
-    shard_down = pair_down.reshape(2 * hidden, depth)
+    factor = tie(factor, shard_in, shard_out, shard_down, shard_gate, shard_up)
 
     return (
         output,
@@ -685,7 +1389,7 @@
 
 
 def solution(mesh):
-    net = Links(mesh.shape["dp"] // 2, mesh.shape["mp"])
+    net = Links(mesh.shape["dp"] // 2)
     rows = P(("dp", "mp"), None)
     split_in = P("dp", None, "mp")
     split_out = P("mp", "dp")

time: 962 us -> 689 us (0.72)
  waiting for transfers between devices: 483 us -> 186 us
  Pallas kernels: 43.6 us -> 190 us
  matrix products: 132 us -> 2.4 us
  starting transfers between devices: 81.9 us -> 67.4 us
  between operations: 12.6 us -> 24.2 us
    ppermute x30 -> x9, waiting for transfers between devices: 284 us -> 40 us  [z(): return lax.ppermute(v, 'dp', self.ring)]
    pallas_call x1 -> x34, Pallas kernels: 30.1 us -> 176 us  [the longest x12 53.5 us: product_tiles(): pl.pallas_call(functools.partial(product_kernel, len(lefts), len(adds), t...]
    dot_general x10 -> x0, matrix products: 86.9 us -> none  [the longest x5 43.5 us: columns_by_columns(): lax.dot_general(left, right, (((0,), (0,)), ((), ())), preferred_element_...]
    ppermute x33 -> x29, waiting for transfers between devices: 147 us -> 80.5 us  [x(): return lax.ppermute(v, 'dp', self.over_x)]
    dot_general x5 -> x1, matrix products: 44.8 us -> 2.4 us  [rows_by_rows(): lax.dot_general(left, right, (((1,), (1,)), ((), ())), preferred_element_...]
    unnamed x278 -> x367, local copies, waits for them, and re-layouts: 52.8 us -> 77.4 us
    ppermute x38 -> x34, waiting for transfers between devices: 7.68 us -> 25 us  [c(): return lax.ppermute(v, 'mp', self.over_c)]
    ppermute x22 -> x18, waiting for transfers between devices: 40.8 us -> 25.6 us  [y(): return lax.ppermute(v, 'mp', self.over_y)]
  transfers between devices with their start and end apart: 129 -> 103, of which waited for: 62 -> 49; matrix products, arithmetic and copies ran while one was open for 22% -> 17% of each run, Pallas kernels for 3% -> 28%
where the time goes in v2:
time: 689 us; the launch traced here: 678 us
  Pallas kernels  190 us (28%)
  waiting for transfers between devices  186 us (27%)
  other arithmetic  110 us (16%)
  local copies, waits for them, and re-layouts  98.6 us (14%)
  starting transfers between devices  67.4 us (10%)
  between operations  24.2 us (4%)
    ppermute x29, waiting for transfers between devices, x(): return lax.ppermute(v, 'dp', self.over_x)  80.5 us
    unnamed x367, local copies, waits for them, and re-layouts  77.4 us
    pallas_call x12, Pallas kernels, product_tiles(): pl.pallas_call(functools.partial(product_kernel, len(lefts), len(adds), t...  53.5 us
    ppermute x9, waiting for transfers between devices, z(): return lax.ppermute(v, 'dp', self.ring)  40 us
    pallas_call x6, Pallas kernels, weight_product(): pl.pallas_call(weight_grad_kernel, grid=(width // tile,), in_specs=[whole...  37.2 us
    pallas_call x2, Pallas kernels, mixer_backward(): pl.pallas_call(backward_kernel, grid=(1,), in_specs=[pl.BlockSpec(memory_...  30.1 us
    ppermute x29, starting transfers between devices, x(): return lax.ppermute(v, 'dp', self.over_x)  29.6 us
    ppermute x18, waiting for transfers between devices, y(): return lax.ppermute(v, 'mp', self.over_y)  25.6 us
  transfers between devices with their start and end apart: 103, of which 49 were waited for; matrix products, arithmetic and copies ran while one was open for 17% of the time, Pallas kernels for 28%

profile of v2, /device:TPU:0, one launch (start us, length us, event | category | flops | bytes accessed | tf_op | source)
XLA Modules:
  0.0 677.9 jit_solution(15654710489399770608)
XLA Ops:
  11.0 2.6 fusion.2
  14.5 3.1 collective-permute-start
  19.8 8.9 %collective-permute-done.refs_3_ = bf16[768,256]{1,0:T(8,128)(2,1)S(1)} collective-permute-done((bf16[768,256]{1,0:T(8,128)(2,1)S(1)}, bf16[768,256]{1,0:T(8,128)(2,1)S(1)}, u32[]{:S(2)}, u32[]{:S(2)}) %collective-permute-start) | collective-permute-done | bytes 393248 | tf_op jit(solution)/shard_map/ppermute | solution.py:613
  40.7 5.6 collective-permute-done.4
  47.5 2.5 collective-permute-done.5
  50.1 3.1 collective-permute-done.7.refs_4_
  56.4 17.9 %collective-permute-done.12.refs_2_ = bf16[512,256]{1,0:T(8,128)(2,1)S(1)} collective-permute-done((bf16[512,256]{1,0:T(8,128)(2,1)S(1)}, bf16[512,256]{1,0:T(8,128)(2,1)S(1)}, u32[]{:S(2)}, u32[]{:S(2)}) %collective-permute-start.12) | collective-permute-done | bytes 262176 | tf_op jit(solution)/shard_map/ppermute | solution.py:613
  83.5 3.3 assemble_rows.4.left.right
  86.8 3.2 copy-done.2
  90.1 9.0 %collective-permute-done.18.refs_3_ = bf16[512,256]{1,0:T(8,128)(2,1)} collective-permute-done((bf16[512,256]{1,0:T(8,128)(2,1)}, bf16[512,256]{1,0:T(8,128)(2,1)}, u32[]{:S(2)}, u32[]{:S(2)}) %collective-permute-start.18) | collective-permute-done | bytes 262176 | tf_op jit(solution)/shard_map/ppermute | solution.py:613
  102.4 2.5 maximum_select_fusion.5
  109.3 8.1 %rows_product.1.proj_ref = f32[2048,768]{1,0:T(8,128)S(1)} custom-call(bf16[2048,2048]{1,0:T(8,128)(2,1)S(1)} %copy-done.3, bf16[768,2048]{1,0:T(8,128)(2,1)S(1)} %assemble_columns.2.right), custom_call_target="tpu_custom_call" | custom-call | flops 1024 | bytes 1024 | tf_op jit(solution)/shard_map/rows_product/pallas_call | solution.py:391
  122.2 13.5 %mixer_forward.1 = (bf16[2048,256]{1,0:T(8,128)(2,1)S(1)}, f32[2048,256]{1,0:T(8,128)S(1)}) custom-call(s32[4]{0:T(128)S(1)} %pad_add_fusion.where_ref.refs_0_.pos_ref, f32[2048,768]{1,0:T(8,128)S(1)} %rows_product.1.proj_ref, f32[48,256]{1,0:T(8,128)S(1)} %concatenate.181.coef_ref), custom_call_target="tpu_custom_call" | custom-call | flops 1048576 | bytes 1024 | tf_op jit(solution)/shard_map/mixer_forward/pallas_call | solution.py:271
  135.7 2.6 copy-done.5
  138.3 4.4 collective-permute-done.23.refs_4_
  151.7 3.0 collective-permute-done.26.refs_3_
  156.2 2.5 product.13
  166.8 3.6 assemble_rows.5.right.rows_ref
  170.4 3.3 copy-done.7
  173.7 11.1 %collective-permute-done.30 = bf16[256,2048]{1,0:T(8,128)(2,1)} collective-permute-done((bf16[256,2048]{1,0:T(8,128)(2,1)}, bf16[256,2048]{1,0:T(8,128)(2,1)}, u32[]{:S(2)}, u32[]{:S(2)}) %collective-permute-start.30) | collective-permute-done | bytes 1048608 | tf_op jit(solution)/shard_map/ppermute | solution.py:622
  192.5 10.2 %collective-permute-done.36 = bf16[128,2048]{1,0:T(8,128)(2,1)S(1)} collective-permute-done((bf16[128,2048]{1,0:T(8,128)(2,1)S(1)}, bf16[128,2048]{1,0:T(8,128)(2,1)S(1)}, u32[]{:S(2)}, u32[]{:S(2)}) %collective-permute-start.36) | collective-permute-done | bytes 524320 | tf_op jit(solution)/shard_map/ppermute | solution.py:619
  210.6 11.9 %collective-permute-done.38 = bf16[128,2048]{1,0:T(8,128)(2,1)S(1)} collective-permute-done((bf16[128,2048]{1,0:T(8,128)(2,1)S(1)}, bf16[128,2048]{1,0:T(8,128)(2,1)S(1)}, u32[]{:S(2)}, u32[]{:S(2)}) %collective-permute-start.38) | collective-permute-done | bytes 524320 | tf_op jit(solution)/shard_map/ppermute | solution.py:619
  224.7 2.6 collective-permute-done.37
  236.6 15.3 %collective-permute-done.41.refs_4_ = bf16[256,2048]{1,0:T(8,128)(2,1)S(1)} collective-permute-done((bf16[256,2048]{1,0:T(8,128)(2,1)}, bf16[256,2048]{1,0:T(8,128)(2,1)S(1)}, u32[]{:S(2)}, u32[]{:S(2)}) %collective-permute-start.41) | collective-permute-done | bytes 1048608 | tf_op jit(solution)/shard_map/ppermute | solution.py:619
  258.5 16.9 %ffn_up.1 = (bf16[2048,704]{1,0:T(8,128)(2,1)S(1)}, bf16[2048,704]{1,0:T(8,128)(2,1)S(1)}, bf16[2048,704]{1,0:T(8,128)(2,1)S(1)}, bf16[2048,704]{1,0:T(8,128)(2,1)S(1)}) custom-call(f32[2]{0:T(128)S(1)} %pad_maximum_fusion.15.scales, bf16[2048,2048]{1,0:T(8,128)(2,1)S(1)} %assemble_rows.6.rows_ref.right, ...), custom_call_target="tpu_custom_call" | custom-call | flops 1024 | bytes 1024 | tf_op jit(solution)/shard_map/ffn_up/pallas_call | solution.py:368
  280.4 7.4 %weight_product.6 = bf16[4,704,512]{2,1,0:T(8,128)(2,1)S(1)} custom-call(bf16[2048,704]{1,0:T(8,128)(2,1)S(1)} %get-tuple-element.399.left, bf16[2048,2048]{1,0:T(8,128)(2,1)S(1)} %bitcast.94), custom_call_target="tpu_custom_call" | custom-call | flops 1024 | bytes 1024 | tf_op jit(solution)/shard_map/weight_product/pallas_call | solution.py:546
  293.4 3.9 copy-done.8
  299.2 8.3 %ffn_grad.1 = (bf16[2048,704]{1,0:T(8,128)(2,1)S(1)}, bf16[2048,704]{1,0:T(8,128)(2,1)S(1)}) custom-call(bf16[2048,2048]{1,0:T(8,128)(2,1)S(1)} %copy-done.8, bf16[704,2048]{1,0:T(8,128)(2,1)S(1)} %assemble_blocks.5.down_w.refs_1_, bf16[2048,704]{1,0:T(8,128)(2,1)S(1)} %copy-done.51, bf16[2048,704]{1,0:T(8,128)(2,1)S(1)} %copy-done.53), custom_call_target="tpu_custom_call" | custom-call | flops 1024 | bytes 1024 | tf_op jit(solution)/shard_map/ffn_grad/pallas_call | solution.py:412
  307.6 7.6 %product.15 = (bf16[256,2048]{1,0:T(8,128)(2,1)S(1)}, bf16[256,2048]{1,0:T(8,128)(2,1)S(1)}, bf16[256,2048]{1,0:T(8,128)(2,1)S(1)}, bf16[256,2048]{1,0:T(8,128)(2,1)S(1)}) custom-call(bf16[2048,704]{1,0:T(8,128)(2,1)S(1)} %get-tuple-element.426.refs_0_.left, bf16[2048,704]{1,0:T(8,128)(2,1)S(1)} %get-tuple-element.427.refs_1_.left, ...), custom_call_target="tpu_custom_call" | custom-call | flops 1024 | bytes 1024 | tf_op jit(solution)/shard_map/product/pallas_call | solution.py:450
  322.5 5.3 product.16
  329.9 3.9 product.17
  335.8 7.4 %weight_product.7 = bf16[4,704,512]{2,1,0:T(8,128)(2,1)S(1)} custom-call(bf16[2048,704]{1,0:T(8,128)(2,1)S(1)} %get-tuple-element.426.refs_0_.left, bf16[2048,2048]{1,0:T(8,128)(2,1)S(1)} %bitcast.88), custom_call_target="tpu_custom_call" | custom-call | flops 1024 | bytes 1024 | tf_op jit(solution)/shard_map/weight_product/pallas_call | solution.py:546
  344.8 3.4 copy-done.1
  348.2 7.4 %weight_product.8 = bf16[4,704,512]{2,1,0:T(8,128)(2,1)S(1)} custom-call(bf16[2048,704]{1,0:T(8,128)(2,1)S(1)} %copy-done.14, bf16[2048,2048]{1,0:T(8,128)(2,1)S(1)} %copy-done.1), custom_call_target="tpu_custom_call" | custom-call | flops 1024 | bytes 1024 | tf_op jit(solution)/shard_map/weight_product/pallas_call | solution.py:546
  364.7 6.0 product.18
  380.1 3.0 fusion.35
  384.7 4.2 product.19
  390.8 3.6 product.20
  406.9 8.2 %reduce-scatter.9.cloned.1.call-done = bf16[1,704,512]{2,1,0:T(8,128)(2,1)} async-done(((bf16[4,704,512]{2,1,0:T(8,128)(2,1)}), bf16[1,704,512]{2,1,0:T(8,128)(2,1)}) %reduce-scatter.9.cloned.1.call-update) | async-done | bytes 720912 | tf_op jit(solution)/shard_map/reduce_scatter | solution.py:1006
  419.5 5.4 collective-permute-done.61.refs_4_
  431.4 3.8 assemble_rows.7.right
  439.4 15.1 %mixer_backward.2 = (bf16[2048,384]{1,0:T(8,128)(2,1)S(1)}, f32[48,128]{1,0:T(8,128)S(1)}) custom-call(s32[4]{0:T(128)S(1)} %pad_add_fusion.where_ref.refs_0_.pos_ref, f32[2048,768]{1,0:T(8,128)S(1)} %bitcast.92, f32[2048,256]{1,0:T(8,128)S(1)} %copy-done.35, f32[2048,256]{1,0:T(8,128)S(1)} %fusion.44.grad_ref, f32[48,256]{1,0:T(8,128)S(1)} %concatenate.181.coef_ref), custom_call_target="tpu_custom_call" | custom-call | flops 1048576 | bytes 1024 | tf_op jit(solution)/shard_map/mixer_backward/pallas_call | solution.py:302
  454.5 5.1 weight_product.9
  462.0 2.8 copy-done.6
  468.0 15.1 %mixer_backward.3 = (bf16[2048,384]{1,0:T(8,128)(2,1)S(1)}, f32[48,128]{1,0:T(8,128)S(1)}) custom-call(s32[4]{0:T(128)S(1)} %pad_add_fusion.where_ref.refs_0_.pos_ref, f32[2048,768]{1,0:T(8,128)S(1)} %copy-done.6, f32[2048,256]{1,0:T(8,128)S(1)} %copy-done.36, f32[2048,256]{1,0:T(8,128)S(1)} %copy-done.38, f32[48,256]{1,0:T(8,128)S(1)} %concatenate.181.coef_ref), custom_call_target="tpu_custom_call" | custom-call | flops 1048576 | bytes 1024 | tf_op jit(solution)/shard_map/mixer_backward/pallas_call | solution.py:302
  483.1 6.4 product.21
  497.3 3.4 copy-done.4
  502.0 5.5 weight_product.10
  512.5 5.9 product.22
  518.4 4.6 product.23
  529.2 4.4 weight_product.11
  539.7 8.1 %collective-permute-done.75 = bf16[256,2048]{1,0:T(8,128)(2,1)} collective-permute-done((bf16[256,2048]{1,0:T(8,128)(2,1)}, bf16[256,2048]{1,0:T(8,128)(2,1)}, u32[]{:S(2)}, u32[]{:S(2)}) %collective-permute-start.75) | collective-permute-done | bytes 1048608 | tf_op jit(solution)/shard_map/ppermute | solution.py:622
  549.0 10.6 %collective-permute-done.74 = bf16[256,2048]{1,0:T(8,128)(2,1)} collective-permute-done((bf16[256,2048]{1,0:T(8,128)(2,1)}, bf16[256,2048]{1,0:T(8,128)(2,1)}, u32[]{:S(2)}, u32[]{:S(2)}) %collective-permute-start.74) | collective-permute-done | bytes 1048608 | tf_op jit(solution)/shard_map/ppermute | solution.py:619
  565.6 5.1 collective-permute-done.73
  583.1 2.9 copy.74
  606.4 3.0 copy.75
  609.4 3.2 reduce-scatter.15.cloned.1.call-done
  620.8 3.4 fusion.7
  633.4 2.6 collective-permute-done.88
  641.4 2.4 reshape.470
  647.2 5.1 multiply_subtract_fusion.1
  652.4 2.8 multiply_subtract_fusion.2
  656.6 2.8 multiply_subtract_fusion.3
  661.0 3.1 multiply_subtract_fusion
  (698 shorter events, 270.9 us)
Async XLA Ops:
  7.2 179.8 %all-gather.7.cloned.1.call-start = ((), (), s32[]{:S(2)}) async-start(), calls=%async_computation.12 | async-start | bytes 3604480 | tf_op jit(solution)/shard_map/all_gather | solution.py:901
  14.5 14.2 %collective-permute-start = (bf16[768,256]{1,0:T(8,128)(2,1)S(1)}, bf16[768,256]{1,0:T(8,128)(2,1)S(1)}, u32[]{:S(2)}, u32[]{:S(2)}) collective-permute-start(bf16[768,256]{1,0:T(8,128)(2,1)S(1)} %get-tuple-element.330.refs_1_), channel_id=1, source_target_pairs={{0,8},{4,12},{8,16},{12,20},{16,24},{20,28},{24,0},{28,4},{1,9},{5... | collective-permute-start | bytes 1179656 | tf_op jit(solution)/shard_map/ppermute | solution.py:613
  30.3 22.9 %collective-permute-start.2 = (bf16[128,2048]{1,0:T(8,128)(2,1)S(1)}, bf16[128,2048]{1,0:T(8,128)(2,1)S(1)}, u32[]{:S(2)}, u32[]{:S(2)}) collective-permute-start(bf16[128,2048]{1,0:T(8,128)(2,1)S(1)} %get-tuple-element.611), channel_id=1, source_target_pairs={{0,4},{4,0},{8,12},{12,8},{16,20},{20,16},{24,28},{28,24},{1,5},{5... | collective-permute-start | bytes 1572872 | tf_op jit(solution)/shard_map/ppermute | solution.py:619
  31.9 21.3 %collective-permute-start.3 = (bf16[128,2048]{1,0:T(8,128)(2,1)S(1)}, bf16[128,2048]{1,0:T(8,128)(2,1)S(1)}, u32[]{:S(2)}, u32[]{:S(2)}) collective-permute-start(bf16[128,2048]{1,0:T(8,128)(2,1)S(1)} %get-tuple-element.610), channel_id=1, source_target_pairs={{0,2},{1,3},{2,0},{3,1},{4,6},{5,7},{6,4},{7,5},{8,10},{9,11},{10,... | collective-permute-start | bytes 1572872 | tf_op jit(solution)/shard_map/ppermute | solution.py:622
  33.4 16.7 %collective-permute-start.6 = (bf16[768,256]{1,0:T(8,128)(2,1)S(1)}, bf16[768,256]{1,0:T(8,128)(2,1)S(1)}, u32[]{:S(2)}, u32[]{:S(2)}) collective-permute-start(bf16[768,256]{1,0:T(8,128)(2,1)S(1)} %collective-permute-done.refs_3_), channel_id=1, source_target_pairs={{0,8},{4,12},{8,16},{12,20},{16,24},{20,28},{24,0},{28,4},{1,9},{5... | collective-permute-start | bytes 1179656 | tf_op jit(solution)/shard_map/ppermute | solution.py:613
  35.0 18.2 %collective-permute-start.7 = (bf16[768,256]{1,0:T(8,128)(2,1)S(1)}, bf16[768,256]{1,0:T(8,128)(2,1)}, u32[]{:S(2)}, u32[]{:S(2)}) collective-permute-start(bf16[768,256]{1,0:T(8,128)(2,1)S(1)} %collective-permute-done.1.refs_2_), channel_id=1, source_target_pairs={{0,8},{4,12},{8,16},{12,20},{16,24},{20,28},{24,0},{28,4},{1,9},{5... | collective-permute-start | bytes 1179656 | tf_op jit(solution)/shard_map/ppermute | solution.py:613
  53.4 25.6 %collective-permute-start.9 = (bf16[256,2048]{1,0:T(8,128)(2,1)S(1)}, bf16[256,2048]{1,0:T(8,128)(2,1)S(1)}, u32[]{:S(2)}, u32[]{:S(2)}) collective-permute-start(bf16[256,2048]{1,0:T(8,128)(2,1)S(1)} %pad_maximum_fusion.4.refs_3_), channel_id=1, source_target_pairs={{0,4},{4,0},{8,12},{12,8},{16,20},{20,16},{24,28},{28,24},{1,5},{5... | collective-permute-start | bytes 3145736 | tf_op jit(solution)/shard_map/ppermute | solution.py:619
  54.0 25.0 %collective-permute-start.8 = (bf16[256,2048]{1,0:T(8,128)(2,1)S(1)}, bf16[256,2048]{1,0:T(8,128)(2,1)}, u32[]{:S(2)}, u32[]{:S(2)}) collective-permute-start(bf16[256,2048]{1,0:T(8,128)(2,1)S(1)} %pad_maximum_fusion.3.refs_1_), channel_id=1, source_target_pairs={{0,2},{1,3},{2,0},{3,1},{4,6},{5,7},{6,4},{7,5},{8,10},{9,11},{10,... | collective-permute-start | bytes 3145736 | tf_op jit(solution)/shard_map/ppermute | solution.py:622
  54.8 19.5 %collective-permute-start.10 = (bf16[768,256]{1,0:T(8,128)(2,1)S(1)}, bf16[768,256]{1,0:T(8,128)(2,1)S(1)}, u32[]{:S(2)}, u32[]{:S(2)}) collective-permute-start(bf16[768,256]{1,0:T(8,128)(2,1)S(1)} %collective-permute-done.6.refs_5_), channel_id=1, source_target_pairs={{0,8},{4,12},{8,16},{12,20},{16,24},{20,28},{24,0},{28,4},{1,9},{5... | collective-permute-start | bytes 1179656 | tf_op jit(solution)/shard_map/ppermute | solution.py:613
  54.9 19.5 %collective-permute-start.12 = (bf16[512,256]{1,0:T(8,128)(2,1)S(1)}, bf16[512,256]{1,0:T(8,128)(2,1)S(1)}, u32[]{:S(2)}, u32[]{:S(2)}) collective-permute-start(bf16[512,256]{1,0:T(8,128)(2,1)S(1)} %pad_maximum_fusion.12.refs_1_), channel_id=1, source_target_pairs={{0,8},{4,12},{8,16},{12,20},{16,24},{20,28},{24,0},{28,4},{1,9},{5... | collective-permute-start | bytes 786440 | tf_op jit(solution)/shard_map/ppermute | solution.py:613
  56.0 23.0 %collective-permute-start.11 = (bf16[768,256]{1,0:T(8,128)(2,1)}, bf16[768,256]{1,0:T(8,128)(2,1)}, u32[]{:S(2)}, u32[]{:S(2)}) collective-permute-start(bf16[768,256]{1,0:T(8,128)(2,1)} %collective-permute-done.7.refs_4_), channel_id=1, source_target_pairs={{0,8},{4,12},{8,16},{12,20},{16,24},{20,28},{24,0},{28,4},{1,9},{5... | collective-permute-start | bytes 1179656 | tf_op jit(solution)/shard_map/ppermute | solution.py:613
  79.6 19.6 %collective-permute-start.19 = (bf16[1408,256]{1,0:T(8,128)(2,1)}, bf16[1408,256]{1,0:T(8,128)(2,1)}, u32[]{:S(2)}, u32[]{:S(2)}) collective-permute-start(bf16[1408,256]{1,0:T(8,128)(2,1)} %copy-done.104), channel_id=1, source_target_pairs={{0,4},{4,0},{8,12},{12,8},{16,20},{20,16},{24,28},{28,24},{1,5},{5... | collective-permute-start | bytes 2162696 | tf_op jit(solution)/shard_map/ppermute | solution.py:619
  80.6 18.5 %collective-permute-start.17 = (bf16[768,256]{1,0:T(8,128)(2,1)}, bf16[768,256]{1,0:T(8,128)(2,1)}, u32[]{:S(2)}, u32[]{:S(2)}) collective-permute-start(bf16[768,256]{1,0:T(8,128)(2,1)} %collective-permute-done.11.refs_6_), channel_id=1, source_target_pairs={{0,8},{4,12},{8,16},{12,20},{16,24},{20,28},{24,0},{28,4},{1,9},{5... | collective-permute-start | bytes 1179656 | tf_op jit(solution)/shard_map/ppermute | solution.py:613
  80.6 18.5 %collective-permute-start.18 = (bf16[512,256]{1,0:T(8,128)(2,1)}, bf16[512,256]{1,0:T(8,128)(2,1)}, u32[]{:S(2)}, u32[]{:S(2)}) collective-permute-start(bf16[512,256]{1,0:T(8,128)(2,1)} %copy-done.96), channel_id=1, source_target_pairs={{0,8},{4,12},{8,16},{12,20},{16,24},{20,28},{24,0},{28,4},{1,9},{5... | collective-permute-start | bytes 786440 | tf_op jit(solution)/shard_map/ppermute | solution.py:613
  102.3 122.3 %all-gather.9.cloned.1.call-start = ((), (), s32[]{:S(2)}) async-start(), calls=%async_computation.13 | async-start | bytes 3604480 | tf_op jit(solution)/shard_map/all_gather | solution.py:901
  119.7 23.0 %collective-permute-start.23 = (bf16[256,2048]{1,0:T(8,128)(2,1)S(1)}, bf16[256,2048]{1,0:T(8,128)(2,1)}, u32[]{:S(2)}, u32[]{:S(2)}) collective-permute-start(bf16[256,2048]{1,0:T(8,128)(2,1)S(1)} %pad_maximum_fusion.6.refs_3_), channel_id=1, source_target_pairs={{0,4},{4,0},{8,12},{12,8},{16,20},{20,16},{24,28},{28,24},{1,5},{5... | collective-permute-start | bytes 3145736 | tf_op jit(solution)/shard_map/ppermute | solution.py:619
  120.7 22.9 %collective-permute-start.22 = (bf16[256,2048]{1,0:T(8,128)(2,1)}, bf16[256,2048]{1,0:T(8,128)(2,1)}, u32[]{:S(2)}, u32[]{:S(2)}) collective-permute-start(bf16[256,2048]{1,0:T(8,128)(2,1)} %pad_maximum_fusion.5.refs_1_), channel_id=1, source_target_pairs={{0,2},{1,3},{2,0},{3,1},{4,6},{5,7},{6,4},{7,5},{8,10},{9,11},{10,... | collective-permute-start | bytes 3145736 | tf_op jit(solution)/shard_map/ppermute | solution.py:622
  122.2 16.1 %collective-permute-start.24 = (bf16[512,256]{1,0:T(8,128)(2,1)}, bf16[512,256]{1,0:T(8,128)(2,1)S(1)}, u32[]{:S(2)}, u32[]{:S(2)}) collective-permute-start(bf16[512,256]{1,0:T(8,128)(2,1)} %collective-permute-done.18.refs_3_), channel_id=1, source_target_pairs={{0,8},{4,12},{8,16},{12,20},{16,24},{20,28},{24,0},{28,4},{1,9},{5... | collective-permute-start | bytes 786440 | tf_op jit(solution)/shard_map/ppermute | solution.py:613
  150.2 16.5 %collective-permute-start.31 = (bf16[256,2048]{1,0:T(8,128)(2,1)}, bf16[256,2048]{1,0:T(8,128)(2,1)}, u32[]{:S(2)}, u32[]{:S(2)}) collective-permute-start(bf16[256,2048]{1,0:T(8,128)(2,1)} %pad_maximum_fusion.5.refs_1_), channel_id=1, source_target_pairs={{0,1},{1,0},{2,3},{3,2},{4,5},{5,4},{6,7},{7,6},{8,9},{9,8},{10,11... | collective-permute-start | bytes 3145736 | tf_op jit(solution)/shard_map/ppermute | solution.py:625
  159.3 25.5 %collective-permute-start.30 = (bf16[256,2048]{1,0:T(8,128)(2,1)}, bf16[256,2048]{1,0:T(8,128)(2,1)}, u32[]{:S(2)}, u32[]{:S(2)}) collective-permute-start(bf16[256,2048]{1,0:T(8,128)(2,1)} %get-tuple-element.361), channel_id=1, source_target_pairs={{0,2},{1,3},{2,0},{3,1},{4,6},{5,7},{6,4},{7,5},{8,10},{9,11},{10,... | collective-permute-start | bytes 3145736 | tf_op jit(solution)/shard_map/ppermute | solution.py:622
  161.8 25.2 %collective-permute-start.29 = (bf16[256,2048]{1,0:T(8,128)(2,1)}, bf16[256,2048]{1,0:T(8,128)(2,1)}, u32[]{:S(2)}, u32[]{:S(2)}) collective-permute-start(bf16[256,2048]{1,0:T(8,128)(2,1)} %get-tuple-element.359), channel_id=1, source_target_pairs={{0,4},{4,0},{8,12},{12,8},{16,20},{20,16},{24,28},{28,24},{1,5},{5... | collective-permute-start | bytes 3145736 | tf_op jit(solution)/shard_map/ppermute | solution.py:619
  162.4 127.3 %all-gather.11.cloned.1.call-start = ((), (), s32[]{:S(2)}) async-start(), calls=%async_computation.14 | async-start | bytes 3604480 | tf_op jit(solution)/shard_map/all_gather | solution.py:901
  207.6 14.9 %collective-permute-start.38 = (bf16[128,2048]{1,0:T(8,128)(2,1)S(1)}, bf16[128,2048]{1,0:T(8,128)(2,1)S(1)}, u32[]{:S(2)}, u32[]{:S(2)}) collective-permute-start(bf16[128,2048]{1,0:T(8,128)(2,1)S(1)} %get-tuple-element.607), channel_id=1, source_target_pairs={{0,4},{4,0},{8,12},{12,8},{16,20},{20,16},{24,28},{28,24},{1,5},{5... | collective-permute-start | bytes 1572872 | tf_op jit(solution)/shard_map/ppermute | solution.py:619
  209.1 13.4 %collective-permute-start.39 = (bf16[128,2048]{1,0:T(8,128)(2,1)S(1)}, bf16[128,2048]{1,0:T(8,128)(2,1)S(1)}, u32[]{:S(2)}, u32[]{:S(2)}) collective-permute-start(bf16[128,2048]{1,0:T(8,128)(2,1)S(1)} %get-tuple-element.606), channel_id=1, source_target_pairs={{0,2},{1,3},{2,0},{3,1},{4,6},{5,7},{6,4},{7,5},{8,10},{9,11},{10,... | collective-permute-start | bytes 1572872 | tf_op jit(solution)/shard_map/ppermute | solution.py:622
  209.6 17.7 %collective-permute-start.37 = (bf16[704,256]{1,0:T(8,128)(2,1)}, bf16[704,256]{1,0:T(8,128)(2,1)}, u32[]{:S(2)}, u32[]{:S(2)}) collective-permute-start(bf16[704,256]{1,0:T(8,128)(2,1)} %get-tuple-element.378), channel_id=1, source_target_pairs={{0,4},{4,0},{8,12},{12,8},{16,20},{20,16},{24,28},{28,24},{1,5},{5... | collective-permute-start | bytes 1081352 | tf_op jit(solution)/shard_map/ppermute | solution.py:619
  229.4 168.6 %reduce-scatter.7.cloned.1.call-start = ((), (), s32[]{:S(2)}) async-start(), calls=%async_computation.6 | async-start | bytes 3604480 | tf_op jit(solution)/shard_map/reduce_scatter | solution.py:1006
  229.4 22.4 %collective-permute-start.41 = (bf16[256,2048]{1,0:T(8,128)(2,1)}, bf16[256,2048]{1,0:T(8,128)(2,1)S(1)}, u32[]{:S(2)}, u32[]{:S(2)}) collective-permute-start(bf16[256,2048]{1,0:T(8,128)(2,1)} %pad_maximum_fusion.8.refs_3_), channel_id=1, source_target_pairs={{0,4},{4,0},{8,12},{12,8},{16,20},{20,16},{24,28},{28,24},{1,5},{5... | collective-permute-start | bytes 3145736 | tf_op jit(solution)/shard_map/ppermute | solution.py:619
  230.9 22.2 %collective-permute-start.40 = (bf16[256,2048]{1,0:T(8,128)(2,1)}, bf16[256,2048]{1,0:T(8,128)(2,1)S(1)}, u32[]{:S(2)}, u32[]{:S(2)}) collective-permute-start(bf16[256,2048]{1,0:T(8,128)(2,1)} %pad_maximum_fusion.7.refs_1_), channel_id=1, source_target_pairs={{0,2},{1,3},{2,0},{3,1},{4,6},{5,7},{6,4},{7,5},{8,10},{9,11},{10,... | collective-permute-start | bytes 3145736 | tf_op jit(solution)/shard_map/ppermute | solution.py:622
  232.7 20.9 %collective-permute-start.43 = (bf16[256,2048]{1,0:T(8,128)(2,1)}, bf16[256,2048]{1,0:T(8,128)(2,1)S(1)}, u32[]{:S(2)}, u32[]{:S(2)}) collective-permute-start(bf16[256,2048]{1,0:T(8,128)(2,1)} %pad_maximum_fusion.8.refs_3_), channel_id=1, source_target_pairs={{0,1},{1,0},{2,3},{3,2},{4,5},{5,4},{6,7},{7,6},{8,9},{9,8},{10,11... | collective-permute-start | bytes 3145736 | tf_op jit(solution)/shard_map/ppermute | solution.py:625
  232.8 20.8 %collective-permute-start.42 = (bf16[256,2048]{1,0:T(8,128)(2,1)}, bf16[256,2048]{1,0:T(8,128)(2,1)S(1)}, u32[]{:S(2)}, u32[]{:S(2)}) collective-permute-start(bf16[256,2048]{1,0:T(8,128)(2,1)} %pad_maximum_fusion.7.refs_1_), channel_id=1, source_target_pairs={{0,1},{1,0},{2,3},{3,2},{4,5},{5,4},{6,7},{7,6},{8,9},{9,8},{10,11... | collective-permute-start | bytes 3145736 | tf_op jit(solution)/shard_map/ppermute | solution.py:625
  289.5 125.6 %reduce-scatter.9.cloned.1.call-start = ((), (), s32[]{:S(2)}) async-start(), calls=%async_computation.7 | async-start | bytes 3604480 | tf_op jit(solution)/shard_map/reduce_scatter | solution.py:1006
  327.7 29.5 %collective-permute-start.51 = (bf16[256,2048]{1,0:T(8,128)(2,1)}, bf16[256,2048]{1,0:T(8,128)(2,1)}, u32[]{:S(2)}, u32[]{:S(2)}) collective-permute-start(bf16[256,2048]{1,0:T(8,128)(2,1)} %get-tuple-element.425), channel_id=1, source_target_pairs={{0,2},{1,3},{2,0},{3,1},{4,6},{5,7},{6,4},{7,5},{8,10},{9,11},{10,... | collective-permute-start | bytes 3145736 | tf_op jit(solution)/shard_map/ppermute | solution.py:622
  329.1 28.1 %collective-permute-start.50 = (bf16[256,2048]{1,0:T(8,128)(2,1)}, bf16[256,2048]{1,0:T(8,128)(2,1)}, u32[]{:S(2)}, u32[]{:S(2)}) collective-permute-start(bf16[256,2048]{1,0:T(8,128)(2,1)} %get-tuple-element.423), channel_id=1, source_target_pairs={{0,4},{4,0},{8,12},{12,8},{16,20},{20,16},{24,28},{28,24},{1,5},{5... | collective-permute-start | bytes 3145736 | tf_op jit(solution)/shard_map/ppermute | solution.py:619
  360.7 173.7 %reduce-scatter.11.cloned.1.call-start = ((), (), s32[]{:S(2)}) async-start(), calls=%async_computation.8 | async-start | bytes 3604480 | tf_op jit(solution)/shard_map/reduce_scatter | solution.py:1006
  360.8 13.8 %collective-permute-start.57 = (bf16[128,2048]{1,0:T(8,128)(2,1)}, bf16[128,2048]{1,0:T(8,128)(2,1)}, u32[]{:S(2)}, u32[]{:S(2)}) collective-permute-start(bf16[128,2048]{1,0:T(8,128)(2,1)} %add_convert_fusion.4), channel_id=1, source_target_pairs={{0,4},{4,0},{8,12},{12,8},{16,20},{20,16},{24,28},{28,24},{1,5},{5... | collective-permute-start | bytes 1572872 | tf_op jit(solution)/shard_map/ppermute | solution.py:619
  362.1 13.2 %collective-permute-start.56 = (bf16[128,2048]{1,0:T(8,128)(2,1)S(1)}, bf16[128,2048]{1,0:T(8,128)(2,1)}, u32[]{:S(2)}, u32[]{:S(2)}) collective-permute-start(bf16[128,2048]{1,0:T(8,128)(2,1)S(1)} %add_convert_fusion.5), channel_id=1, source_target_pairs={{0,2},{1,3},{2,0},{3,1},{4,6},{5,7},{6,4},{7,5},{8,10},{9,11},{10,... | collective-permute-start | bytes 1572872 | tf_op jit(solution)/shard_map/ppermute | solution.py:622
  371.7 13.0 %collective-permute-start.54 = (bf16[256,2048]{1,0:T(8,128)(2,1)}, bf16[256,2048]{1,0:T(8,128)(2,1)}, u32[]{:S(2)}, u32[]{:S(2)}) collective-permute-start(bf16[256,2048]{1,0:T(8,128)(2,1)} %get-tuple-element.437), channel_id=1, source_target_pairs={{0,1},{1,0},{2,3},{3,2},{4,5},{5,4},{6,7},{7,6},{8,9},{9,8},{10,11... | collective-permute-start | bytes 3145736 | tf_op jit(solution)/shard_map/ppermute | solution.py:625
  372.2 214.8 %reduce-scatter.13.cloned.1.call-start = ((), (), s32[]{:S(2)}) async-start(), calls=%async_computation.9 | async-start | bytes 1966080 | tf_op jit(solution)/shard_map/reduce_scatter | solution.py:1006
  383.2 13.6 %collective-permute-start.58 = (bf16[128,2048]{1,0:T(8,128)(2,1)S(1)}, bf16[128,2048]{1,0:T(8,128)(2,1)S(1)}, u32[]{:S(2)}, u32[]{:S(2)}) collective-permute-start(bf16[128,2048]{1,0:T(8,128)(2,1)S(1)} %get-tuple-element.605), channel_id=1, source_target_pairs={{0,4},{4,0},{8,12},{12,8},{16,20},{20,16},{24,28},{28,24},{1,5},{5... | collective-permute-start | bytes 1572872 | tf_op jit(solution)/shard_map/ppermute | solution.py:619
  384.0 13.9 %collective-permute-start.59 = (bf16[128,2048]{1,0:T(8,128)(2,1)S(1)}, bf16[128,2048]{1,0:T(8,128)(2,1)}, u32[]{:S(2)}, u32[]{:S(2)}) collective-permute-start(bf16[128,2048]{1,0:T(8,128)(2,1)S(1)} %get-tuple-element.604), channel_id=1, source_target_pairs={{0,2},{1,3},{2,0},{3,1},{4,6},{5,7},{6,4},{7,5},{8,10},{9,11},{10,... | collective-permute-start | bytes 1572872 | tf_op jit(solution)/shard_map/ppermute | solution.py:622
  400.3 24.5 %collective-permute-start.61 = (bf16[256,2048]{1,0:T(8,128)(2,1)}, bf16[256,2048]{1,0:T(8,128)(2,1)}, u32[]{:S(2)}, u32[]{:S(2)}) collective-permute-start(bf16[256,2048]{1,0:T(8,128)(2,1)} %pad_maximum_fusion.10.refs_3_), channel_id=1, source_target_pairs={{0,4},{4,0},{8,12},{12,8},{16,20},{20,16},{24,28},{28,24},{1,5},{5... | collective-permute-start | bytes 3145736 | tf_op jit(solution)/shard_map/ppermute | solution.py:619
  402.3 24.7 %collective-permute-start.60 = (bf16[256,2048]{1,0:T(8,128)(2,1)}, bf16[256,2048]{1,0:T(8,128)(2,1)}, u32[]{:S(2)}, u32[]{:S(2)}) collective-permute-start(bf16[256,2048]{1,0:T(8,128)(2,1)} %pad_maximum_fusion.9.refs_1_), channel_id=1, source_target_pairs={{0,2},{1,3},{2,0},{3,1},{4,6},{5,7},{6,4},{7,5},{8,10},{9,11},{10,... | collective-permute-start | bytes 3145736 | tf_op jit(solution)/shard_map/ppermute | solution.py:622
  403.3 24.5 %collective-permute-start.65 = (bf16[256,2048]{1,0:T(8,128)(2,1)}, bf16[256,2048]{1,0:T(8,128)(2,1)}, u32[]{:S(2)}, u32[]{:S(2)}) collective-permute-start(bf16[256,2048]{1,0:T(8,128)(2,1)} %pad_maximum_fusion.10.refs_3_), channel_id=1, source_target_pairs={{0,1},{1,0},{2,3},{3,2},{4,5},{5,4},{6,7},{7,6},{8,9},{9,8},{10,11... | collective-permute-start | bytes 3145736 | tf_op jit(solution)/shard_map/ppermute | solution.py:625
  403.3 24.5 %collective-permute-start.64 = (bf16[256,2048]{1,0:T(8,128)(2,1)}, bf16[256,2048]{1,0:T(8,128)(2,1)}, u32[]{:S(2)}, u32[]{:S(2)}) collective-permute-start(bf16[256,2048]{1,0:T(8,128)(2,1)} %pad_maximum_fusion.9.refs_1_), channel_id=1, source_target_pairs={{0,1},{1,0},{2,3},{3,2},{4,5},{5,4},{6,7},{7,6},{8,9},{9,8},{10,11... | collective-permute-start | bytes 3145736 | tf_op jit(solution)/shard_map/ppermute | solution.py:625
  492.5 107.7 %reduce-scatter.17.cloned.1.call-start = ((), (), s32[]{:S(2)}) async-start(), calls=%async_computation.11 | async-start | bytes 1966080 | tf_op jit(solution)/shard_map/reduce_scatter | solution.py:1006
  492.6 15.0 %collective-permute-start.70 = (bf16[256,2048]{1,0:T(8,128)(2,1)}, bf16[256,2048]{1,0:T(8,128)(2,1)}, u32[]{:S(2)}, u32[]{:S(2)}) collective-permute-start(bf16[256,2048]{1,0:T(8,128)(2,1)} %copy-done.103), channel_id=1, source_target_pairs={{0,1},{1,0},{2,3},{3,2},{4,5},{5,4},{6,7},{7,6},{8,9},{9,8},{10,11... | collective-permute-start | bytes 3145736 | tf_op jit(solution)/shard_map/ppermute | solution.py:625
  493.0 16.1 %collective-permute-start.69 = (bf16[256,2048]{1,0:T(8,128)(2,1)}, bf16[256,2048]{1,0:T(8,128)(2,1)}, u32[]{:S(2)}, u32[]{:S(2)}) collective-permute-start(bf16[256,2048]{1,0:T(8,128)(2,1)} %copy-done.102), channel_id=1, source_target_pairs={{0,1},{1,0},{2,3},{3,2},{4,5},{5,4},{6,7},{7,6},{8,9},{9,8},{10,11... | collective-permute-start | bytes 3145736 | tf_op jit(solution)/shard_map/ppermute | solution.py:625
  493.1 16.5 %collective-permute-start.68 = (bf16[256,2048]{1,0:T(8,128)(2,1)}, bf16[256,2048]{1,0:T(8,128)(2,1)}, u32[]{:S(2)}, u32[]{:S(2)}) collective-permute-start(bf16[256,2048]{1,0:T(8,128)(2,1)} %copy-done.101), channel_id=1, source_target_pairs={{0,1},{1,0},{2,3},{3,2},{4,5},{5,4},{6,7},{7,6},{8,9},{9,8},{10,11... | collective-permute-start | bytes 3145736 | tf_op jit(solution)/shard_map/ppermute | solution.py:625
  493.5 29.4 %collective-permute-start.63 = (bf16[256,2048]{1,0:T(8,128)(2,1)}, bf16[256,2048]{1,0:T(8,128)(2,1)}, u32[]{:S(2)}, u32[]{:S(2)}) collective-permute-start(bf16[256,2048]{1,0:T(8,128)(2,1)} %copy-done.99), channel_id=1, source_target_pairs={{0,2},{1,3},{2,0},{3,1},{4,6},{5,7},{6,4},{7,5},{8,10},{9,11},{10,... | collective-permute-start | bytes 3145736 | tf_op jit(solution)/shard_map/ppermute | solution.py:622
  495.4 27.6 %collective-permute-start.62 = (bf16[256,2048]{1,0:T(8,128)(2,1)}, bf16[256,2048]{1,0:T(8,128)(2,1)}, u32[]{:S(2)}, u32[]{:S(2)}) collective-permute-start(bf16[256,2048]{1,0:T(8,128)(2,1)} %copy-done.98), channel_id=1, source_target_pairs={{0,4},{4,0},{8,12},{12,8},{16,20},{20,16},{24,28},{28,24},{1,5},{5... | collective-permute-start | bytes 3145736 | tf_op jit(solution)/shard_map/ppermute | solution.py:619
  507.5 69.8 %collective-permute-start.81 = (bf16[704,256]{1,0:T(8,128)(2,1)}, bf16[704,256]{1,0:T(8,128)(2,1)}, u32[]{:S(2)}, u32[]{:S(2)}) collective-permute-start(bf16[704,256]{1,0:T(8,128)(2,1)} %dynamic-slice_convert_fusion.2), channel_id=1, source_target_pairs={{0,4},{4,0},{8,12},{12,8},{16,20},{20,16},{24,28},{28,24},{1,5},{5... | collective-permute-start | bytes 1081352 | tf_op jit(solution)/shard_map/ppermute | solution.py:619
  509.1 71.1 %collective-permute-start.80 = (bf16[704,256]{1,0:T(8,128)(2,1)}, bf16[704,256]{1,0:T(8,128)(2,1)}, u32[]{:S(2)}, u32[]{:S(2)}) collective-permute-start(bf16[704,256]{1,0:T(8,128)(2,1)} %dynamic-slice_convert_fusion.1), channel_id=1, source_target_pairs={{0,4},{4,0},{8,12},{12,8},{16,20},{20,16},{24,28},{28,24},{1,5},{5... | collective-permute-start | bytes 1081352 | tf_op jit(solution)/shard_map/ppermute | solution.py:619
  523.0 24.8 %collective-permute-start.75 = (bf16[256,2048]{1,0:T(8,128)(2,1)}, bf16[256,2048]{1,0:T(8,128)(2,1)}, u32[]{:S(2)}, u32[]{:S(2)}) collective-permute-start(bf16[256,2048]{1,0:T(8,128)(2,1)} %get-tuple-element.501), channel_id=1, source_target_pairs={{0,2},{1,3},{2,0},{3,1},{4,6},{5,7},{6,4},{7,5},{8,10},{9,11},{10,... | collective-permute-start | bytes 3145736 | tf_op jit(solution)/shard_map/ppermute | solution.py:622
  524.3 35.3 %collective-permute-start.74 = (bf16[256,2048]{1,0:T(8,128)(2,1)}, bf16[256,2048]{1,0:T(8,128)(2,1)}, u32[]{:S(2)}, u32[]{:S(2)}) collective-permute-start(bf16[256,2048]{1,0:T(8,128)(2,1)} %get-tuple-element.499), channel_id=1, source_target_pairs={{0,4},{4,0},{8,12},{12,8},{16,20},{20,16},{24,28},{28,24},{1,5},{5... | collective-permute-start | bytes 3145736 | tf_op jit(solution)/shard_map/ppermute | solution.py:619
  537.0 75.6 %reduce-scatter.15.cloned.1.call-start = ((), (), s32[]{:S(2)}) async-start(), calls=%async_computation.10 | async-start | bytes 1310720 | tf_op jit(solution)/shard_map/reduce_scatter | solution.py:1006
  538.6 32.2 %collective-permute-start.73 = (bf16[128,2048]{1,0:T(8,128)(2,1)}, bf16[128,2048]{1,0:T(8,128)(2,1)S(1)}, u32[]{:S(2)}, u32[]{:S(2)}) collective-permute-start(bf16[128,2048]{1,0:T(8,128)(2,1)} %add_convert_fusion.2), channel_id=1, source_target_pairs={{0,4},{4,0},{8,12},{12,8},{16,20},{20,16},{24,28},{28,24},{1,5},{5... | collective-permute-start | bytes 1572872 | tf_op jit(solution)/shard_map/ppermute | solution.py:619
  547.8 23.5 %collective-permute-start.72 = (bf16[128,2048]{1,0:T(8,128)(2,1)}, bf16[128,2048]{1,0:T(8,128)(2,1)S(1)}, u32[]{:S(2)}, u32[]{:S(2)}) collective-permute-start(bf16[128,2048]{1,0:T(8,128)(2,1)} %add_convert_fusion.3), channel_id=1, source_target_pairs={{0,2},{1,3},{2,0},{3,1},{4,6},{5,7},{6,4},{7,5},{8,10},{9,11},{10,... | collective-permute-start | bytes 1572872 | tf_op jit(solution)/shard_map/ppermute | solution.py:622
  561.7 25.3 %collective-permute-start.78 = (bf16[128,2048]{1,0:T(8,128)(2,1)}, bf16[128,2048]{1,0:T(8,128)(2,1)}, u32[]{:S(2)}, u32[]{:S(2)}) collective-permute-start(bf16[128,2048]{1,0:T(8,128)(2,1)} %add_convert_fusion), channel_id=1, source_target_pairs={{0,4},{4,0},{8,12},{12,8},{16,20},{20,16},{24,28},{28,24},{1,5},{5... | collective-permute-start | bytes 1572872 | tf_op jit(solution)/shard_map/ppermute | solution.py:619
  570.8 16.2 %collective-permute-start.77 = (bf16[128,2048]{1,0:T(8,128)(2,1)}, bf16[128,2048]{1,0:T(8,128)(2,1)}, u32[]{:S(2)}, u32[]{:S(2)}) collective-permute-start(bf16[128,2048]{1,0:T(8,128)(2,1)} %add_convert_fusion.1), channel_id=1, source_target_pairs={{0,2},{1,3},{2,0},{3,1},{4,6},{5,7},{6,4},{7,5},{8,10},{9,11},{10,... | collective-permute-start | bytes 1572872 | tf_op jit(solution)/shard_map/ppermute | solution.py:622
  571.3 15.6 %collective-permute-start.79 = (f32[48,256]{1,0:T(8,128)}, f32[48,256]{1,0:T(8,128)S(1)}, u32[]{:S(2)}, u32[]{:S(2)}) collective-permute-start(f32[48,256]{1,0:T(8,128)} %add.362), channel_id=1, source_target_pairs={{0,16},{4,20},{8,24},{12,28},{16,0},{20,4},{24,8},{28,12},{1,17},{... | collective-permute-start | bytes 147464 | tf_op jit(solution)/shard_map/ppermute | solution.py:616
  586.0 17.0 %collective-permute-start.82 = (bf16[704,256]{1,0:T(8,128)(2,1)S(1)}, bf16[704,256]{1,0:T(8,128)(2,1)}, u32[]{:S(2)}, u32[]{:S(2)}) collective-permute-start(bf16[704,256]{1,0:T(8,128)(2,1)S(1)} %dynamic-slice_convert_fusion), channel_id=1, source_target_pairs={{0,4},{4,0},{8,12},{12,8},{16,20},{20,16},{24,28},{28,24},{1,5},{5... | collective-permute-start | bytes 1081352 | tf_op jit(solution)/shard_map/ppermute | solution.py:619
  592.4 27.0 %collective-permute-start.84 = (f32[48,256]{1,0:T(8,128)S(1)}, f32[48,256]{1,0:T(8,128)}, u32[]{:S(2)}, u32[]{:S(2)}) collective-permute-start(f32[48,256]{1,0:T(8,128)S(1)} %get-tuple-element.591), channel_id=1, source_target_pairs={{0,4},{4,0},{8,12},{12,8},{16,20},{20,16},{24,28},{28,24},{1,5},{5... | collective-permute-start | bytes 147464 | tf_op jit(solution)/shard_map/ppermute | solution.py:619
  593.5 45.1 %collective-permute-start.90 = (bf16[384,256]{1,0:T(8,128)(2,1)}, bf16[384,256]{1,0:T(8,128)(2,1)}, u32[]{:S(2)}, u32[]{:S(2)}) collective-permute-start(bf16[384,256]{1,0:T(8,128)(2,1)} %dynamic-slice_convert_fusion.4), channel_id=1, source_target_pairs={{0,4},{4,0},{8,12},{12,8},{16,20},{20,16},{24,28},{28,24},{1,5},{5... | collective-permute-start | bytes 589832 | tf_op jit(solution)/shard_map/ppermute | solution.py:619
  632.3 33.9 %collective-permute-start.93 = (f32[1,2,2,48,256]{4,3,2,1,0:T(8,128)S(1)}, f32[1,2,2,48,256]{4,3,2,1,0:T(8,128)S(1)}, u32[]{:S(2)}, u32[]{:S(2)}) collective-permute-start(f32[1,2,2,48,256]{4,3,2,1,0:T(8,128)S(1)} %maximum_select_fusion.10), channel_id=1, source_target_pairs={{0,2},{1,3},{2,0},{3,1},{4,6},{5,7},{6,4},{7,5},{8,10},{9,11},{10,... | collective-permute-start | bytes 589832 | tf_op jit(solution)/shard_map/ppermute | solution.py:622
  (221 other events, 1513.2 us)
Sparse Core Ops, SparseCore 0:
  102.5 61.9 all-gather.6
  166.6 57.8 all-gather.8
  229.5 56.3 all-gather.10
  289.6 54.0 reduce-scatter.6
  360.9 54.1 reduce-scatter.8
  417.2 56.0 reduce-scatter.10
  492.6 33.2 reduce-scatter.12
  537.2 35.0 reduce-scatter.16
  587.1 25.5 reduce-scatter.14

commit v3 on v2

--- a/solution.py
+++ b/solution.py
@@ -289,7 +289,7 @@
             pltpu.VMEM((LENGTH, LANES), f32),
             pltpu.VMEM((LENGTH, LANES), f32),
         ],
-        compiler_params=pltpu.CompilerParams(vmem_limit_bytes=28 << 20),
+        compiler_params=pltpu.CompilerParams(vmem_limit_bytes=16 << 20),
         cost_estimate=pl.CostEstimate(
             flops=1 << 20, bytes_accessed=1 << 10, transcendentals=0
         ),
@@ -297,25 +297,25 @@
     )(position, proj, coef)
 
 
-def mixer_backward(position, proj, conv, grad, coef, tile):
-    rows = proj.shape[0]
+def mixer_backward(position, proj, conv, grad, coef):
+    rows, channels = proj.shape[0], coef.shape[1]
     return pl.pallas_call(
         backward_kernel,
-        grid=(1,),
+        grid=(channels // LANES,),
         in_specs=[
             pl.BlockSpec(memory_space=pltpu.SMEM),
-            pl.BlockSpec((rows, 3 * LANES), lambda i: (0, tile)),
-            pl.BlockSpec((rows, LANES), lambda i: (0, tile)),
-            pl.BlockSpec((rows, LANES), lambda i: (0, tile)),
-            pl.BlockSpec((COEF_ROWS, LANES), lambda i: (0, tile)),
+            pl.BlockSpec((rows, 3 * LANES), lambda i: (0, i)),
+            pl.BlockSpec((rows, LANES), lambda i: (0, i)),
+            pl.BlockSpec((rows, LANES), lambda i: (0, i)),
+            pl.BlockSpec((COEF_ROWS, LANES), lambda i: (0, i)),
         ],
         out_specs=[
-            pl.BlockSpec((rows, 3 * LANES), lambda i: (0, 0)),
-            pl.BlockSpec((COEF_ROWS, LANES), lambda i: (0, 0)),
+            pl.BlockSpec((rows, 3 * LANES), lambda i: (0, i)),
+            pl.BlockSpec((COEF_ROWS, LANES), lambda i: (0, i)),
         ],
         out_shape=[
-            jax.ShapeDtypeStruct((rows, 3 * LANES), bf16),
-            jax.ShapeDtypeStruct((COEF_ROWS, LANES), f32),
+            jax.ShapeDtypeStruct((rows, 3 * channels), bf16),
+            jax.ShapeDtypeStruct((COEF_ROWS, channels), f32),
         ],
         scratch_shapes=[
             pltpu.VMEM((3, PAD + LENGTH, LANES), f32),
@@ -325,7 +325,7 @@
             pltpu.VMEM((LENGTH, LANES), f32),
             pltpu.VMEM((LENGTH, LANES), f32),
         ],
-        compiler_params=pltpu.CompilerParams(vmem_limit_bytes=32 << 20),
+        compiler_params=pltpu.CompilerParams(vmem_limit_bytes=24 << 20),
         cost_estimate=pl.CostEstimate(
             flops=1 << 20, bytes_accessed=1 << 10, transcendentals=0
         ),
@@ -376,7 +376,7 @@
         ],
         out_specs=[tile] * 4,
         out_shape=[jax.ShapeDtypeStruct((count, hidden), bf16)] * 4,
-        compiler_params=pltpu.CompilerParams(vmem_limit_bytes=24 << 20),
+        compiler_params=pltpu.CompilerParams(vmem_limit_bytes=20 << 20),
         cost_estimate=NO_COST,
         name="ffn_up",
     )(scales, rows, gate_w, up_w)
@@ -394,7 +394,7 @@
         in_specs=[pl.BlockSpec((TILE, width), lambda i: (i, 0)), whole_spec(right)],
         out_specs=pl.BlockSpec((TILE, right.shape[0]), lambda i: (i, 0)),
         out_shape=jax.ShapeDtypeStruct((count, right.shape[0]), f32),
-        compiler_params=pltpu.CompilerParams(vmem_limit_bytes=24 << 20),
+        compiler_params=pltpu.CompilerParams(vmem_limit_bytes=13 << 20),
         cost_estimate=NO_COST,
         name="rows_product",
     )(left, right)
@@ -420,7 +420,7 @@
         ],
         out_specs=[tile] * 2,
         out_shape=[jax.ShapeDtypeStruct((count, hidden), bf16)] * 2,
-        compiler_params=pltpu.CompilerParams(vmem_limit_bytes=24 << 20),
+        compiler_params=pltpu.CompilerParams(vmem_limit_bytes=14 << 20),
         cost_estimate=NO_COST,
         name="ffn_grad",
     )(rows, down_w, by_gate, by_up)
@@ -457,7 +457,7 @@
         + [whole_spec(add) for add in adds],
         out_specs=[tile_spec] * tiles,
         out_shape=[jax.ShapeDtypeStruct((TILE, width), bf16)] * tiles,
-        compiler_params=pltpu.CompilerParams(vmem_limit_bytes=28 << 20),
+        compiler_params=pltpu.CompilerParams(vmem_limit_bytes=22 << 20),
         cost_estimate=NO_COST,
         name="product",
     )(*lefts, *rights, *adds)
@@ -524,6 +524,55 @@
         cost_estimate=NO_COST,
         name="ffn_weights",
     )(where, gate_weight, up_weight, down_weight)
+
+
+def branch_grads_kernel(out_w, rows_ref, branch_ref, grad_ref, blocks_ref, total):
+    step = pl.program_id(0)
+    rows = rows_ref[...]
+    grad_ref[...] = lax.dot_general(rows, out_w[...], NT, preferred_element_type=f32)
+    term = lax.dot_general(
+        branch_ref[...], rows, (((0,), (0,)), ((), ())), preferred_element_type=f32
+    )
+
+    @pl.when(step == 0)
+    def _():
+        total[...] = term
+
+    @pl.when(step > 0)
+    def _():
+        total[...] += term
+
+    @pl.when(step == pl.num_programs(0) - 1)
+    def _():
+        groups, _, width = blocks_ref.shape
+        for i in range(groups):
+            blocks_ref[i] = total[:, i * width : (i + 1) * width].astype(bf16)
+
+
+def branch_grads(rows, out_w, branch, groups):
+    count, model = rows.shape
+    channels = out_w.shape[0]
+    return pl.pallas_call(
+        branch_grads_kernel,
+        grid=(count // TILE,),
+        in_specs=[
+            whole_spec(out_w),
+            pl.BlockSpec((TILE, model), lambda i: (i, 0)),
+            pl.BlockSpec((TILE, channels), lambda i: (i, 0)),
+        ],
+        out_specs=[
+            pl.BlockSpec((TILE, channels), lambda i: (i, 0)),
+            pl.BlockSpec((groups, channels, model // groups), lambda i: (0, 0, 0)),
+        ],
+        out_shape=[
+            jax.ShapeDtypeStruct((count, channels), f32),
+            jax.ShapeDtypeStruct((groups, channels, model // groups), bf16),
+        ],
+        scratch_shapes=[pltpu.VMEM((channels, model), f32)],
+        compiler_params=pltpu.CompilerParams(vmem_limit_bytes=12 << 20),
+        cost_estimate=NO_COST,
+        name="branch_grads",
+    )(out_w, rows, branch)
 
 
 def weight_grad_kernel(left, right, out):
@@ -549,10 +598,77 @@
         in_specs=[whole_spec(left), pl.BlockSpec((depth, tile), lambda i: (0, i))],
         out_specs=out_spec,
         out_shape=jax.ShapeDtypeStruct(shape, bf16),
-        compiler_params=pltpu.CompilerParams(vmem_limit_bytes=28 << 20),
+        compiler_params=pltpu.CompilerParams(vmem_limit_bytes=16 << 20),
         cost_estimate=NO_COST,
         name="weight_product",
     )(left, right)
+
+
+def finish_kernel(where_ref, total, mine, other, square):
+    width = mine.shape[1]
+    for side, target in ((where_ref[3], mine), (1 - where_ref[3], other)):
+        target[...] = total[:, pl.ds(pl.multiple_of(side * width, LANES), width)]
+    values = total[...].astype(f32)
+    square[...] = jnp.sum(values * values, axis=0, keepdims=True)
+
+
+def finish_units(where, total, x):
+    units, width = total.shape
+    width = width // 2
+    if width % LANES != 0:
+        mine = lax.dynamic_slice_in_dim(total, x * width, width, 1)
+        other = lax.dynamic_slice_in_dim(total, (1 - x) * width, width, 1)
+        values = total.astype(f32)
+        return mine, other, jnp.sum(values * values, axis=0, keepdims=True)
+    return pl.pallas_call(
+        finish_kernel,
+        in_specs=[
+            pl.BlockSpec(memory_space=pltpu.SMEM),
+            pl.BlockSpec(memory_space=pltpu.VMEM),
+        ],
+        out_specs=[pl.BlockSpec(memory_space=pltpu.VMEM)] * 3,
+        out_shape=halves_spec(units, width) + [jax.ShapeDtypeStruct((1, 2 * width), f32)],
+        compiler_params=pltpu.CompilerParams(vmem_limit_bytes=8 << 20),
+        cost_estimate=NO_COST,
+        name="finish_units",
+    )(where, total)
+
+
+def rows_shard_kernel(where_ref, mine, other, out):
+    units = mine.shape[0]
+    for side, source in ((where_ref[3], mine), (1 - where_ref[3], other)):
+        rows = pl.ds(pl.multiple_of(side * units, units), units)
+        out[rows, :] = source[...].astype(f32)
+
+
+def turned_shard_kernel(where_ref, mine, other, out, rows):
+    rows_shard_kernel(where_ref, mine, other, rows)
+    out[...] = rows[...].T
+
+
+def in_shard_kernel(where_ref, mine, other, out):
+    units = mine.shape[0] // 3
+    for side, source in ((where_ref[3], mine), (1 - where_ref[3], other)):
+        for tile in range(units // LANES):
+            start = pl.multiple_of(side * units + tile * LANES, LANES)
+            for j in range(3):
+                row = (tile * 3 + j) * LANES
+                block = source[row : row + LANES, :].astype(f32)
+                out[j, :, pl.ds(start, LANES)] = block.T
+
+
+def shard_of(kernel, where, mine, other, shape, scratch=()):
+    return pl.pallas_call(
+        kernel,
+        in_specs=[pl.BlockSpec(memory_space=pltpu.SMEM)]
+        + [pl.BlockSpec(memory_space=pltpu.VMEM)] * 2,
+        out_specs=pl.BlockSpec(memory_space=pltpu.VMEM),
+        out_shape=jax.ShapeDtypeStruct(shape, f32),
+        scratch_shapes=list(scratch),
+        compiler_params=pltpu.CompilerParams(vmem_limit_bytes=12 << 20),
+        cost_estimate=NO_COST,
+        name="shard",
+    )(where, mine, other)
 
 
 def rows_by_rows(left, right):
@@ -826,19 +942,16 @@
         held = [tie(tile, *self.chain.held) for tile in self.far]
         self.far = [self.net.c(tile) for tile in held]
 
-    def near(self, *more):
-        got = self.chain.wait(*self.far, *more)
-        self.far = got[:4]
-        self.for_x, self.for_y = self.tiles(2, 2, self.far[2:])
-        return got[4:]
+    def arrived(self):
+        self.far = self.chain.wait(*self.far)
+
+    def near(self):
+        self.a, self.b, self.for_x, self.for_y = self.tiles(0, 4, self.far)
 
     def send(self):
         net = self.net
         for_x, for_y = (tie(tile, *self.chain.held) for tile in (self.for_x, self.for_y))
         self.from_x, self.from_y = net.x(for_x), net.y(for_y)
-
-    def hold(self):
-        self.a, self.b = self.tiles(0, 2, self.far[:2])
 
     def second(self, *more):
         net, chain, piece = self.net, self.chain, TILE // 2
@@ -851,12 +964,16 @@
         return got[2:]
 
     def last(self, *more):
+        got = self.chain.wait(self.a_y, self.b_x, *more)
+        self.a_y, self.b_x = got[:2]
+        return (self.sum(), *got[2:])
+
+    def sum(self):
         piece = TILE // 2
-        got = self.chain.wait(self.a_y, self.b_x, *more)
-        a_y, b_x = got[:2]
+        a_y, b_x = self.a_y, self.b_x
         a = self.a[:piece].astype(f32) + self.from_x[:piece].astype(f32) + a_y.astype(f32)
         b = self.b[:piece].astype(f32) + self.from_y[:piece].astype(f32) + b_x.astype(f32)
-        return (jnp.concatenate([a, b], axis=0), *got[2:])
+        return jnp.concatenate([a, b], axis=0)
 
 
 def pick(pair, index):
@@ -949,64 +1066,24 @@
         return wholes
 
 
-class ScatterUnits:
-    def __init__(self, net, chain, grads, x, z, depth):
-        self.net, self.chain, self.grads, self.x, self.z = net, chain, grads, x, z
-        self.depth = depth
-        self.step = 0
-        self.total = self.part()
-        chain.mark(self.total)
-        self.hop()
-
-    def part(self):
-        groups = self.net.groups
-        place = lax.rem(self.z + 2 * groups - 1 - self.step, groups)
-        parts = [
-            lax.dynamic_slice_in_dim(grad, place * 2 * self.depth, 2 * self.depth, 1)
-            for grad in self.grads
-        ]
-        return parts[0] if len(parts) == 1 else jnp.concatenate(parts, axis=0)
-
-    def hop(self):
-        self.total = self.net.z(self.total)
-
-    def got(self):
-        self.came(self.chain.wait(self.total))
-
-    def came(self, total):
-        self.step += 1
-        total = total.astype(f32) + self.part().astype(f32)
-        self.total = low(total) if self.step < self.net.groups - 1 else total
-        self.chain.mark(self.total)
-        if self.step < self.net.groups - 1:
-            self.hop()
-
-    def finish(self):
-        while self.step < self.net.groups - 1:
-            self.got()
-        self.square = jnp.sum(self.total * self.total)
-        other = lax.dynamic_slice_in_dim(self.total, (1 - self.x) * self.depth, self.depth, 1)
-        self.other = low(other)
-        self.chain.mark(self.square, self.other)
+class ReducedUnits:
+    def __init__(self, net, chain, blocks, x):
+        self.net, self.chain, self.x = net, chain, x
+        self.total = lax.psum_scatter(blocks, "dp", axis_index_groups=net.lines)
+
+    def finish(self, where, total=None):
+        total = self.chain.wait(self.total) if total is None else total
+        self.mine, self.other, self.square = finish_units(where, total, self.x)
+        self.chain.mark(self.mine, self.other, self.square)
 
     def trade(self):
         self.traded = self.net.x(tie(self.other, *self.chain.held))
 
-    def pair(self):
-        got, total = self.chain.wait(self.traded, self.total)
-        mine = lax.dynamic_slice_in_dim(total, self.x * self.depth, self.depth, 1)
-        got = got.astype(f32)
-        return jnp.where(self.x == 0, jnp.stack([mine, got]), jnp.stack([got, mine]))
-
-
-class ReducedUnits(ScatterUnits):
-    def __init__(self, net, chain, blocks, x, z, depth):
-        self.net, self.chain, self.x, self.z, self.depth = net, chain, x, z, depth
-        self.step = net.groups - 1
-        self.total = lax.psum_scatter(blocks, "dp", axis_index_groups=net.lines)
-
-    def came(self, total):
-        self.total = total.astype(f32)
+    def shard(self, kernel, where, shape, scratch=()):
+        got = self.chain(self.traded)
+        shard = shard_of(kernel, where, self.mine, got, shape, scratch)
+        self.chain.mark(shard)
+        return shard
 
 
 def on_device(
@@ -1150,10 +1227,10 @@
     (w_out,) = ring_out.whole(position, [(0, channels)])
     product = ScatterProduct(net, chain, [branch], [w_out])
     product.trade()
+    product.arrived()
     product.near()
     product.send()
     back_rows.trade()
-    product.hold()
     back_all = back_rows.whole(position)
     (gate_blocks,) = product.second(gate_blocks)
     ring_down.trade(*chain.held)
@@ -1181,21 +1258,13 @@
     )
     chain.mark(inner_scaled, inner_low)
 
-    def weight_grad(left, right):
-        grad = weight_product(chain(left), right)
-        chain.mark(grad)
-        return grad
-
     def blocks_of(left, right):
         grad = weight_product(chain(left), right, net.groups)
         chain.mark(grad)
         return grad
 
     def reduced(grad):
-        return ReducedUnits(net, chain, chain(grad), x, z, depth)
-
-    def scattered(*grads):
-        return ScatterUnits(net, chain, grads, x, z, depth)
+        return ReducedUnits(net, chain, chain(grad), x)
 
     sum_down = reduced(blocks_of(inner_scaled, back_all))
     w_down = assemble_blocks(chain.wait(down_blocks), position)
@@ -1204,9 +1273,9 @@
     chain.mark(grad_gate, grad_up)
     product = ScatterProduct(net, chain, [grad_gate, grad_up], [w_gate, w_up])
     product.trade()
+    product.arrived()
     product.near()
     product.send()
-    product.hold()
     grad_gate = blocks_of(grad_gate, normed_two_all)
     grad_up = blocks_of(grad_up, normed_two_all)
     product.second()
@@ -1219,119 +1288,103 @@
     grad_middle_low = low(grad_middle)
     chain.mark(grad_middle_low)
     grad_middle_rows = GatherRows(net, chain, grad_middle_low)
+    output_product.arrived()
     output_product.near()
-    output_product.hold()
     (got,) = grad_middle_rows.second(sum_down.total)
-    sum_down.came(got)
-    sum_down.finish()
-    sum_gate.came(chain.wait(sum_gate.total))
-    sum_gate.finish()
-    grad_middle_rows.third()
+    sum_down.finish(position, got)
+    (got,) = grad_middle_rows.third(sum_gate.total)
     grad_middle_rows.trade()
+    output_product.send()
+    sum_gate.finish(position, got)
     sum_down.trade()
     sum_gate.trade()
-    output_product.send()
     grad_middle_all = grad_middle_rows.whole(position)
-    grad_branch = rows_by_rows(chain(grad_middle_all), w_out)
+    grad_branch, grad_out = branch_grads(chain(grad_middle_all), w_out, branch, net.groups)
     chain.mark(grad_branch)
-    proj_grads, small_sums, sums_in = [], [], []
-    for tile in range(tiles):
-        part, sums = mixer_backward(position, proj, conv, chain(grad_branch), coef, tile)
-        chain.mark(part)
-        proj_grads.append(part)
-        small_sums.append(sums)
-        if tile == 0:
-            sums_in.append(reduced(blocks_of(part, normed_all)))
-    span_in = 3 * LANES
-    w_in_parts = [w_in[tile * span_in : (tile + 1) * span_in] for tile in range(tiles)]
-    product = ScatterProduct(net, chain, proj_grads, w_in_parts)
+    sum_out = reduced(grad_out)
+    grad_proj, sums = mixer_backward(position, proj, conv, chain(grad_branch), coef)
+    chain.mark(grad_proj)
+    product = ScatterProduct(net, chain, [grad_proj], [w_in])
+    output_product.from_x, output_product.from_y, sum_down.traded, sum_gate.traded = chain.wait(
+        output_product.from_x, output_product.from_y, sum_down.traded, sum_gate.traded
+    )
     product.trade()
-    grads_in = [blocks_of(part, normed_all) for part in proj_grads[1:]]
+    grad_in = blocks_of(grad_proj, normed_all)
+    product.arrived()
+    sum_in = reduced(grad_in)
     product.near()
     product.send()
-    sums_in += [reduced(grad) for grad in grads_in]
-    product.hold()
-    output_product.second()
-    grad_out = blocks_of(branch, grad_middle_all)
-
-    sums = chain(jnp.concatenate(small_sums, axis=1))
+    sum_up.finish(position)
+    turned = [pltpu.VMEM((2 * hidden, depth), f32)]
+    shard_down = sum_down.shard(rows_shard_kernel, position, (2 * hidden, depth))
+    shard_gate = sum_gate.shard(turned_shard_kernel, position, (depth, 2 * hidden), turned)
+
+    sums = chain(sums)
     sums = jnp.concatenate(
         [sums[:RATE_ROW], -rates_own * residues_own * sums[RATE_ROW:]], axis=0
     )
     chain.mark(sums)
     sums_across = net.z_across(sums, net.bits[0])
-    sum_up.came(chain.wait(sum_up.total))
-    sum_up.finish()
     (across,) = product.second(sums_across)
-    sum_out = reduced(grad_out)
+    output_product.second()
     sum_up.trade()
     sums = chain(sums) + across
     chain.mark(sums)
     sums_across = net.z_across(sums, net.bits[1])
-    (more,) = output_product.last()
-    output = low(middle + more)
-    chain.mark(output)
-
-    def pair_of(total):
-        pair = chain(total.pair())
-        chain.mark(pair)
-        return pair
-
-    shard_down = pair_of(sum_down).reshape(2 * hidden, depth)
-    shard_gate = chain(pair_of(sum_gate).reshape(2 * hidden, depth).T)
-    chain.mark(shard_gate)
-    grad_normed, first, across = product.last(sums_in[0].total, sums_across)
+    grad_normed, across = product.last(sums_across)
     sums = sums + across
     for bit in net.bits[2:]:
         sums = sums + net.z_across(sums, bit)
-    sums_near = net.x(sums)
     grad_from_first, gain_one = norm_back(resid, scale_one, gains[0], grad_normed)
     grad_input = grad_middle + grad_from_first
     chain.mark(gain_one)
-    sums_in[0].came(first)
-    sums_in[0].finish()
-    sums_in[0].trade()
-    sums_in[1].came(chain.wait(sums_in[1].total))
-    sums_in[1].finish()
-    sums_in[1].trade()
-    shard_up = chain(pair_of(sum_up).reshape(2 * hidden, depth).T)
-    chain.mark(shard_up)
-    sum_out.came(chain.wait(sum_out.total))
-    sum_out.finish()
+    sum_out.finish(position)
     sum_out.trade()
-
-    totals = (sum_down, sum_gate, sum_up, sum_out, *sums_in)
-    square = sum((total.square for total in totals)) + jnp.sum(sums * sums) / net.groups
+    sum_in.finish(position)
+    sum_in.trade()
+
+    totals = (sum_down, sum_gate, sum_up, sum_out, sum_in)
+    square = sum((jnp.sum(total.square) for total in totals))
+    square = square + jnp.sum(sums * sums) / net.groups
     last = jnp.concatenate(
         [gain_one.reshape(-1, LANES), gain_two.reshape(-1, LANES), jnp.full((8, LANES), square)]
     )
     last = chain(last)
     chain.mark(last)
-    sums = in_order(sums[None], chain.wait(sums_near)[None], x, 0)[None]
-    across, more = chain.wait(net.c(last), net.c(sums))
+    last = last + chain.wait(net.c(last))
+    chain.mark(last)
+    across, more = chain.wait(net.x(last), net.x(tie(sums, last)))
+    last = last + across
+    sums = in_order(sums[None], more[None], x, 0)[None]
+    across, more = chain.wait(net.y(last), net.c(tie(sums, last)))
     last = last + across
     sums = in_order(sums, more, c, 0)[None]
-    for hop in (net.x, net.y):
-        last = last + chain.wait(hop(last))
-        chain.mark(last)
+    chain.mark(last)
     for bit in net.bits:
         across = net.z_across(last, bit)
         if bit == net.bits[0]:
             more = net.y(tie(sums, last))
-        if bit == net.bits[1]:
-            shard_out = pair_of(sum_out).reshape(2 * channels, depth)
-            shard_in = chain(
-                jnp.stack([total.pair().reshape(2, 3, LANES, depth) for total in sums_in])
-                .transpose(4, 2, 1, 0, 3)
-                .reshape(depth, 3, 2 * channels)
+            shard_out = sum_out.shard(rows_shard_kernel, position, (2 * channels, depth))
+            shard_up = sum_up.shard(
+                turned_shard_kernel, position, (depth, 2 * hidden), turned
             )
-            chain.mark(shard_in)
-        last = last + chain.wait(across)
+            across, more = chain.wait(across, more)
+            sums = in_order(sums, more, y, 0)
+            sums = sums.reshape(8, COEF_ROWS, channels).transpose(1, 0, 2)
+            sums = chain(sums.reshape(COEF_ROWS, model))
+            chain.mark(sums)
+        else:
+            if bit == net.bits[1]:
+                shard_in = sum_in.shard(in_shard_kernel, position, (3, depth, 2 * channels))
+                (rest,) = output_product.last()
+                output = low(middle + rest)
+                chain.mark(output)
+            across = chain.wait(across)
+        last = last + across
         chain.mark(last)
-    sums = in_order(sums, chain.wait(more), y, 0)
+    shard_in = shard_in.transpose(1, 0, 2)
     input_grad = low(grad_input)
     radial_grad = scale_one[:, 0] * jnp.sum(resid * grad_input, axis=1) / model**0.5
-    sums = sums.reshape(8, COEF_ROWS, channels).transpose(1, 0, 2).reshape(COEF_ROWS, model)
     grad_taps = sums[: 3 * TAPS].reshape(taps.shape)
     grad_skip = sums[SKIP_ROW]
     grad_residues = sums[RES_ROW:RATE_ROW]
@@ -1341,7 +1394,7 @@
     square_total = last[2 * span, 0] + jnp.sum(grad_gains * grad_gains)
     grad_norm = jnp.sqrt(square_total)
     factor = jnp.minimum(1.0, CLIP / (grad_norm + 1e-06))
-    factor = tie(factor, shard_in, shard_out, shard_down, shard_gate, shard_up)
+    factor = tie(factor, shard_in, shard_out, shard_down, shard_gate, shard_up, sums)
 
     return (
         output,

time: 689 us -> 665 us (0.965)
  other arithmetic: 110 us -> 87.3 us
  local copies, waits for them, and re-layouts: 98.6 us -> 106 us
    unnamed x367 -> x342, local copies, waits for them, and re-layouts: 77.4 us -> 98.1 us
    pallas_call x2 -> x12, Pallas kernels: 30.1 us -> 46.3 us  [the longest x1 30.1 us: mixer_backward(): pl.pallas_call(backward_kernel, grid=(channels // LANES,), in_specs=[pl.B...]
    ppermute x18, waiting for transfers between devices: 25.6 us -> 38.5 us  [y(): return lax.ppermute(v, 'mp', self.over_y)]
    reduce_scatter x6 -> x5, waiting for transfers between devices: 11.5 us -> 0.05 us  [__init__(): self.total = lax.psum_scatter(blocks, 'dp', axis_index_groups=net.lines)]
    reshape x3 -> x1, local copies, waits for them, and re-layouts: 8.28 us -> 0.78 us  [on_device(): sums = chain(sums.reshape(COEF_ROWS, model))]
    ppermute x9, waiting for transfers between devices: 40 us -> 32.5 us  [z(): return lax.ppermute(v, 'dp', self.ring)]
    convert_element_type x6 -> x0, other arithmetic: 7.02 us -> none  [came(): self.total = total.astype(f32)]
    pallas_call x6 -> x4, Pallas kernels: 37.2 us -> 30.3 us  [weight_product(): pl.pallas_call(weight_grad_kernel, grid=(width // tile,), in_specs=[whole...]
  transfers between devices with their start and end apart: 103 -> 101, of which waited for: 49 -> 48; matrix products, arithmetic and copies ran while one was open for 17% -> 9% of each run, Pallas kernels for 28% -> 29%
where the time goes in v3:
time: 665 us; the launch traced here: 655 us
  Pallas kernels  192 us (29%)
  waiting for transfers between devices  180 us (27%)
  local copies, waits for them, and re-layouts  106 us (16%)
  other arithmetic  87.3 us (13%)
  starting transfers between devices  66.1 us (10%)
  between operations  23.3 us (4%)
    unnamed x342, local copies, waits for them, and re-layouts  98.1 us
    ppermute x28, waiting for transfers between devices, x(): return lax.ppermute(v, 'dp', self.over_x)  78.6 us
    pallas_call x8, Pallas kernels, product_tiles(): pl.pallas_call(functools.partial(product_kernel, len(lefts), len(adds), t...  47 us
    ppermute x18, waiting for transfers between devices, y(): return lax.ppermute(v, 'mp', self.over_y)  38.5 us
    ppermute x28, starting transfers between devices, x(): return lax.ppermute(v, 'dp', self.over_x)  32.6 us
    ppermute x9, waiting for transfers between devices, z(): return lax.ppermute(v, 'dp', self.ring)  32.5 us
    pallas_call x4, Pallas kernels, weight_product(): pl.pallas_call(weight_grad_kernel, grid=(width // tile,), in_specs=[whole...  30.3 us
    pallas_call x1, Pallas kernels, mixer_backward(): pl.pallas_call(backward_kernel, grid=(channels // LANES,), in_specs=[pl.B...  30.1 us
  transfers between devices with their start and end apart: 101, of which 48 were waited for; matrix products, arithmetic and copies ran while one was open for 9% of the time, Pallas kernels for 29%

profile of v3, /device:TPU:0, one launch (start us, length us, event | category | flops | bytes accessed | tf_op | source)
XLA Modules:
  0.0 654.9 jit_solution(16093395610867437952)
XLA Ops:
  11.0 2.6 fusion.2
  14.5 3.0 collective-permute-start.1
  19.8 6.8 %collective-permute-done.1.refs_2_ = bf16[768,256]{1,0:T(8,128)(2,1)S(1)} collective-permute-done((bf16[768,256]{1,0:T(8,128)(2,1)S(1)}, bf16[768,256]{1,0:T(8,128)(2,1)S(1)}, u32[]{:S(2)}, u32[]{:S(2)}) %collective-permute-start.1) | collective-permute-done | bytes 393248 | tf_op jit(solution)/shard_map/ppermute | solution.py:735
  26.6 3.3 collective-permute-done.refs_3_
  37.5 2.3 ffn_weights.1
  39.9 8.2 %collective-permute-done.4 = bf16[256,256]{1,0:T(8,128)(2,1)S(1)} collective-permute-done((bf16[256,256]{1,0:T(8,128)(2,1)S(1)}, bf16[256,256]{1,0:T(8,128)(2,1)S(1)}, u32[]{:S(2)}, u32[]{:S(2)}) %collective-permute-start.4) | collective-permute-done | bytes 131104 | tf_op jit(solution)/shard_map/ppermute | solution.py:735
  48.6 3.2 collective-permute-done.5
  56.3 18.2 %collective-permute-done.12.refs_2_ = bf16[512,256]{1,0:T(8,128)(2,1)S(1)} collective-permute-done((bf16[512,256]{1,0:T(8,128)(2,1)S(1)}, bf16[512,256]{1,0:T(8,128)(2,1)S(1)}, u32[]{:S(2)}, u32[]{:S(2)}) %collective-permute-start.12) | collective-permute-done | bytes 262176 | tf_op jit(solution)/shard_map/ppermute | solution.py:729
  80.5 2.1 collective-permute-done.15.refs_6_
  83.1 3.3 assemble_rows.4.left.right
  86.4 3.2 copy-done.2
  89.6 9.3 %collective-permute-done.18.refs_3_ = bf16[512,256]{1,0:T(8,128)(2,1)} collective-permute-done((bf16[512,256]{1,0:T(8,128)(2,1)}, bf16[512,256]{1,0:T(8,128)(2,1)}, u32[]{:S(2)}, u32[]{:S(2)}) %collective-permute-start.18) | collective-permute-done | bytes 262176 | tf_op jit(solution)/shard_map/ppermute | solution.py:729
  112.2 8.1 %rows_product.1.proj_ref = f32[2048,768]{1,0:T(8,128)S(1)} custom-call(bf16[2048,2048]{1,0:T(8,128)(2,1)S(1)} %copy-done.3, bf16[768,2048]{1,0:T(8,128)(2,1)S(1)} %assemble_columns.2.right.refs_1_), custom_call_target="tpu_custom_call" | custom-call | flops 1024 | bytes 1024 | tf_op jit(solution)/shard_map/rows_product/pallas_call | solution.py:391
  123.9 13.5 %mixer_forward.1 = (bf16[2048,256]{1,0:T(8,128)(2,1)S(1)}, f32[2048,256]{1,0:T(8,128)S(1)}) custom-call(s32[4]{0:T(128)S(1)} %pad_add_fusion.where_ref.refs_0_.pos_ref, f32[2048,768]{1,0:T(8,128)S(1)} %rows_product.1.proj_ref, f32[48,256]{1,0:T(8,128)S(1)} %concatenate.150.coef_ref), custom_call_target="tpu_custom_call" | custom-call | flops 1048576 | bytes 1024 | tf_op jit(solution)/shard_map/mixer_forward/pallas_call | solution.py:271
  137.4 2.6 copy-done.6
  141.4 4.0 collective-permute-done.23.refs_4_
  147.9 2.2 product.8
  154.4 3.0 collective-permute-done.27.refs_4_
  158.9 3.8 product.9
  171.6 3.9 assemble_rows.5.right.rows_ref
  175.5 3.2 copy-done.4
  178.7 12.0 %collective-permute-done.30 = bf16[256,2048]{1,0:T(8,128)(2,1)} collective-permute-done((bf16[256,2048]{1,0:T(8,128)(2,1)}, bf16[256,2048]{1,0:T(8,128)(2,1)}, u32[]{:S(2)}, u32[]{:S(2)}) %collective-permute-start.30) | collective-permute-done | bytes 1048608 | tf_op jit(solution)/shard_map/ppermute | solution.py:738
  200.1 8.0 %collective-permute-done.36 = bf16[128,2048]{1,0:T(8,128)(2,1)S(1)} collective-permute-done((bf16[128,2048]{1,0:T(8,128)(2,1)S(1)}, bf16[128,2048]{1,0:T(8,128)(2,1)S(1)}, u32[]{:S(2)}, u32[]{:S(2)}) %collective-permute-start.36) | collective-permute-done | bytes 524320 | tf_op jit(solution)/shard_map/ppermute | solution.py:735
  216.6 8.5 %collective-permute-done.39 = bf16[128,2048]{1,0:T(8,128)(2,1)S(1)} collective-permute-done((bf16[128,2048]{1,0:T(8,128)(2,1)S(1)}, bf16[128,2048]{1,0:T(8,128)(2,1)S(1)}, u32[]{:S(2)}, u32[]{:S(2)}) %collective-permute-start.39) | collective-permute-done | bytes 524320 | tf_op jit(solution)/shard_map/ppermute | solution.py:738
  225.1 4.4 collective-permute-done.38
  231.6 2.2 collective-permute-done.37
  239.8 2.3 copy-done.54
  243.1 15.1 %collective-permute-done.41.refs_4_ = bf16[256,2048]{1,0:T(8,128)(2,1)S(1)} collective-permute-done((bf16[256,2048]{1,0:T(8,128)(2,1)}, bf16[256,2048]{1,0:T(8,128)(2,1)S(1)}, u32[]{:S(2)}, u32[]{:S(2)}) %collective-permute-start.41) | collective-permute-done | bytes 1048608 | tf_op jit(solution)/shard_map/ppermute | solution.py:735
  259.3 2.1 collective-permute-done.44.refs_6_
  264.8 16.9 %ffn_up.1 = (bf16[2048,704]{1,0:T(8,128)(2,1)S(1)}, bf16[2048,704]{1,0:T(8,128)(2,1)S(1)}, bf16[2048,704]{1,0:T(8,128)(2,1)S(1)}, bf16[2048,704]{1,0:T(8,128)(2,1)S(1)}) custom-call(f32[2]{0:T(128)S(1)} %pad_maximum_fusion.14.scales, bf16[2048,2048]{1,0:T(8,128)(2,1)S(1)} %assemble_rows.6.rows_ref.right, bf16[704,2048]{1,0:T(8,128)(2,1)S(1)} %copy-done.12, ...), custom_call_target="tpu_custom_call" | custom-call | flops 1024 | bytes 1024 | tf_op jit(solution)/shard_map/ffn_up/pallas_call | solution.py:368
  286.8 7.4 %weight_product.4 = bf16[4,704,512]{2,1,0:T(8,128)(2,1)S(1)} custom-call(bf16[2048,704]{1,0:T(8,128)(2,1)S(1)} %get-tuple-element.395.left, bf16[2048,2048]{1,0:T(8,128)(2,1)S(1)} %bitcast.45), custom_call_target="tpu_custom_call" | custom-call | flops 1024 | bytes 1024 | tf_op jit(solution)/shard_map/weight_product/pallas_call | solution.py:595
  300.8 3.4 copy-done.5
  306.1 8.3 %ffn_grad.1 = (bf16[2048,704]{1,0:T(8,128)(2,1)S(1)}, bf16[2048,704]{1,0:T(8,128)(2,1)S(1)}) custom-call(bf16[2048,2048]{1,0:T(8,128)(2,1)S(1)} %copy-done.5, bf16[704,2048]{1,0:T(8,128)(2,1)S(1)} %assemble_blocks.5.down_w.refs_1_, bf16[2048,704]{1,0:T(8,128)(2,1)S(1)} %copy-done.50, bf16[2048,704]{1,0:T(8,128)(2,1)S(1)} %copy-done.52), custom_call_target="tpu_custom_call" | custom-call | flops 1024 | bytes 1024 | tf_op jit(solution)/shard_map/ffn_grad/pallas_call | solution.py:412
  314.5 7.6 %product.10 = (bf16[256,2048]{1,0:T(8,128)(2,1)S(1)}, bf16[256,2048]{1,0:T(8,128)(2,1)S(1)}, bf16[256,2048]{1,0:T(8,128)(2,1)S(1)}, bf16[256,2048]{1,0:T(8,128)(2,1)S(1)}) custom-call(bf16[2048,704]{1,0:T(8,128)(2,1)S(1)} %get-tuple-element.421.refs_0_.left, bf16[2048,704]{1,0:T(8,128)(2,1)S(1)} %get-tuple-element.422.refs_1_.left, ...), custom_call_target="tpu_custom_call" | custom-call | flops 1024 | bytes 1024 | tf_op jit(solution)/shard_map/product/pallas_call | solution.py:450
  331.3 9.2 %product.11 = (bf16[256,2048]{1,0:T(8,128)(2,1)S(1)}, bf16[256,2048]{1,0:T(8,128)(2,1)S(1)}, bf16[256,2048]{1,0:T(8,128)(2,1)}, bf16[256,2048]{1,0:T(8,128)(2,1)}) custom-call(bf16[2048,704]{1,0:T(8,128)(2,1)S(1)} %copy-done.21, bf16[2048,704]{1,0:T(8,128)(2,1)S(1)} %get-tuple-element.422.refs_1_.left, bf16[704,2048]{1,0:T(8,128)(2,1)S(1)} %copy-done.13, ...), custom_call_target="tpu_custom_call" | custom-call | flops 1024 | bytes 1024 | tf_op jit(solution)/shard_map/product/pallas_call | solution.py:450
  343.9 7.4 %weight_product.5 = bf16[4,704,512]{2,1,0:T(8,128)(2,1)S(1)} custom-call(bf16[2048,704]{1,0:T(8,128)(2,1)S(1)} %copy-done.21, bf16[2048,2048]{1,0:T(8,128)(2,1)S(1)} %bitcast.41), custom_call_target="tpu_custom_call" | custom-call | flops 1024 | bytes 1024 | tf_op jit(solution)/shard_map/weight_product/pallas_call | solution.py:595
  352.9 3.4 copy-done.1
  358.2 7.4 %weight_product.6 = bf16[4,704,512]{2,1,0:T(8,128)(2,1)S(1)} custom-call(bf16[2048,704]{1,0:T(8,128)(2,1)S(1)} %copy-done.19, bf16[2048,2048]{1,0:T(8,128)(2,1)S(1)} %copy-done.1), custom_call_target="tpu_custom_call" | custom-call | flops 1024 | bytes 1024 | tf_op jit(solution)/shard_map/weight_product/pallas_call | solution.py:595
  367.9 2.1 add_convert_fusion.5
  374.9 2.3 copy-done.9
  379.1 4.4 product.12
  390.8 3.0 fusion.34
  396.5 4.9 product.13
  405.4 2.3 collective-permute-done.59
  408.9 2.4 pad_maximum_fusion.9.refs_1_
  416.8 19.9 %collective-permute-done.61.refs_4_ = bf16[256,2048]{1,0:T(8,128)(2,1)} collective-permute-done((bf16[256,2048]{1,0:T(8,128)(2,1)}, bf16[256,2048]{1,0:T(8,128)(2,1)}, u32[]{:S(2)}, u32[]{:S(2)}) %collective-permute-start.61) | collective-permute-done | bytes 1048608 | tf_op jit(solution)/shard_map/ppermute | solution.py:735
  443.6 3.6 assemble_rows.7.rows_ref
  447.2 7.7 %branch_grads.1 = (f32[2048,256]{1,0:T(8,128)S(1)}, bf16[4,256,512]{2,1,0:T(8,128)(2,1)S(1)}) custom-call(bf16[256,2048]{1,0:T(8,128)(2,1)S(1)} %copy-done.23, bf16[2048,2048]{1,0:T(8,128)(2,1)S(1)} %assemble_rows.7.rows_ref, bf16[2048,256]{1,0:T(8,128)(2,1)S(1)} %copy-done.32), custom_call_target="tpu_custom_call" | custom-call | flops 1024 | bytes 1024 | tf_op jit(solution)/shard_map/branch_grads/pallas_call | solution.py:555
  459.8 3.0 copy-done.7
  466.1 30.1 %mixer_backward.1 = (bf16[2048,768]{1,0:T(8,128)(2,1)S(1)}, f32[48,256]{1,0:T(8,128)S(1)}) custom-call(s32[4]{0:T(128)S(1)} %pad_add_fusion.where_ref.refs_0_.pos_ref, f32[2048,768]{1,0:T(8,128)S(1)} %copy-done.7, f32[2048,256]{1,0:T(8,128)S(1)} %copy-done.60, f32[2048,256]{1,0:T(8,128)S(1)} %copy-done.62, f32[48,256]{1,0:T(8,128)S(1)} %concatenate.150.coef_ref), custom_call_target="tpu_custom_call" | custom-call | flops 1048576 | bytes 1024 | tf_op jit(solution)/shard_map/mixer_backward/pallas_call | solution.py:302
  496.2 6.4 product.14
  505.2 8.0 %weight_product.7 = bf16[4,768,512]{2,1,0:T(8,128)(2,1)S(1)} custom-call(bf16[2048,768]{1,0:T(8,128)(2,1)S(1)} %get-tuple-element.486.refs_0_.left, bf16[2048,2048]{1,0:T(8,128)(2,1)S(1)} %bitcast.43), custom_call_target="tpu_custom_call" | custom-call | flops 1024 | bytes 1024 | tf_op jit(solution)/shard_map/weight_product/pallas_call | solution.py:595
  516.8 8.4 %product.15 = (bf16[256,2048]{1,0:T(8,128)(2,1)S(1)}, bf16[256,2048]{1,0:T(8,128)(2,1)S(1)}, bf16[256,2048]{1,0:T(8,128)(2,1)}, bf16[256,2048]{1,0:T(8,128)(2,1)}) custom-call(bf16[2048,768]{1,0:T(8,128)(2,1)S(1)} %copy-done.17, bf16[768,2048]{1,0:T(8,128)(2,1)S(1)} %assemble_columns.2.right.refs_1_, bf16[256,2048]{1,0:T(8,128)(2,1)} %collective-permute-done.70.refs_2_, ...), custom_call_target="tpu_custom_call" | custom-call | flops 1024 | bytes 1024 | tf_op jit(solution)/shard_map/product/pallas_call | solution.py:450
  537.2 6.0 collective-permute-done.76
  543.2 9.4 %collective-permute-done.75 = bf16[256,2048]{1,0:T(8,128)(2,1)} collective-permute-done((bf16[256,2048]{1,0:T(8,128)(2,1)}, bf16[256,2048]{1,0:T(8,128)(2,1)}, u32[]{:S(2)}, u32[]{:S(2)}) %collective-permute-start.75) | collective-permute-done | bytes 1048608 | tf_op jit(solution)/shard_map/ppermute | solution.py:738
  584.9 2.5 collective-permute-start.84
  587.5 4.2 fusion.9
  595.5 2.1 collective-permute-done.86
  607.2 2.8 collective-permute-done.82.other
  624.8 2.9 multiply_subtract_fusion.4
  627.8 4.7 multiply_subtract_fusion.2
  632.6 2.8 multiply_subtract_fusion.1
  636.3 2.9 multiply_subtract_fusion.3
  640.4 3.1 multiply_subtract_fusion
  (629 shorter events, 244.2 us)
Async XLA Ops:
  7.2 185.1 %all-gather.7.cloned.1.call-start = ((), (), s32[]{:S(2)}) async-start(), calls=%async_computation.10 | async-start | bytes 3604480 | tf_op jit(solution)/shard_map/all_gather | solution.py:1018
  14.5 12.1 %collective-permute-start.1 = (bf16[768,256]{1,0:T(8,128)(2,1)S(1)}, bf16[768,256]{1,0:T(8,128)(2,1)S(1)}, u32[]{:S(2)}, u32[]{:S(2)}) collective-permute-start(bf16[768,256]{1,0:T(8,128)(2,1)S(1)} %get-tuple-element.294), channel_id=1, source_target_pairs={{0,4},{4,0},{8,12},{12,8},{16,20},{20,16},{24,28},{28,24},{1,5},{5... | collective-permute-start | bytes 1179656 | tf_op jit(solution)/shard_map/ppermute | solution.py:735
  17.5 12.4 %collective-permute-start = (bf16[768,256]{1,0:T(8,128)(2,1)S(1)}, bf16[768,256]{1,0:T(8,128)(2,1)S(1)}, u32[]{:S(2)}, u32[]{:S(2)}) collective-permute-start(bf16[768,256]{1,0:T(8,128)(2,1)S(1)} %get-tuple-element.327.refs_1_), channel_id=1, source_target_pairs={{0,8},{4,12},{8,16},{12,20},{16,24},{20,28},{24,0},{28,4},{1,9},{5... | collective-permute-start | bytes 1179656 | tf_op jit(solution)/shard_map/ppermute | solution.py:729
  31.4 21.5 %collective-permute-start.3 = (bf16[128,2048]{1,0:T(8,128)(2,1)S(1)}, bf16[128,2048]{1,0:T(8,128)(2,1)S(1)}, u32[]{:S(2)}, u32[]{:S(2)}) collective-permute-start(bf16[128,2048]{1,0:T(8,128)(2,1)S(1)} %get-tuple-element.602), channel_id=1, source_target_pairs={{0,2},{1,3},{2,0},{3,1},{4,6},{5,7},{6,4},{7,5},{8,10},{9,11},{10,... | collective-permute-start | bytes 1572872 | tf_op jit(solution)/shard_map/ppermute | solution.py:738
  33.0 19.9 %collective-permute-start.2 = (bf16[128,2048]{1,0:T(8,128)(2,1)S(1)}, bf16[128,2048]{1,0:T(8,128)(2,1)S(1)}, u32[]{:S(2)}, u32[]{:S(2)}) collective-permute-start(bf16[128,2048]{1,0:T(8,128)(2,1)S(1)} %get-tuple-element.603), channel_id=1, source_target_pairs={{0,4},{4,0},{8,12},{12,8},{16,20},{20,16},{24,28},{28,24},{1,5},{5... | collective-permute-start | bytes 1572872 | tf_op jit(solution)/shard_map/ppermute | solution.py:735
  33.5 18.3 %collective-permute-start.7 = (bf16[768,256]{1,0:T(8,128)(2,1)S(1)}, bf16[768,256]{1,0:T(8,128)(2,1)}, u32[]{:S(2)}, u32[]{:S(2)}) collective-permute-start(bf16[768,256]{1,0:T(8,128)(2,1)S(1)} %collective-permute-done.1.refs_2_), channel_id=1, source_target_pairs={{0,8},{4,12},{8,16},{12,20},{16,24},{20,28},{24,0},{28,4},{1,9},{5... | collective-permute-start | bytes 1179656 | tf_op jit(solution)/shard_map/ppermute | solution.py:729
  33.5 19.4 %collective-permute-start.6 = (bf16[768,256]{1,0:T(8,128)(2,1)S(1)}, bf16[768,256]{1,0:T(8,128)(2,1)S(1)}, u32[]{:S(2)}, u32[]{:S(2)}) collective-permute-start(bf16[768,256]{1,0:T(8,128)(2,1)S(1)} %collective-permute-done.refs_3_), channel_id=1, source_target_pairs={{0,8},{4,12},{8,16},{12,20},{16,24},{20,28},{24,0},{28,4},{1,9},{5... | collective-permute-start | bytes 1179656 | tf_op jit(solution)/shard_map/ppermute | solution.py:729
  34.8 13.2 %collective-permute-start.4 = (bf16[256,256]{1,0:T(8,128)(2,1)S(1)}, bf16[256,256]{1,0:T(8,128)(2,1)S(1)}, u32[]{:S(2)}, u32[]{:S(2)}) collective-permute-start(bf16[256,256]{1,0:T(8,128)(2,1)S(1)} %get-tuple-element.297), channel_id=1, source_target_pairs={{0,4},{4,0},{8,12},{12,8},{16,20},{20,16},{24,28},{28,24},{1,5},{5... | collective-permute-start | bytes 393224 | tf_op jit(solution)/shard_map/ppermute | solution.py:735
  53.1 25.7 %collective-permute-start.9 = (bf16[256,2048]{1,0:T(8,128)(2,1)S(1)}, bf16[256,2048]{1,0:T(8,128)(2,1)S(1)}, u32[]{:S(2)}, u32[]{:S(2)}) collective-permute-start(bf16[256,2048]{1,0:T(8,128)(2,1)S(1)} %pad_maximum_fusion.4.refs_3_), channel_id=1, source_target_pairs={{0,4},{4,0},{8,12},{12,8},{16,20},{20,16},{24,28},{28,24},{1,5},{5... | collective-permute-start | bytes 3145736 | tf_op jit(solution)/shard_map/ppermute | solution.py:735
  54.7 24.2 %collective-permute-start.8 = (bf16[256,2048]{1,0:T(8,128)(2,1)S(1)}, bf16[256,2048]{1,0:T(8,128)(2,1)}, u32[]{:S(2)}, u32[]{:S(2)}) collective-permute-start(bf16[256,2048]{1,0:T(8,128)(2,1)S(1)} %pad_maximum_fusion.3.refs_1_), channel_id=1, source_target_pairs={{0,2},{1,3},{2,0},{3,1},{4,6},{5,7},{6,4},{7,5},{8,10},{9,11},{10,... | collective-permute-start | bytes 3145736 | tf_op jit(solution)/shard_map/ppermute | solution.py:738
  55.2 19.3 %collective-permute-start.10 = (bf16[768,256]{1,0:T(8,128)(2,1)S(1)}, bf16[768,256]{1,0:T(8,128)(2,1)S(1)}, u32[]{:S(2)}, u32[]{:S(2)}) collective-permute-start(bf16[768,256]{1,0:T(8,128)(2,1)S(1)} %collective-permute-done.6.refs_5_), channel_id=1, source_target_pairs={{0,8},{4,12},{8,16},{12,20},{16,24},{20,28},{24,0},{28,4},{1,9},{5... | collective-permute-start | bytes 1179656 | tf_op jit(solution)/shard_map/ppermute | solution.py:729
  55.2 19.3 %collective-permute-start.12 = (bf16[512,256]{1,0:T(8,128)(2,1)S(1)}, bf16[512,256]{1,0:T(8,128)(2,1)S(1)}, u32[]{:S(2)}, u32[]{:S(2)}) collective-permute-start(bf16[512,256]{1,0:T(8,128)(2,1)S(1)} %pad_maximum_fusion.12.refs_1_), channel_id=1, source_target_pairs={{0,8},{4,12},{8,16},{12,20},{16,24},{20,28},{24,0},{28,4},{1,9},{5... | collective-permute-start | bytes 786440 | tf_op jit(solution)/shard_map/ppermute | solution.py:729
  55.3 23.5 %collective-permute-start.11 = (bf16[768,256]{1,0:T(8,128)(2,1)}, bf16[768,256]{1,0:T(8,128)(2,1)}, u32[]{:S(2)}, u32[]{:S(2)}) collective-permute-start(bf16[768,256]{1,0:T(8,128)(2,1)} %collective-permute-done.7.refs_4_), channel_id=1, source_target_pairs={{0,8},{4,12},{8,16},{12,20},{16,24},{20,28},{24,0},{28,4},{1,9},{5... | collective-permute-start | bytes 1179656 | tf_op jit(solution)/shard_map/ppermute | solution.py:729
  79.3 19.6 %collective-permute-start.19 = (bf16[1408,256]{1,0:T(8,128)(2,1)}, bf16[1408,256]{1,0:T(8,128)(2,1)}, u32[]{:S(2)}, u32[]{:S(2)}) collective-permute-start(bf16[1408,256]{1,0:T(8,128)(2,1)} %copy-done.117), channel_id=1, source_target_pairs={{0,4},{4,0},{8,12},{12,8},{16,20},{20,16},{24,28},{28,24},{1,5},{5... | collective-permute-start | bytes 2162696 | tf_op jit(solution)/shard_map/ppermute | solution.py:735
  80.4 18.5 %collective-permute-start.17 = (bf16[768,256]{1,0:T(8,128)(2,1)}, bf16[768,256]{1,0:T(8,128)(2,1)}, u32[]{:S(2)}, u32[]{:S(2)}) collective-permute-start(bf16[768,256]{1,0:T(8,128)(2,1)} %collective-permute-done.11.refs_6_), channel_id=1, source_target_pairs={{0,8},{4,12},{8,16},{12,20},{16,24},{20,28},{24,0},{28,4},{1,9},{5... | collective-permute-start | bytes 1179656 | tf_op jit(solution)/shard_map/ppermute | solution.py:729
  80.4 18.5 %collective-permute-start.18 = (bf16[512,256]{1,0:T(8,128)(2,1)}, bf16[512,256]{1,0:T(8,128)(2,1)}, u32[]{:S(2)}, u32[]{:S(2)}) collective-permute-start(bf16[512,256]{1,0:T(8,128)(2,1)} %copy-done.110), channel_id=1, source_target_pairs={{0,8},{4,12},{8,16},{12,20},{16,24},{20,28},{24,0},{28,4},{1,9},{5... | collective-permute-start | bytes 786440 | tf_op jit(solution)/shard_map/ppermute | solution.py:729
  101.3 130.3 %all-gather.9.cloned.1.call-start = ((), (), s32[]{:S(2)}) async-start(), calls=%async_computation.11 | async-start | bytes 3604480 | tf_op jit(solution)/shard_map/all_gather | solution.py:1018
  102.5 17.9 %collective-permute-start.21 = (bf16[128,2048]{1,0:T(8,128)(2,1)S(1)}, bf16[128,2048]{1,0:T(8,128)(2,1)S(1)}, u32[]{:S(2)}, u32[]{:S(2)}) collective-permute-start(bf16[128,2048]{1,0:T(8,128)(2,1)S(1)} %get-tuple-element.600), channel_id=1, source_target_pairs={{0,2},{1,3},{2,0},{3,1},{4,6},{5,7},{6,4},{7,5},{8,10},{9,11},{10,... | collective-permute-start | bytes 1572872 | tf_op jit(solution)/shard_map/ppermute | solution.py:738
  103.5 16.8 %collective-permute-start.20 = (bf16[128,2048]{1,0:T(8,128)(2,1)S(1)}, bf16[128,2048]{1,0:T(8,128)(2,1)S(1)}, u32[]{:S(2)}, u32[]{:S(2)}) collective-permute-start(bf16[128,2048]{1,0:T(8,128)(2,1)S(1)} %get-tuple-element.601), channel_id=1, source_target_pairs={{0,4},{4,0},{8,12},{12,8},{16,20},{20,16},{24,28},{28,24},{1,5},{5... | collective-permute-start | bytes 1572872 | tf_op jit(solution)/shard_map/ppermute | solution.py:735
  121.6 23.9 %collective-permute-start.23 = (bf16[256,2048]{1,0:T(8,128)(2,1)S(1)}, bf16[256,2048]{1,0:T(8,128)(2,1)}, u32[]{:S(2)}, u32[]{:S(2)}) collective-permute-start(bf16[256,2048]{1,0:T(8,128)(2,1)S(1)} %pad_maximum_fusion.6.refs_3_), channel_id=1, source_target_pairs={{0,4},{4,0},{8,12},{12,8},{16,20},{20,16},{24,28},{28,24},{1,5},{5... | collective-permute-start | bytes 3145736 | tf_op jit(solution)/shard_map/ppermute | solution.py:735
  122.4 23.9 %collective-permute-start.22 = (bf16[256,2048]{1,0:T(8,128)(2,1)}, bf16[256,2048]{1,0:T(8,128)(2,1)}, u32[]{:S(2)}, u32[]{:S(2)}) collective-permute-start(bf16[256,2048]{1,0:T(8,128)(2,1)} %pad_maximum_fusion.5.refs_1_), channel_id=1, source_target_pairs={{0,2},{1,3},{2,0},{3,1},{4,6},{5,7},{6,4},{7,5},{8,10},{9,11},{10,... | collective-permute-start | bytes 3145736 | tf_op jit(solution)/shard_map/ppermute | solution.py:738
  123.9 17.5 %collective-permute-start.24 = (bf16[512,256]{1,0:T(8,128)(2,1)}, bf16[512,256]{1,0:T(8,128)(2,1)S(1)}, u32[]{:S(2)}, u32[]{:S(2)}) collective-permute-start(bf16[512,256]{1,0:T(8,128)(2,1)} %collective-permute-done.18.refs_3_), channel_id=1, source_target_pairs={{0,8},{4,12},{8,16},{12,20},{16,24},{20,28},{24,0},{28,4},{1,9},{5... | collective-permute-start | bytes 786440 | tf_op jit(solution)/shard_map/ppermute | solution.py:729
  151.3 14.8 %collective-permute-start.32 = (bf16[256,2048]{1,0:T(8,128)(2,1)S(1)}, bf16[256,2048]{1,0:T(8,128)(2,1)S(1)}, u32[]{:S(2)}, u32[]{:S(2)}) collective-permute-start(bf16[256,2048]{1,0:T(8,128)(2,1)S(1)} %pad_maximum_fusion.6.refs_3_), channel_id=1, source_target_pairs={{0,1},{1,0},{2,3},{3,2},{4,5},{5,4},{6,7},{7,6},{8,9},{9,8},{10,11... | collective-permute-start | bytes 3145736 | tf_op jit(solution)/shard_map/ppermute | solution.py:741
  152.9 15.8 %collective-permute-start.31 = (bf16[256,2048]{1,0:T(8,128)(2,1)}, bf16[256,2048]{1,0:T(8,128)(2,1)}, u32[]{:S(2)}, u32[]{:S(2)}) collective-permute-start(bf16[256,2048]{1,0:T(8,128)(2,1)} %pad_maximum_fusion.5.refs_1_), channel_id=1, source_target_pairs={{0,1},{1,0},{2,3},{3,2},{4,5},{5,4},{6,7},{7,6},{8,9},{9,8},{10,11... | collective-permute-start | bytes 3145736 | tf_op jit(solution)/shard_map/ppermute | solution.py:741
  165.2 25.5 %collective-permute-start.30 = (bf16[256,2048]{1,0:T(8,128)(2,1)}, bf16[256,2048]{1,0:T(8,128)(2,1)}, u32[]{:S(2)}, u32[]{:S(2)}) collective-permute-start(bf16[256,2048]{1,0:T(8,128)(2,1)} %get-tuple-element.357), channel_id=1, source_target_pairs={{0,2},{1,3},{2,0},{3,1},{4,6},{5,7},{6,4},{7,5},{8,10},{9,11},{10,... | collective-permute-start | bytes 3145736 | tf_op jit(solution)/shard_map/ppermute | solution.py:738
  167.0 25.2 %collective-permute-start.29 = (bf16[256,2048]{1,0:T(8,128)(2,1)}, bf16[256,2048]{1,0:T(8,128)(2,1)}, u32[]{:S(2)}, u32[]{:S(2)}) collective-permute-start(bf16[256,2048]{1,0:T(8,128)(2,1)} %get-tuple-element.355), channel_id=1, source_target_pairs={{0,4},{4,0},{8,12},{12,8},{16,20},{20,16},{24,28},{28,24},{1,5},{5... | collective-permute-start | bytes 3145736 | tf_op jit(solution)/shard_map/ppermute | solution.py:735
  168.2 128.0 %all-gather.11.cloned.1.call-start = ((), (), s32[]{:S(2)}) async-start(), calls=%async_computation.12 | async-start | bytes 3604480 | tf_op jit(solution)/shard_map/all_gather | solution.py:1018
  195.2 12.9 %collective-permute-start.36 = (bf16[128,2048]{1,0:T(8,128)(2,1)S(1)}, bf16[128,2048]{1,0:T(8,128)(2,1)S(1)}, u32[]{:S(2)}, u32[]{:S(2)}) collective-permute-start(bf16[128,2048]{1,0:T(8,128)(2,1)S(1)} %add_convert_fusion.6), channel_id=1, source_target_pairs={{0,4},{4,0},{8,12},{12,8},{16,20},{20,16},{24,28},{28,24},{1,5},{5... | collective-permute-start | bytes 1572872 | tf_op jit(solution)/shard_map/ppermute | solution.py:735
  196.3 12.5 %collective-permute-start.35 = (bf16[128,2048]{1,0:T(8,128)(2,1)S(1)}, bf16[128,2048]{1,0:T(8,128)(2,1)S(1)}, u32[]{:S(2)}, u32[]{:S(2)}) collective-permute-start(bf16[128,2048]{1,0:T(8,128)(2,1)S(1)} %add_convert_fusion.7), channel_id=1, source_target_pairs={{0,2},{1,3},{2,0},{3,1},{4,6},{5,7},{6,4},{7,5},{8,10},{9,11},{10,... | collective-permute-start | bytes 1572872 | tf_op jit(solution)/shard_map/ppermute | solution.py:738
  213.3 11.8 %collective-permute-start.39 = (bf16[128,2048]{1,0:T(8,128)(2,1)S(1)}, bf16[128,2048]{1,0:T(8,128)(2,1)S(1)}, u32[]{:S(2)}, u32[]{:S(2)}) collective-permute-start(bf16[128,2048]{1,0:T(8,128)(2,1)S(1)} %get-tuple-element.598), channel_id=1, source_target_pairs={{0,2},{1,3},{2,0},{3,1},{4,6},{5,7},{6,4},{7,5},{8,10},{9,11},{10,... | collective-permute-start | bytes 1572872 | tf_op jit(solution)/shard_map/ppermute | solution.py:738
  214.6 14.9 %collective-permute-start.38 = (bf16[128,2048]{1,0:T(8,128)(2,1)S(1)}, bf16[128,2048]{1,0:T(8,128)(2,1)S(1)}, u32[]{:S(2)}, u32[]{:S(2)}) collective-permute-start(bf16[128,2048]{1,0:T(8,128)(2,1)S(1)} %get-tuple-element.599), channel_id=1, source_target_pairs={{0,4},{4,0},{8,12},{12,8},{16,20},{20,16},{24,28},{28,24},{1,5},{5... | collective-permute-start | bytes 1572872 | tf_op jit(solution)/shard_map/ppermute | solution.py:735
  215.5 18.4 %collective-permute-start.37 = (bf16[704,256]{1,0:T(8,128)(2,1)}, bf16[704,256]{1,0:T(8,128)(2,1)}, u32[]{:S(2)}, u32[]{:S(2)}) collective-permute-start(bf16[704,256]{1,0:T(8,128)(2,1)} %get-tuple-element.374), channel_id=1, source_target_pairs={{0,4},{4,0},{8,12},{12,8},{16,20},{20,16},{24,28},{28,24},{1,5},{5... | collective-permute-start | bytes 1081352 | tf_op jit(solution)/shard_map/ppermute | solution.py:735
  236.1 172.8 %reduce-scatter.6.cloned.1.call-start = ((), (), s32[]{:S(2)}) async-start(), calls=%async_computation.5 | async-start | bytes 3604480 | tf_op jit(solution)/shard_map/reduce_scatter | solution.py:1072
  236.2 22.0 %collective-permute-start.41 = (bf16[256,2048]{1,0:T(8,128)(2,1)}, bf16[256,2048]{1,0:T(8,128)(2,1)S(1)}, u32[]{:S(2)}, u32[]{:S(2)}) collective-permute-start(bf16[256,2048]{1,0:T(8,128)(2,1)} %pad_maximum_fusion.8.refs_3_), channel_id=1, source_target_pairs={{0,4},{4,0},{8,12},{12,8},{16,20},{20,16},{24,28},{28,24},{1,5},{5... | collective-permute-start | bytes 3145736 | tf_op jit(solution)/shard_map/ppermute | solution.py:735
  237.1 21.7 %collective-permute-start.40 = (bf16[256,2048]{1,0:T(8,128)(2,1)}, bf16[256,2048]{1,0:T(8,128)(2,1)S(1)}, u32[]{:S(2)}, u32[]{:S(2)}) collective-permute-start(bf16[256,2048]{1,0:T(8,128)(2,1)} %pad_maximum_fusion.7.refs_1_), channel_id=1, source_target_pairs={{0,2},{1,3},{2,0},{3,1},{4,6},{5,7},{6,4},{7,5},{8,10},{9,11},{10,... | collective-permute-start | bytes 3145736 | tf_op jit(solution)/shard_map/ppermute | solution.py:738
  239.3 20.1 %collective-permute-start.43 = (bf16[256,2048]{1,0:T(8,128)(2,1)}, bf16[256,2048]{1,0:T(8,128)(2,1)S(1)}, u32[]{:S(2)}, u32[]{:S(2)}) collective-permute-start(bf16[256,2048]{1,0:T(8,128)(2,1)} %pad_maximum_fusion.8.refs_3_), channel_id=1, source_target_pairs={{0,1},{1,0},{2,3},{3,2},{4,5},{5,4},{6,7},{7,6},{8,9},{9,8},{10,11... | collective-permute-start | bytes 3145736 | tf_op jit(solution)/shard_map/ppermute | solution.py:741
  239.3 20.0 %collective-permute-start.42 = (bf16[256,2048]{1,0:T(8,128)(2,1)}, bf16[256,2048]{1,0:T(8,128)(2,1)S(1)}, u32[]{:S(2)}, u32[]{:S(2)}) collective-permute-start(bf16[256,2048]{1,0:T(8,128)(2,1)} %pad_maximum_fusion.7.refs_1_), channel_id=1, source_target_pairs={{0,1},{1,0},{2,3},{3,2},{4,5},{5,4},{6,7},{7,6},{8,9},{9,8},{10,11... | collective-permute-start | bytes 3145736 | tf_op jit(solution)/shard_map/ppermute | solution.py:741
  295.9 140.9 %reduce-scatter.8.cloned.1.call-start = ((), (), s32[]{:S(2)}) async-start(), calls=%async_computation.6 | async-start | bytes 3604480 | tf_op jit(solution)/shard_map/reduce_scatter | solution.py:1072
  342.4 25.5 %collective-permute-start.51 = (bf16[256,2048]{1,0:T(8,128)(2,1)}, bf16[256,2048]{1,0:T(8,128)(2,1)}, u32[]{:S(2)}, u32[]{:S(2)}) collective-permute-start(bf16[256,2048]{1,0:T(8,128)(2,1)} %get-tuple-element.420), channel_id=1, source_target_pairs={{0,2},{1,3},{2,0},{3,1},{4,6},{5,7},{6,4},{7,5},{8,10},{9,11},{10,... | collective-permute-start | bytes 3145736 | tf_op jit(solution)/shard_map/ppermute | solution.py:738
  342.7 25.2 %collective-permute-start.50 = (bf16[256,2048]{1,0:T(8,128)(2,1)}, bf16[256,2048]{1,0:T(8,128)(2,1)}, u32[]{:S(2)}, u32[]{:S(2)}) collective-permute-start(bf16[256,2048]{1,0:T(8,128)(2,1)} %get-tuple-element.418), channel_id=1, source_target_pairs={{0,4},{4,0},{8,12},{12,8},{16,20},{20,16},{24,28},{28,24},{1,5},{5... | collective-permute-start | bytes 3145736 | tf_op jit(solution)/shard_map/ppermute | solution.py:735
  372.1 156.0 %reduce-scatter.10.cloned.1.call-start = ((), (), s32[]{:S(2)}) async-start(), calls=%async_computation.7 | async-start | bytes 3604480 | tf_op jit(solution)/shard_map/reduce_scatter | solution.py:1072
  372.1 13.5 %collective-permute-start.57 = (bf16[128,2048]{1,0:T(8,128)(2,1)}, bf16[128,2048]{1,0:T(8,128)(2,1)}, u32[]{:S(2)}, u32[]{:S(2)}) collective-permute-start(bf16[128,2048]{1,0:T(8,128)(2,1)} %add_convert_fusion.4), channel_id=1, source_target_pairs={{0,4},{4,0},{8,12},{12,8},{16,20},{20,16},{24,28},{28,24},{1,5},{5... | collective-permute-start | bytes 1572872 | tf_op jit(solution)/shard_map/ppermute | solution.py:735
  373.4 12.8 %collective-permute-start.56 = (bf16[128,2048]{1,0:T(8,128)(2,1)}, bf16[128,2048]{1,0:T(8,128)(2,1)}, u32[]{:S(2)}, u32[]{:S(2)}) collective-permute-start(bf16[128,2048]{1,0:T(8,128)(2,1)} %add_convert_fusion.5), channel_id=1, source_target_pairs={{0,2},{1,3},{2,0},{3,1},{4,6},{5,7},{6,4},{7,5},{8,10},{9,11},{10,... | collective-permute-start | bytes 1572872 | tf_op jit(solution)/shard_map/ppermute | solution.py:738
  374.6 201.8 %reduce-scatter.14.cloned.1.call-start = ((), (), s32[]{:S(2)}) async-start(), calls=%async_computation.9 | async-start | bytes 1310720 | tf_op jit(solution)/shard_map/reduce_scatter | solution.py:1072
  383.5 12.9 %collective-permute-start.55 = (bf16[256,2048]{1,0:T(8,128)(2,1)S(1)}, bf16[256,2048]{1,0:T(8,128)(2,1)S(1)}, u32[]{:S(2)}, u32[]{:S(2)}) collective-permute-start(bf16[256,2048]{1,0:T(8,128)(2,1)S(1)} %get-tuple-element.434), channel_id=1, source_target_pairs={{0,1},{1,0},{2,3},{3,2},{4,5},{5,4},{6,7},{7,6},{8,9},{9,8},{10,11... | collective-permute-start | bytes 3145736 | tf_op jit(solution)/shard_map/ppermute | solution.py:741
  384.0 12.5 %collective-permute-start.54 = (bf16[256,2048]{1,0:T(8,128)(2,1)S(1)}, bf16[256,2048]{1,0:T(8,128)(2,1)S(1)}, u32[]{:S(2)}, u32[]{:S(2)}) collective-permute-start(bf16[256,2048]{1,0:T(8,128)(2,1)S(1)} %get-tuple-element.432), channel_id=1, source_target_pairs={{0,1},{1,0},{2,3},{3,2},{4,5},{5,4},{6,7},{7,6},{8,9},{9,8},{10,11... | collective-permute-start | bytes 3145736 | tf_op jit(solution)/shard_map/ppermute | solution.py:741
  393.9 13.8 %collective-permute-start.59 = (bf16[128,2048]{1,0:T(8,128)(2,1)S(1)}, bf16[128,2048]{1,0:T(8,128)(2,1)S(1)}, u32[]{:S(2)}, u32[]{:S(2)}) collective-permute-start(bf16[128,2048]{1,0:T(8,128)(2,1)S(1)} %get-tuple-element.596), channel_id=1, source_target_pairs={{0,2},{1,3},{2,0},{3,1},{4,6},{5,7},{6,4},{7,5},{8,10},{9,11},{10,... | collective-permute-start | bytes 1572872 | tf_op jit(solution)/shard_map/ppermute | solution.py:738
  395.2 13.7 %collective-permute-start.58 = (bf16[128,2048]{1,0:T(8,128)(2,1)S(1)}, bf16[128,2048]{1,0:T(8,128)(2,1)}, u32[]{:S(2)}, u32[]{:S(2)}) collective-permute-start(bf16[128,2048]{1,0:T(8,128)(2,1)S(1)} %get-tuple-element.597), channel_id=1, source_target_pairs={{0,4},{4,0},{8,12},{12,8},{16,20},{20,16},{24,28},{28,24},{1,5},{5... | collective-permute-start | bytes 1572872 | tf_op jit(solution)/shard_map/ppermute | solution.py:735
  412.4 24.3 %collective-permute-start.61 = (bf16[256,2048]{1,0:T(8,128)(2,1)}, bf16[256,2048]{1,0:T(8,128)(2,1)}, u32[]{:S(2)}, u32[]{:S(2)}) collective-permute-start(bf16[256,2048]{1,0:T(8,128)(2,1)} %pad_maximum_fusion.10.refs_3_), channel_id=1, source_target_pairs={{0,4},{4,0},{8,12},{12,8},{16,20},{20,16},{24,28},{28,24},{1,5},{5... | collective-permute-start | bytes 3145736 | tf_op jit(solution)/shard_map/ppermute | solution.py:735
  413.1 23.6 %collective-permute-start.60 = (bf16[256,2048]{1,0:T(8,128)(2,1)}, bf16[256,2048]{1,0:T(8,128)(2,1)}, u32[]{:S(2)}, u32[]{:S(2)}) collective-permute-start(bf16[256,2048]{1,0:T(8,128)(2,1)} %pad_maximum_fusion.9.refs_1_), channel_id=1, source_target_pairs={{0,2},{1,3},{2,0},{3,1},{4,6},{5,7},{6,4},{7,5},{8,10},{9,11},{10,... | collective-permute-start | bytes 3145736 | tf_op jit(solution)/shard_map/ppermute | solution.py:738
  414.1 24.8 %collective-permute-start.67 = (bf16[256,2048]{1,0:T(8,128)(2,1)}, bf16[256,2048]{1,0:T(8,128)(2,1)}, u32[]{:S(2)}, u32[]{:S(2)}) collective-permute-start(bf16[256,2048]{1,0:T(8,128)(2,1)} %pad_maximum_fusion.10.refs_3_), channel_id=1, source_target_pairs={{0,1},{1,0},{2,3},{3,2},{4,5},{5,4},{6,7},{7,6},{8,9},{9,8},{10,11... | collective-permute-start | bytes 3145736 | tf_op jit(solution)/shard_map/ppermute | solution.py:741
  414.1 29.4 %collective-permute-start.66 = (bf16[256,2048]{1,0:T(8,128)(2,1)}, bf16[256,2048]{1,0:T(8,128)(2,1)}, u32[]{:S(2)}, u32[]{:S(2)}) collective-permute-start(bf16[256,2048]{1,0:T(8,128)(2,1)} %pad_maximum_fusion.9.refs_1_), channel_id=1, source_target_pairs={{0,1},{1,0},{2,3},{3,2},{4,5},{5,4},{6,7},{7,6},{8,9},{9,8},{10,11... | collective-permute-start | bytes 3145736 | tf_op jit(solution)/shard_map/ppermute | solution.py:741
  437.3 66.8 %collective-permute-start.62 = (bf16[256,2048]{1,0:T(8,128)(2,1)}, bf16[256,2048]{1,0:T(8,128)(2,1)}, u32[]{:S(2)}, u32[]{:S(2)}) collective-permute-start(bf16[256,2048]{1,0:T(8,128)(2,1)} %copy-done.116), channel_id=1, source_target_pairs={{0,4},{4,0},{8,12},{12,8},{16,20},{20,16},{24,28},{28,24},{1,5},{5... | collective-permute-start | bytes 3145736 | tf_op jit(solution)/shard_map/ppermute | solution.py:735
  438.9 65.2 %collective-permute-start.63 = (bf16[256,2048]{1,0:T(8,128)(2,1)}, bf16[256,2048]{1,0:T(8,128)(2,1)}, u32[]{:S(2)}, u32[]{:S(2)}) collective-permute-start(bf16[256,2048]{1,0:T(8,128)(2,1)} %copy-done.115), channel_id=1, source_target_pairs={{0,2},{1,3},{2,0},{3,1},{4,6},{5,7},{6,4},{7,5},{8,10},{9,11},{10,... | collective-permute-start | bytes 3145736 | tf_op jit(solution)/shard_map/ppermute | solution.py:738
  457.2 123.3 %reduce-scatter.12.cloned.1.call-start = ((), (), s32[]{:S(2)}) async-start(), calls=%async_computation.8 | async-start | bytes 3932160 | tf_op jit(solution)/shard_map/reduce_scatter | solution.py:1072
  457.7 45.0 %collective-permute-start.64 = (bf16[704,256]{1,0:T(8,128)(2,1)}, bf16[704,256]{1,0:T(8,128)(2,1)S(1)}, u32[]{:S(2)}, u32[]{:S(2)}) collective-permute-start(bf16[704,256]{1,0:T(8,128)(2,1)} %copy-done.118), channel_id=1, source_target_pairs={{0,4},{4,0},{8,12},{12,8},{16,20},{20,16},{24,28},{28,24},{1,5},{5... | collective-permute-start | bytes 1081352 | tf_op jit(solution)/shard_map/ppermute | solution.py:735
  458.0 45.4 %collective-permute-start.65 = (bf16[704,256]{1,0:T(8,128)(2,1)}, bf16[704,256]{1,0:T(8,128)(2,1)S(1)}, u32[]{:S(2)}, u32[]{:S(2)}) collective-permute-start(bf16[704,256]{1,0:T(8,128)(2,1)} %copy-done.119), channel_id=1, source_target_pairs={{0,4},{4,0},{8,12},{12,8},{16,20},{20,16},{24,28},{28,24},{1,5},{5... | collective-permute-start | bytes 1081352 | tf_op jit(solution)/shard_map/ppermute | solution.py:735
  527.1 25.4 %collective-permute-start.75 = (bf16[256,2048]{1,0:T(8,128)(2,1)}, bf16[256,2048]{1,0:T(8,128)(2,1)}, u32[]{:S(2)}, u32[]{:S(2)}) collective-permute-start(bf16[256,2048]{1,0:T(8,128)(2,1)} %get-tuple-element.494), channel_id=1, source_target_pairs={{0,2},{1,3},{2,0},{3,1},{4,6},{5,7},{6,4},{7,5},{8,10},{9,11},{10,... | collective-permute-start | bytes 3145736 | tf_op jit(solution)/shard_map/ppermute | solution.py:738
  527.7 25.2 %collective-permute-start.74 = (bf16[256,2048]{1,0:T(8,128)(2,1)}, bf16[256,2048]{1,0:T(8,128)(2,1)}, u32[]{:S(2)}, u32[]{:S(2)}) collective-permute-start(bf16[256,2048]{1,0:T(8,128)(2,1)} %get-tuple-element.492), channel_id=1, source_target_pairs={{0,4},{4,0},{8,12},{12,8},{16,20},{20,16},{24,28},{28,24},{1,5},{5... | collective-permute-start | bytes 3145736 | tf_op jit(solution)/shard_map/ppermute | solution.py:735
  555.0 16.4 %collective-permute-start.80 = (bf16[128,2048]{1,0:T(8,128)(2,1)}, bf16[128,2048]{1,0:T(8,128)(2,1)}, u32[]{:S(2)}, u32[]{:S(2)}) collective-permute-start(bf16[128,2048]{1,0:T(8,128)(2,1)} %add_convert_fusion.2), channel_id=1, source_target_pairs={{0,4},{4,0},{8,12},{12,8},{16,20},{20,16},{24,28},{28,24},{1,5},{5... | collective-permute-start | bytes 1572872 | tf_op jit(solution)/shard_map/ppermute | solution.py:735
  557.3 14.1 %collective-permute-start.79 = (bf16[128,2048]{1,0:T(8,128)(2,1)}, bf16[128,2048]{1,0:T(8,128)(2,1)}, u32[]{:S(2)}, u32[]{:S(2)}) collective-permute-start(bf16[128,2048]{1,0:T(8,128)(2,1)} %add_convert_fusion.3), channel_id=1, source_target_pairs={{0,2},{1,3},{2,0},{3,1},{4,6},{5,7},{6,4},{7,5},{8,10},{9,11},{10,... | collective-permute-start | bytes 1572872 | tf_op jit(solution)/shard_map/ppermute | solution.py:738
  566.5 44.4 %collective-permute-start.78 = (bf16[128,2048]{1,0:T(8,128)(2,1)}, bf16[128,2048]{1,0:T(8,128)(2,1)}, u32[]{:S(2)}, u32[]{:S(2)}) collective-permute-start(bf16[128,2048]{1,0:T(8,128)(2,1)} %add_convert_fusion), channel_id=1, source_target_pairs={{0,4},{4,0},{8,12},{12,8},{16,20},{20,16},{24,28},{28,24},{1,5},{5... | collective-permute-start | bytes 1572872 | tf_op jit(solution)/shard_map/ppermute | solution.py:735
  568.2 42.7 %collective-permute-start.77 = (bf16[128,2048]{1,0:T(8,128)(2,1)}, bf16[128,2048]{1,0:T(8,128)(2,1)}, u32[]{:S(2)}, u32[]{:S(2)}) collective-permute-start(bf16[128,2048]{1,0:T(8,128)(2,1)} %add_convert_fusion.1), channel_id=1, source_target_pairs={{0,2},{1,3},{2,0},{3,1},{4,6},{5,7},{6,4},{7,5},{8,10},{9,11},{10,... | collective-permute-start | bytes 1572872 | tf_op jit(solution)/shard_map/ppermute | solution.py:738
  569.8 29.2 %collective-permute-start.90 = (bf16[704,256]{1,0:T(8,128)(2,1)}, bf16[704,256]{1,0:T(8,128)(2,1)}, u32[]{:S(2)}, u32[]{:S(2)}) collective-permute-start(bf16[704,256]{1,0:T(8,128)(2,1)} %get-tuple-element.538), channel_id=1, source_target_pairs={{0,4},{4,0},{8,12},{12,8},{16,20},{20,16},{24,28},{28,24},{1,5},{5... | collective-permute-start | bytes 1081352 | tf_op jit(solution)/shard_map/ppermute | solution.py:735
  (208 other events, 1337.5 us)
Sparse Core Ops, SparseCore 0:
  101.4 62.4 all-gather.6
  168.3 56.4 all-gather.8
  236.3 56.0 all-gather.10
  296.0 53.3 reduce-scatter.5
  372.2 53.7 reduce-scatter.7
  428.2 56.0 reduce-scatter.9
  487.1 27.0 reduce-scatter.13
  516.6 60.9 reduce-scatter.11

commit v4 on v3

--- a/solution.py
+++ b/solution.py
@@ -108,7 +108,7 @@
             u = u_ref[tile_rows(t), :]
             return [a * h + u for a, h in zip(decay, state)]
 
-        state = lax.fori_loop(0, CHUNK, ends, [zero] * POLES, unroll=2)
+        state = lax.fori_loop(0, CHUNK, ends, [zero] * POLES, unroll=8)
         start = []
         for a, h in zip(decay, state):
             jump = power_of_two(a, 7)
@@ -126,7 +126,7 @@
             y_ref[tile_rows(t), :] = terms[0]
             return state
 
-        lax.fori_loop(0, CHUNK, outputs, start, unroll=2)
+        lax.fori_loop(0, CHUNK, outputs, start, unroll=8)
         for n in range(CHUNKS):
             rows = pl.ds(chunk_row(pos_ref, seq, n), CHUNK)
             strided = pl.ds(n, CHUNK, stride=CHUNKS)
@@ -193,7 +193,7 @@
                 after.append((ab + g, a * e + ab))
             return after
 
-        state = lax.fori_loop(0, CHUNK, ends, [(zero, zero)] * POLES, unroll=2)
+        state = lax.fori_loop(0, CHUNK, ends, [(zero, zero)] * POLES, unroll=8)
         start = []
         for a, (b, e) in zip(decay, state):
             jump = power_of_two(a, 7)
@@ -229,7 +229,7 @@
                 return after
 
             begin = [(*start[p], res_sums[p], rate_sums[p]) for p in modes]
-            after = lax.fori_loop(0, CHUNK, outputs, begin, unroll=2)
+            after = lax.fori_loop(0, CHUNK, outputs, begin, unroll=8)
             for p, (_, _, res, rate) in zip(modes, after):
                 res_sums[p], rate_sums[p] = res, rate
 
@@ -390,11 +390,11 @@
     count, width = left.shape
     return pl.pallas_call(
         rows_kernel,
-        grid=(count // TILE,),
-        in_specs=[pl.BlockSpec((TILE, width), lambda i: (i, 0)), whole_spec(right)],
-        out_specs=pl.BlockSpec((TILE, right.shape[0]), lambda i: (i, 0)),
+        grid=(count // (2 * TILE),),
+        in_specs=[pl.BlockSpec((2 * TILE, width), lambda i: (i, 0)), whole_spec(right)],
+        out_specs=pl.BlockSpec((2 * TILE, right.shape[0]), lambda i: (i, 0)),
         out_shape=jax.ShapeDtypeStruct((count, right.shape[0]), f32),
-        compiler_params=pltpu.CompilerParams(vmem_limit_bytes=13 << 20),
+        compiler_params=pltpu.CompilerParams(vmem_limit_bytes=16 << 20),
         cost_estimate=NO_COST,
         name="rows_product",
     )(left, right)
@@ -408,19 +408,19 @@
 
 def ffn_grad(rows, down_w, by_gate, by_up):
     count, hidden = rows.shape[0], down_w.shape[0]
-    tile = pl.BlockSpec((TILE, hidden), lambda i: (i, 0))
+    tile = pl.BlockSpec((2 * TILE, hidden), lambda i: (i, 0))
     return pl.pallas_call(
         grad_kernel,
-        grid=(count // TILE,),
+        grid=(count // (2 * TILE),),
         in_specs=[
-            pl.BlockSpec((TILE, rows.shape[1]), lambda i: (i, 0)),
+            pl.BlockSpec((2 * TILE, rows.shape[1]), lambda i: (i, 0)),
             whole_spec(down_w),
             tile,
             tile,
         ],
         out_specs=[tile] * 2,
         out_shape=[jax.ShapeDtypeStruct((count, hidden), bf16)] * 2,
-        compiler_params=pltpu.CompilerParams(vmem_limit_bytes=14 << 20),
+        compiler_params=pltpu.CompilerParams(vmem_limit_bytes=18 << 20),
         cost_estimate=NO_COST,
         name="ffn_grad",
     )(rows, down_w, by_gate, by_up)

time: 665 us -> 657 us (0.988)
  Pallas kernels: 192 us -> 185 us
  transfers between devices with their start and end apart: 101 -> 101, of which waited for: 48 -> 51; matrix products, arithmetic and copies ran while one was open for 9% -> 9% of each run, Pallas kernels for 29% -> 28%
where the time goes in v4:
time: 657 us; the launch traced here: 649 us
  Pallas kernels  185 us (28%)
  waiting for transfers between devices  180 us (27%)
  local copies, waits for them, and re-layouts  106 us (16%)
  other arithmetic  87.3 us (13%)
  starting transfers between devices  67.2 us (10%)
  between operations  23.3 us (4%)
    unnamed x342, local copies, waits for them, and re-layouts  98 us
    ppermute x28, waiting for transfers between devices, x(): return lax.ppermute(v, 'dp', self.over_x)  77.8 us
    pallas_call x8, Pallas kernels, product_tiles(): pl.pallas_call(functools.partial(product_kernel, len(lefts), len(adds), t...  47 us
    ppermute x18, waiting for transfers between devices, y(): return lax.ppermute(v, 'mp', self.over_y)  38.6 us
    ppermute x9, waiting for transfers between devices, z(): return lax.ppermute(v, 'dp', self.ring)  32.7 us
    ppermute x28, starting transfers between devices, x(): return lax.ppermute(v, 'dp', self.over_x)  31.9 us
    pallas_call x4, Pallas kernels, weight_product(): pl.pallas_call(weight_grad_kernel, grid=(width // tile,), in_specs=[whole...  30.2 us
    pallas_call x1, Pallas kernels, mixer_backward(): pl.pallas_call(backward_kernel, grid=(channels // LANES,), in_specs=[pl.B...  26.2 us
  transfers between devices with their start and end apart: 101, of which 51 were waited for; matrix products, arithmetic and copies ran while one was open for 9% of the time, Pallas kernels for 28%

profile of v4, /device:TPU:0, one launch (start us, length us, event | category | flops | bytes accessed | tf_op | source)
XLA Modules:
  0.0 649.3 jit_solution(6789053841951367035)
XLA Ops:
  11.0 2.6 fusion.2
  14.5 3.0 collective-permute-start.1
  19.8 6.8 %collective-permute-done.1.refs_2_ = bf16[768,256]{1,0:T(8,128)(2,1)S(1)} collective-permute-done((bf16[768,256]{1,0:T(8,128)(2,1)S(1)}, bf16[768,256]{1,0:T(8,128)(2,1)S(1)}, u32[]{:S(2)}, u32[]{:S(2)}) %collective-permute-start.1) | collective-permute-done | bytes 393248 | tf_op jit(solution)/shard_map/ppermute | solution.py:735
  26.6 3.3 collective-permute-done.refs_3_
  37.5 2.3 ffn_weights.1
  39.9 8.2 %collective-permute-done.4 = bf16[256,256]{1,0:T(8,128)(2,1)S(1)} collective-permute-done((bf16[256,256]{1,0:T(8,128)(2,1)S(1)}, bf16[256,256]{1,0:T(8,128)(2,1)S(1)}, u32[]{:S(2)}, u32[]{:S(2)}) %collective-permute-start.4) | collective-permute-done | bytes 131104 | tf_op jit(solution)/shard_map/ppermute | solution.py:735
  48.6 3.2 collective-permute-done.5
  56.3 18.2 %collective-permute-done.12.refs_2_ = bf16[512,256]{1,0:T(8,128)(2,1)S(1)} collective-permute-done((bf16[512,256]{1,0:T(8,128)(2,1)S(1)}, bf16[512,256]{1,0:T(8,128)(2,1)S(1)}, u32[]{:S(2)}, u32[]{:S(2)}) %collective-permute-start.12) | collective-permute-done | bytes 262176 | tf_op jit(solution)/shard_map/ppermute | solution.py:729
  80.5 2.1 collective-permute-done.15.refs_6_
  83.1 3.3 assemble_rows.4.left.right
  86.4 3.2 copy-done.2
  89.6 9.3 %collective-permute-done.18.refs_3_ = bf16[512,256]{1,0:T(8,128)(2,1)} collective-permute-done((bf16[512,256]{1,0:T(8,128)(2,1)}, bf16[512,256]{1,0:T(8,128)(2,1)}, u32[]{:S(2)}, u32[]{:S(2)}) %collective-permute-start.18) | collective-permute-done | bytes 262176 | tf_op jit(solution)/shard_map/ppermute | solution.py:729
  110.1 2.0 assemble_columns.2.right.refs_1_
  112.2 7.3 %rows_product.1.proj_ref = f32[2048,768]{1,0:T(8,128)S(1)} custom-call(bf16[2048,2048]{1,0:T(8,128)(2,1)S(1)} %copy-done.3, bf16[768,2048]{1,0:T(8,128)(2,1)S(1)} %assemble_columns.2.right.refs_1_), custom_call_target="tpu_custom_call" | custom-call | flops 1024 | bytes 1024 | tf_op jit(solution)/shard_map/rows_product/pallas_call | solution.py:391
  123.2 11.5 %mixer_forward.1 = (bf16[2048,256]{1,0:T(8,128)(2,1)S(1)}, f32[2048,256]{1,0:T(8,128)S(1)}) custom-call(s32[4]{0:T(128)S(1)} %pad_add_fusion.where_ref.refs_0_.pos_ref, f32[2048,768]{1,0:T(8,128)S(1)} %rows_product.1.proj_ref, f32[48,256]{1,0:T(8,128)S(1)} %concatenate.150.coef_ref), custom_call_target="tpu_custom_call" | custom-call | flops 1048576 | bytes 1024 | tf_op jit(solution)/shard_map/mixer_forward/pallas_call | solution.py:271
  134.8 2.6 copy-done.6
  138.9 5.8 collective-permute-done.23.refs_4_
  147.2 2.2 product.8
  153.6 3.0 collective-permute-done.27.refs_4_
  158.1 3.8 product.9
  170.8 3.9 assemble_rows.5.right.rows_ref
  174.8 3.2 copy-done.4
  177.9 12.0 %collective-permute-done.30 = bf16[256,2048]{1,0:T(8,128)(2,1)} collective-permute-done((bf16[256,2048]{1,0:T(8,128)(2,1)}, bf16[256,2048]{1,0:T(8,128)(2,1)}, u32[]{:S(2)}, u32[]{:S(2)}) %collective-permute-start.30) | collective-permute-done | bytes 1048608 | tf_op jit(solution)/shard_map/ppermute | solution.py:738
  199.3 8.0 %collective-permute-done.36 = bf16[128,2048]{1,0:T(8,128)(2,1)S(1)} collective-permute-done((bf16[128,2048]{1,0:T(8,128)(2,1)S(1)}, bf16[128,2048]{1,0:T(8,128)(2,1)S(1)}, u32[]{:S(2)}, u32[]{:S(2)}) %collective-permute-start.36) | collective-permute-done | bytes 524320 | tf_op jit(solution)/shard_map/ppermute | solution.py:735
  215.8 8.5 %collective-permute-done.39 = bf16[128,2048]{1,0:T(8,128)(2,1)S(1)} collective-permute-done((bf16[128,2048]{1,0:T(8,128)(2,1)S(1)}, bf16[128,2048]{1,0:T(8,128)(2,1)S(1)}, u32[]{:S(2)}, u32[]{:S(2)}) %collective-permute-start.39) | collective-permute-done | bytes 524320 | tf_op jit(solution)/shard_map/ppermute | solution.py:738
  224.3 4.4 collective-permute-done.38
  230.8 2.2 collective-permute-done.37
  239.0 2.3 copy-done.54
  242.4 15.0 %collective-permute-done.41.refs_4_ = bf16[256,2048]{1,0:T(8,128)(2,1)S(1)} collective-permute-done((bf16[256,2048]{1,0:T(8,128)(2,1)}, bf16[256,2048]{1,0:T(8,128)(2,1)S(1)}, u32[]{:S(2)}, u32[]{:S(2)}) %collective-permute-start.41) | collective-permute-done | bytes 1048608 | tf_op jit(solution)/shard_map/ppermute | solution.py:735
  258.6 2.1 collective-permute-done.44.refs_6_
  264.0 16.9 %ffn_up.1 = (bf16[2048,704]{1,0:T(8,128)(2,1)S(1)}, bf16[2048,704]{1,0:T(8,128)(2,1)S(1)}, bf16[2048,704]{1,0:T(8,128)(2,1)S(1)}, bf16[2048,704]{1,0:T(8,128)(2,1)S(1)}) custom-call(f32[2]{0:T(128)S(1)} %pad_maximum_fusion.14.scales, bf16[2048,2048]{1,0:T(8,128)(2,1)S(1)} %assemble_rows.6.rows_ref.right, bf16[704,2048]{1,0:T(8,128)(2,1)S(1)} %copy-done.12, ...), custom_call_target="tpu_custom_call" | custom-call | flops 1024 | bytes 1024 | tf_op jit(solution)/shard_map/ffn_up/pallas_call | solution.py:368
  286.0 7.4 %weight_product.4 = bf16[4,704,512]{2,1,0:T(8,128)(2,1)S(1)} custom-call(bf16[2048,704]{1,0:T(8,128)(2,1)S(1)} %get-tuple-element.395.left, bf16[2048,2048]{1,0:T(8,128)(2,1)S(1)} %bitcast.45), custom_call_target="tpu_custom_call" | custom-call | flops 1024 | bytes 1024 | tf_op jit(solution)/shard_map/weight_product/pallas_call | solution.py:595
  300.1 3.4 copy-done.5
  305.3 7.5 %ffn_grad.1 = (bf16[2048,704]{1,0:T(8,128)(2,1)S(1)}, bf16[2048,704]{1,0:T(8,128)(2,1)S(1)}) custom-call(bf16[2048,2048]{1,0:T(8,128)(2,1)S(1)} %copy-done.5, bf16[704,2048]{1,0:T(8,128)(2,1)S(1)} %assemble_blocks.5.down_w.refs_1_, bf16[2048,704]{1,0:T(8,128)(2,1)S(1)} %copy-done.50, bf16[2048,704]{1,0:T(8,128)(2,1)S(1)} %copy-done.52), custom_call_target="tpu_custom_call" | custom-call | flops 1024 | bytes 1024 | tf_op jit(solution)/shard_map/ffn_grad/pallas_call | solution.py:412
  312.9 7.6 %product.10 = (bf16[256,2048]{1,0:T(8,128)(2,1)S(1)}, bf16[256,2048]{1,0:T(8,128)(2,1)S(1)}, bf16[256,2048]{1,0:T(8,128)(2,1)S(1)}, bf16[256,2048]{1,0:T(8,128)(2,1)S(1)}) custom-call(bf16[2048,704]{1,0:T(8,128)(2,1)S(1)} %get-tuple-element.421.refs_0_.left, bf16[2048,704]{1,0:T(8,128)(2,1)S(1)} %get-tuple-element.422.refs_1_.left, ...), custom_call_target="tpu_custom_call" | custom-call | flops 1024 | bytes 1024 | tf_op jit(solution)/shard_map/product/pallas_call | solution.py:450
  329.7 9.2 %product.11 = (bf16[256,2048]{1,0:T(8,128)(2,1)S(1)}, bf16[256,2048]{1,0:T(8,128)(2,1)S(1)}, bf16[256,2048]{1,0:T(8,128)(2,1)}, bf16[256,2048]{1,0:T(8,128)(2,1)}) custom-call(bf16[2048,704]{1,0:T(8,128)(2,1)S(1)} %copy-done.21, bf16[2048,704]{1,0:T(8,128)(2,1)S(1)} %get-tuple-element.422.refs_1_.left, bf16[704,2048]{1,0:T(8,128)(2,1)S(1)} %copy-done.13, ...), custom_call_target="tpu_custom_call" | custom-call | flops 1024 | bytes 1024 | tf_op jit(solution)/shard_map/product/pallas_call | solution.py:450
  342.4 7.4 %weight_product.5 = bf16[4,704,512]{2,1,0:T(8,128)(2,1)S(1)} custom-call(bf16[2048,704]{1,0:T(8,128)(2,1)S(1)} %copy-done.21, bf16[2048,2048]{1,0:T(8,128)(2,1)S(1)} %bitcast.41), custom_call_target="tpu_custom_call" | custom-call | flops 1024 | bytes 1024 | tf_op jit(solution)/shard_map/weight_product/pallas_call | solution.py:595
  351.4 3.4 copy-done.1
  356.7 7.4 %weight_product.6 = bf16[4,704,512]{2,1,0:T(8,128)(2,1)S(1)} custom-call(bf16[2048,704]{1,0:T(8,128)(2,1)S(1)} %copy-done.19, bf16[2048,2048]{1,0:T(8,128)(2,1)S(1)} %copy-done.1), custom_call_target="tpu_custom_call" | custom-call | flops 1024 | bytes 1024 | tf_op jit(solution)/shard_map/weight_product/pallas_call | solution.py:595
  366.4 2.1 add_convert_fusion.5
  373.5 2.2 copy-done.9
  377.6 4.4 product.12
  389.2 3.0 fusion.34
  394.9 4.9 product.13
  403.8 2.3 collective-permute-done.59
  407.3 2.4 pad_maximum_fusion.9.refs_1_
  415.2 19.9 %collective-permute-done.61.refs_4_ = bf16[256,2048]{1,0:T(8,128)(2,1)} collective-permute-done((bf16[256,2048]{1,0:T(8,128)(2,1)}, bf16[256,2048]{1,0:T(8,128)(2,1)}, u32[]{:S(2)}, u32[]{:S(2)}) %collective-permute-start.61) | collective-permute-done | bytes 1048608 | tf_op jit(solution)/shard_map/ppermute | solution.py:735
  442.0 3.6 assemble_rows.7.rows_ref
  445.6 7.7 %branch_grads.1 = (f32[2048,256]{1,0:T(8,128)S(1)}, bf16[4,256,512]{2,1,0:T(8,128)(2,1)S(1)}) custom-call(bf16[256,2048]{1,0:T(8,128)(2,1)S(1)} %copy-done.23, bf16[2048,2048]{1,0:T(8,128)(2,1)S(1)} %assemble_rows.7.rows_ref, bf16[2048,256]{1,0:T(8,128)(2,1)S(1)} %copy-done.32), custom_call_target="tpu_custom_call" | custom-call | flops 1024 | bytes 1024 | tf_op jit(solution)/shard_map/branch_grads/pallas_call | solution.py:555
  457.9 3.0 copy-done.7
  464.3 26.2 %mixer_backward.1 = (bf16[2048,768]{1,0:T(8,128)(2,1)S(1)}, f32[48,256]{1,0:T(8,128)S(1)}) custom-call(s32[4]{0:T(128)S(1)} %pad_add_fusion.where_ref.refs_0_.pos_ref, f32[2048,768]{1,0:T(8,128)S(1)} %copy-done.7, f32[2048,256]{1,0:T(8,128)S(1)} %copy-done.60, f32[2048,256]{1,0:T(8,128)S(1)} %copy-done.62, f32[48,256]{1,0:T(8,128)S(1)} %concatenate.150.coef_ref), custom_call_target="tpu_custom_call" | custom-call | flops 1048576 | bytes 1024 | tf_op jit(solution)/shard_map/mixer_backward/pallas_call | solution.py:302
  490.5 6.4 product.14
  499.4 8.0 %weight_product.7 = bf16[4,768,512]{2,1,0:T(8,128)(2,1)S(1)} custom-call(bf16[2048,768]{1,0:T(8,128)(2,1)S(1)} %get-tuple-element.486.refs_0_.left, bf16[2048,2048]{1,0:T(8,128)(2,1)S(1)} %bitcast.43), custom_call_target="tpu_custom_call" | custom-call | flops 1024 | bytes 1024 | tf_op jit(solution)/shard_map/weight_product/pallas_call | solution.py:595
  511.0 8.4 %product.15 = (bf16[256,2048]{1,0:T(8,128)(2,1)S(1)}, bf16[256,2048]{1,0:T(8,128)(2,1)S(1)}, bf16[256,2048]{1,0:T(8,128)(2,1)}, bf16[256,2048]{1,0:T(8,128)(2,1)}) custom-call(bf16[2048,768]{1,0:T(8,128)(2,1)S(1)} %copy-done.17, bf16[768,2048]{1,0:T(8,128)(2,1)S(1)} %assemble_columns.2.right.refs_1_, bf16[256,2048]{1,0:T(8,128)(2,1)} %collective-permute-done.70.refs_2_, ...), custom_call_target="tpu_custom_call" | custom-call | flops 1024 | bytes 1024 | tf_op jit(solution)/shard_map/product/pallas_call | solution.py:450
  531.5 5.7 collective-permute-done.76
  537.2 9.7 %collective-permute-done.75 = bf16[256,2048]{1,0:T(8,128)(2,1)} collective-permute-done((bf16[256,2048]{1,0:T(8,128)(2,1)}, bf16[256,2048]{1,0:T(8,128)(2,1)}, u32[]{:S(2)}, u32[]{:S(2)}) %collective-permute-start.75) | collective-permute-done | bytes 1048608 | tf_op jit(solution)/shard_map/ppermute | solution.py:738
  547.2 2.1 add_convert_fusion.2
  582.4 4.2 fusion.9
  589.8 2.1 collective-permute-done.86
  619.2 2.9 multiply_subtract_fusion.4
  622.1 4.7 multiply_subtract_fusion.2
  626.9 2.8 multiply_subtract_fusion.1
  630.7 2.9 multiply_subtract_fusion.3
  634.8 3.1 multiply_subtract_fusion
  (629 shorter events, 245.7 us)
Async XLA Ops:
  7.2 184.3 %all-gather.7.cloned.1.call-start = ((), (), s32[]{:S(2)}) async-start(), calls=%async_computation.10 | async-start | bytes 3604480 | tf_op jit(solution)/shard_map/all_gather | solution.py:1018
  14.5 12.1 %collective-permute-start.1 = (bf16[768,256]{1,0:T(8,128)(2,1)S(1)}, bf16[768,256]{1,0:T(8,128)(2,1)S(1)}, u32[]{:S(2)}, u32[]{:S(2)}) collective-permute-start(bf16[768,256]{1,0:T(8,128)(2,1)S(1)} %get-tuple-element.294), channel_id=1, source_target_pairs={{0,4},{4,0},{8,12},{12,8},{16,20},{20,16},{24,28},{28,24},{1,5},{5... | collective-permute-start | bytes 1179656 | tf_op jit(solution)/shard_map/ppermute | solution.py:735
  17.5 12.4 %collective-permute-start = (bf16[768,256]{1,0:T(8,128)(2,1)S(1)}, bf16[768,256]{1,0:T(8,128)(2,1)S(1)}, u32[]{:S(2)}, u32[]{:S(2)}) collective-permute-start(bf16[768,256]{1,0:T(8,128)(2,1)S(1)} %get-tuple-element.327.refs_1_), channel_id=1, source_target_pairs={{0,8},{4,12},{8,16},{12,20},{16,24},{20,28},{24,0},{28,4},{1,9},{5... | collective-permute-start | bytes 1179656 | tf_op jit(solution)/shard_map/ppermute | solution.py:729
  31.4 21.5 %collective-permute-start.3 = (bf16[128,2048]{1,0:T(8,128)(2,1)S(1)}, bf16[128,2048]{1,0:T(8,128)(2,1)S(1)}, u32[]{:S(2)}, u32[]{:S(2)}) collective-permute-start(bf16[128,2048]{1,0:T(8,128)(2,1)S(1)} %get-tuple-element.602), channel_id=1, source_target_pairs={{0,2},{1,3},{2,0},{3,1},{4,6},{5,7},{6,4},{7,5},{8,10},{9,11},{10,... | collective-permute-start | bytes 1572872 | tf_op jit(solution)/shard_map/ppermute | solution.py:738
  33.0 19.9 %collective-permute-start.2 = (bf16[128,2048]{1,0:T(8,128)(2,1)S(1)}, bf16[128,2048]{1,0:T(8,128)(2,1)S(1)}, u32[]{:S(2)}, u32[]{:S(2)}) collective-permute-start(bf16[128,2048]{1,0:T(8,128)(2,1)S(1)} %get-tuple-element.603), channel_id=1, source_target_pairs={{0,4},{4,0},{8,12},{12,8},{16,20},{20,16},{24,28},{28,24},{1,5},{5... | collective-permute-start | bytes 1572872 | tf_op jit(solution)/shard_map/ppermute | solution.py:735
  33.5 18.3 %collective-permute-start.7 = (bf16[768,256]{1,0:T(8,128)(2,1)S(1)}, bf16[768,256]{1,0:T(8,128)(2,1)}, u32[]{:S(2)}, u32[]{:S(2)}) collective-permute-start(bf16[768,256]{1,0:T(8,128)(2,1)S(1)} %collective-permute-done.1.refs_2_), channel_id=1, source_target_pairs={{0,8},{4,12},{8,16},{12,20},{16,24},{20,28},{24,0},{28,4},{1,9},{5... | collective-permute-start | bytes 1179656 | tf_op jit(solution)/shard_map/ppermute | solution.py:729
  33.5 19.4 %collective-permute-start.6 = (bf16[768,256]{1,0:T(8,128)(2,1)S(1)}, bf16[768,256]{1,0:T(8,128)(2,1)S(1)}, u32[]{:S(2)}, u32[]{:S(2)}) collective-permute-start(bf16[768,256]{1,0:T(8,128)(2,1)S(1)} %collective-permute-done.refs_3_), channel_id=1, source_target_pairs={{0,8},{4,12},{8,16},{12,20},{16,24},{20,28},{24,0},{28,4},{1,9},{5... | collective-permute-start | bytes 1179656 | tf_op jit(solution)/shard_map/ppermute | solution.py:729
  34.8 13.2 %collective-permute-start.4 = (bf16[256,256]{1,0:T(8,128)(2,1)S(1)}, bf16[256,256]{1,0:T(8,128)(2,1)S(1)}, u32[]{:S(2)}, u32[]{:S(2)}) collective-permute-start(bf16[256,256]{1,0:T(8,128)(2,1)S(1)} %get-tuple-element.297), channel_id=1, source_target_pairs={{0,4},{4,0},{8,12},{12,8},{16,20},{20,16},{24,28},{28,24},{1,5},{5... | collective-permute-start | bytes 393224 | tf_op jit(solution)/shard_map/ppermute | solution.py:735
  53.1 25.7 %collective-permute-start.9 = (bf16[256,2048]{1,0:T(8,128)(2,1)S(1)}, bf16[256,2048]{1,0:T(8,128)(2,1)S(1)}, u32[]{:S(2)}, u32[]{:S(2)}) collective-permute-start(bf16[256,2048]{1,0:T(8,128)(2,1)S(1)} %pad_maximum_fusion.4.refs_3_), channel_id=1, source_target_pairs={{0,4},{4,0},{8,12},{12,8},{16,20},{20,16},{24,28},{28,24},{1,5},{5... | collective-permute-start | bytes 3145736 | tf_op jit(solution)/shard_map/ppermute | solution.py:735
  54.7 24.2 %collective-permute-start.8 = (bf16[256,2048]{1,0:T(8,128)(2,1)S(1)}, bf16[256,2048]{1,0:T(8,128)(2,1)}, u32[]{:S(2)}, u32[]{:S(2)}) collective-permute-start(bf16[256,2048]{1,0:T(8,128)(2,1)S(1)} %pad_maximum_fusion.3.refs_1_), channel_id=1, source_target_pairs={{0,2},{1,3},{2,0},{3,1},{4,6},{5,7},{6,4},{7,5},{8,10},{9,11},{10,... | collective-permute-start | bytes 3145736 | tf_op jit(solution)/shard_map/ppermute | solution.py:738
  55.2 19.3 %collective-permute-start.10 = (bf16[768,256]{1,0:T(8,128)(2,1)S(1)}, bf16[768,256]{1,0:T(8,128)(2,1)S(1)}, u32[]{:S(2)}, u32[]{:S(2)}) collective-permute-start(bf16[768,256]{1,0:T(8,128)(2,1)S(1)} %collective-permute-done.6.refs_5_), channel_id=1, source_target_pairs={{0,8},{4,12},{8,16},{12,20},{16,24},{20,28},{24,0},{28,4},{1,9},{5... | collective-permute-start | bytes 1179656 | tf_op jit(solution)/shard_map/ppermute | solution.py:729
  55.2 19.3 %collective-permute-start.12 = (bf16[512,256]{1,0:T(8,128)(2,1)S(1)}, bf16[512,256]{1,0:T(8,128)(2,1)S(1)}, u32[]{:S(2)}, u32[]{:S(2)}) collective-permute-start(bf16[512,256]{1,0:T(8,128)(2,1)S(1)} %pad_maximum_fusion.12.refs_1_), channel_id=1, source_target_pairs={{0,8},{4,12},{8,16},{12,20},{16,24},{20,28},{24,0},{28,4},{1,9},{5... | collective-permute-start | bytes 786440 | tf_op jit(solution)/shard_map/ppermute | solution.py:729
  55.3 23.5 %collective-permute-start.11 = (bf16[768,256]{1,0:T(8,128)(2,1)}, bf16[768,256]{1,0:T(8,128)(2,1)}, u32[]{:S(2)}, u32[]{:S(2)}) collective-permute-start(bf16[768,256]{1,0:T(8,128)(2,1)} %collective-permute-done.7.refs_4_), channel_id=1, source_target_pairs={{0,8},{4,12},{8,16},{12,20},{16,24},{20,28},{24,0},{28,4},{1,9},{5... | collective-permute-start | bytes 1179656 | tf_op jit(solution)/shard_map/ppermute | solution.py:729
  79.3 19.6 %collective-permute-start.19 = (bf16[1408,256]{1,0:T(8,128)(2,1)}, bf16[1408,256]{1,0:T(8,128)(2,1)}, u32[]{:S(2)}, u32[]{:S(2)}) collective-permute-start(bf16[1408,256]{1,0:T(8,128)(2,1)} %copy-done.117), channel_id=1, source_target_pairs={{0,4},{4,0},{8,12},{12,8},{16,20},{20,16},{24,28},{28,24},{1,5},{5... | collective-permute-start | bytes 2162696 | tf_op jit(solution)/shard_map/ppermute | solution.py:735
  80.4 18.5 %collective-permute-start.17 = (bf16[768,256]{1,0:T(8,128)(2,1)}, bf16[768,256]{1,0:T(8,128)(2,1)}, u32[]{:S(2)}, u32[]{:S(2)}) collective-permute-start(bf16[768,256]{1,0:T(8,128)(2,1)} %collective-permute-done.11.refs_6_), channel_id=1, source_target_pairs={{0,8},{4,12},{8,16},{12,20},{16,24},{20,28},{24,0},{28,4},{1,9},{5... | collective-permute-start | bytes 1179656 | tf_op jit(solution)/shard_map/ppermute | solution.py:729
  80.4 18.5 %collective-permute-start.18 = (bf16[512,256]{1,0:T(8,128)(2,1)}, bf16[512,256]{1,0:T(8,128)(2,1)}, u32[]{:S(2)}, u32[]{:S(2)}) collective-permute-start(bf16[512,256]{1,0:T(8,128)(2,1)} %copy-done.110), channel_id=1, source_target_pairs={{0,8},{4,12},{8,16},{12,20},{16,24},{20,28},{24,0},{28,4},{1,9},{5... | collective-permute-start | bytes 786440 | tf_op jit(solution)/shard_map/ppermute | solution.py:729
  101.3 129.5 %all-gather.9.cloned.1.call-start = ((), (), s32[]{:S(2)}) async-start(), calls=%async_computation.11 | async-start | bytes 3604480 | tf_op jit(solution)/shard_map/all_gather | solution.py:1018
  102.5 17.1 %collective-permute-start.21 = (bf16[128,2048]{1,0:T(8,128)(2,1)S(1)}, bf16[128,2048]{1,0:T(8,128)(2,1)S(1)}, u32[]{:S(2)}, u32[]{:S(2)}) collective-permute-start(bf16[128,2048]{1,0:T(8,128)(2,1)S(1)} %get-tuple-element.600), channel_id=1, source_target_pairs={{0,2},{1,3},{2,0},{3,1},{4,6},{5,7},{6,4},{7,5},{8,10},{9,11},{10,... | collective-permute-start | bytes 1572872 | tf_op jit(solution)/shard_map/ppermute | solution.py:738
  103.5 16.0 %collective-permute-start.20 = (bf16[128,2048]{1,0:T(8,128)(2,1)S(1)}, bf16[128,2048]{1,0:T(8,128)(2,1)S(1)}, u32[]{:S(2)}, u32[]{:S(2)}) collective-permute-start(bf16[128,2048]{1,0:T(8,128)(2,1)S(1)} %get-tuple-element.601), channel_id=1, source_target_pairs={{0,4},{4,0},{8,12},{12,8},{16,20},{20,16},{24,28},{28,24},{1,5},{5... | collective-permute-start | bytes 1572872 | tf_op jit(solution)/shard_map/ppermute | solution.py:735
  120.8 23.9 %collective-permute-start.23 = (bf16[256,2048]{1,0:T(8,128)(2,1)S(1)}, bf16[256,2048]{1,0:T(8,128)(2,1)}, u32[]{:S(2)}, u32[]{:S(2)}) collective-permute-start(bf16[256,2048]{1,0:T(8,128)(2,1)S(1)} %pad_maximum_fusion.6.refs_3_), channel_id=1, source_target_pairs={{0,4},{4,0},{8,12},{12,8},{16,20},{20,16},{24,28},{28,24},{1,5},{5... | collective-permute-start | bytes 3145736 | tf_op jit(solution)/shard_map/ppermute | solution.py:735
  121.6 23.9 %collective-permute-start.22 = (bf16[256,2048]{1,0:T(8,128)(2,1)}, bf16[256,2048]{1,0:T(8,128)(2,1)}, u32[]{:S(2)}, u32[]{:S(2)}) collective-permute-start(bf16[256,2048]{1,0:T(8,128)(2,1)} %pad_maximum_fusion.5.refs_1_), channel_id=1, source_target_pairs={{0,2},{1,3},{2,0},{3,1},{4,6},{5,7},{6,4},{7,5},{8,10},{9,11},{10,... | collective-permute-start | bytes 3145736 | tf_op jit(solution)/shard_map/ppermute | solution.py:738
  123.1 15.8 %collective-permute-start.24 = (bf16[512,256]{1,0:T(8,128)(2,1)}, bf16[512,256]{1,0:T(8,128)(2,1)S(1)}, u32[]{:S(2)}, u32[]{:S(2)}) collective-permute-start(bf16[512,256]{1,0:T(8,128)(2,1)} %collective-permute-done.18.refs_3_), channel_id=1, source_target_pairs={{0,8},{4,12},{8,16},{12,20},{16,24},{20,28},{24,0},{28,4},{1,9},{5... | collective-permute-start | bytes 786440 | tf_op jit(solution)/shard_map/ppermute | solution.py:729
  150.5 14.8 %collective-permute-start.32 = (bf16[256,2048]{1,0:T(8,128)(2,1)S(1)}, bf16[256,2048]{1,0:T(8,128)(2,1)S(1)}, u32[]{:S(2)}, u32[]{:S(2)}) collective-permute-start(bf16[256,2048]{1,0:T(8,128)(2,1)S(1)} %pad_maximum_fusion.6.refs_3_), channel_id=1, source_target_pairs={{0,1},{1,0},{2,3},{3,2},{4,5},{5,4},{6,7},{7,6},{8,9},{9,8},{10,11... | collective-permute-start | bytes 3145736 | tf_op jit(solution)/shard_map/ppermute | solution.py:741
  152.1 15.3 %collective-permute-start.31 = (bf16[256,2048]{1,0:T(8,128)(2,1)}, bf16[256,2048]{1,0:T(8,128)(2,1)}, u32[]{:S(2)}, u32[]{:S(2)}) collective-permute-start(bf16[256,2048]{1,0:T(8,128)(2,1)} %pad_maximum_fusion.5.refs_1_), channel_id=1, source_target_pairs={{0,1},{1,0},{2,3},{3,2},{4,5},{5,4},{6,7},{7,6},{8,9},{9,8},{10,11... | collective-permute-start | bytes 3145736 | tf_op jit(solution)/shard_map/ppermute | solution.py:741
  164.4 25.5 %collective-permute-start.30 = (bf16[256,2048]{1,0:T(8,128)(2,1)}, bf16[256,2048]{1,0:T(8,128)(2,1)}, u32[]{:S(2)}, u32[]{:S(2)}) collective-permute-start(bf16[256,2048]{1,0:T(8,128)(2,1)} %get-tuple-element.357), channel_id=1, source_target_pairs={{0,2},{1,3},{2,0},{3,1},{4,6},{5,7},{6,4},{7,5},{8,10},{9,11},{10,... | collective-permute-start | bytes 3145736 | tf_op jit(solution)/shard_map/ppermute | solution.py:738
  166.2 25.2 %collective-permute-start.29 = (bf16[256,2048]{1,0:T(8,128)(2,1)}, bf16[256,2048]{1,0:T(8,128)(2,1)}, u32[]{:S(2)}, u32[]{:S(2)}) collective-permute-start(bf16[256,2048]{1,0:T(8,128)(2,1)} %get-tuple-element.355), channel_id=1, source_target_pairs={{0,4},{4,0},{8,12},{12,8},{16,20},{20,16},{24,28},{28,24},{1,5},{5... | collective-permute-start | bytes 3145736 | tf_op jit(solution)/shard_map/ppermute | solution.py:735
  167.4 128.0 %all-gather.11.cloned.1.call-start = ((), (), s32[]{:S(2)}) async-start(), calls=%async_computation.12 | async-start | bytes 3604480 | tf_op jit(solution)/shard_map/all_gather | solution.py:1018
  194.4 12.9 %collective-permute-start.36 = (bf16[128,2048]{1,0:T(8,128)(2,1)S(1)}, bf16[128,2048]{1,0:T(8,128)(2,1)S(1)}, u32[]{:S(2)}, u32[]{:S(2)}) collective-permute-start(bf16[128,2048]{1,0:T(8,128)(2,1)S(1)} %add_convert_fusion.6), channel_id=1, source_target_pairs={{0,4},{4,0},{8,12},{12,8},{16,20},{20,16},{24,28},{28,24},{1,5},{5... | collective-permute-start | bytes 1572872 | tf_op jit(solution)/shard_map/ppermute | solution.py:735
  195.5 12.5 %collective-permute-start.35 = (bf16[128,2048]{1,0:T(8,128)(2,1)S(1)}, bf16[128,2048]{1,0:T(8,128)(2,1)S(1)}, u32[]{:S(2)}, u32[]{:S(2)}) collective-permute-start(bf16[128,2048]{1,0:T(8,128)(2,1)S(1)} %add_convert_fusion.7), channel_id=1, source_target_pairs={{0,2},{1,3},{2,0},{3,1},{4,6},{5,7},{6,4},{7,5},{8,10},{9,11},{10,... | collective-permute-start | bytes 1572872 | tf_op jit(solution)/shard_map/ppermute | solution.py:738
  212.5 11.8 %collective-permute-start.39 = (bf16[128,2048]{1,0:T(8,128)(2,1)S(1)}, bf16[128,2048]{1,0:T(8,128)(2,1)S(1)}, u32[]{:S(2)}, u32[]{:S(2)}) collective-permute-start(bf16[128,2048]{1,0:T(8,128)(2,1)S(1)} %get-tuple-element.598), channel_id=1, source_target_pairs={{0,2},{1,3},{2,0},{3,1},{4,6},{5,7},{6,4},{7,5},{8,10},{9,11},{10,... | collective-permute-start | bytes 1572872 | tf_op jit(solution)/shard_map/ppermute | solution.py:738
  213.8 14.9 %collective-permute-start.38 = (bf16[128,2048]{1,0:T(8,128)(2,1)S(1)}, bf16[128,2048]{1,0:T(8,128)(2,1)S(1)}, u32[]{:S(2)}, u32[]{:S(2)}) collective-permute-start(bf16[128,2048]{1,0:T(8,128)(2,1)S(1)} %get-tuple-element.599), channel_id=1, source_target_pairs={{0,4},{4,0},{8,12},{12,8},{16,20},{20,16},{24,28},{28,24},{1,5},{5... | collective-permute-start | bytes 1572872 | tf_op jit(solution)/shard_map/ppermute | solution.py:735
  214.7 18.4 %collective-permute-start.37 = (bf16[704,256]{1,0:T(8,128)(2,1)}, bf16[704,256]{1,0:T(8,128)(2,1)}, u32[]{:S(2)}, u32[]{:S(2)}) collective-permute-start(bf16[704,256]{1,0:T(8,128)(2,1)} %get-tuple-element.374), channel_id=1, source_target_pairs={{0,4},{4,0},{8,12},{12,8},{16,20},{20,16},{24,28},{28,24},{1,5},{5... | collective-permute-start | bytes 1081352 | tf_op jit(solution)/shard_map/ppermute | solution.py:735
  235.3 172.0 %reduce-scatter.6.cloned.1.call-start = ((), (), s32[]{:S(2)}) async-start(), calls=%async_computation.5 | async-start | bytes 3604480 | tf_op jit(solution)/shard_map/reduce_scatter | solution.py:1072
  235.4 22.0 %collective-permute-start.41 = (bf16[256,2048]{1,0:T(8,128)(2,1)}, bf16[256,2048]{1,0:T(8,128)(2,1)S(1)}, u32[]{:S(2)}, u32[]{:S(2)}) collective-permute-start(bf16[256,2048]{1,0:T(8,128)(2,1)} %pad_maximum_fusion.8.refs_3_), channel_id=1, source_target_pairs={{0,4},{4,0},{8,12},{12,8},{16,20},{20,16},{24,28},{28,24},{1,5},{5... | collective-permute-start | bytes 3145736 | tf_op jit(solution)/shard_map/ppermute | solution.py:735
  236.3 21.7 %collective-permute-start.40 = (bf16[256,2048]{1,0:T(8,128)(2,1)}, bf16[256,2048]{1,0:T(8,128)(2,1)S(1)}, u32[]{:S(2)}, u32[]{:S(2)}) collective-permute-start(bf16[256,2048]{1,0:T(8,128)(2,1)} %pad_maximum_fusion.7.refs_1_), channel_id=1, source_target_pairs={{0,2},{1,3},{2,0},{3,1},{4,6},{5,7},{6,4},{7,5},{8,10},{9,11},{10,... | collective-permute-start | bytes 3145736 | tf_op jit(solution)/shard_map/ppermute | solution.py:738
  238.5 20.1 %collective-permute-start.43 = (bf16[256,2048]{1,0:T(8,128)(2,1)}, bf16[256,2048]{1,0:T(8,128)(2,1)S(1)}, u32[]{:S(2)}, u32[]{:S(2)}) collective-permute-start(bf16[256,2048]{1,0:T(8,128)(2,1)} %pad_maximum_fusion.8.refs_3_), channel_id=1, source_target_pairs={{0,1},{1,0},{2,3},{3,2},{4,5},{5,4},{6,7},{7,6},{8,9},{9,8},{10,11... | collective-permute-start | bytes 3145736 | tf_op jit(solution)/shard_map/ppermute | solution.py:741
  238.5 20.0 %collective-permute-start.42 = (bf16[256,2048]{1,0:T(8,128)(2,1)}, bf16[256,2048]{1,0:T(8,128)(2,1)S(1)}, u32[]{:S(2)}, u32[]{:S(2)}) collective-permute-start(bf16[256,2048]{1,0:T(8,128)(2,1)} %pad_maximum_fusion.7.refs_1_), channel_id=1, source_target_pairs={{0,1},{1,0},{2,3},{3,2},{4,5},{5,4},{6,7},{7,6},{8,9},{9,8},{10,11... | collective-permute-start | bytes 3145736 | tf_op jit(solution)/shard_map/ppermute | solution.py:741
  295.1 140.1 %reduce-scatter.8.cloned.1.call-start = ((), (), s32[]{:S(2)}) async-start(), calls=%async_computation.6 | async-start | bytes 3604480 | tf_op jit(solution)/shard_map/reduce_scatter | solution.py:1072
  340.8 25.5 %collective-permute-start.51 = (bf16[256,2048]{1,0:T(8,128)(2,1)}, bf16[256,2048]{1,0:T(8,128)(2,1)}, u32[]{:S(2)}, u32[]{:S(2)}) collective-permute-start(bf16[256,2048]{1,0:T(8,128)(2,1)} %get-tuple-element.420), channel_id=1, source_target_pairs={{0,2},{1,3},{2,0},{3,1},{4,6},{5,7},{6,4},{7,5},{8,10},{9,11},{10,... | collective-permute-start | bytes 3145736 | tf_op jit(solution)/shard_map/ppermute | solution.py:738
  341.2 25.2 %collective-permute-start.50 = (bf16[256,2048]{1,0:T(8,128)(2,1)}, bf16[256,2048]{1,0:T(8,128)(2,1)}, u32[]{:S(2)}, u32[]{:S(2)}) collective-permute-start(bf16[256,2048]{1,0:T(8,128)(2,1)} %get-tuple-element.418), channel_id=1, source_target_pairs={{0,4},{4,0},{8,12},{12,8},{16,20},{20,16},{24,28},{28,24},{1,5},{5... | collective-permute-start | bytes 3145736 | tf_op jit(solution)/shard_map/ppermute | solution.py:735
  370.5 151.9 %reduce-scatter.10.cloned.1.call-start = ((), (), s32[]{:S(2)}) async-start(), calls=%async_computation.7 | async-start | bytes 3604480 | tf_op jit(solution)/shard_map/reduce_scatter | solution.py:1072
  370.6 13.5 %collective-permute-start.57 = (bf16[128,2048]{1,0:T(8,128)(2,1)}, bf16[128,2048]{1,0:T(8,128)(2,1)}, u32[]{:S(2)}, u32[]{:S(2)}) collective-permute-start(bf16[128,2048]{1,0:T(8,128)(2,1)} %add_convert_fusion.4), channel_id=1, source_target_pairs={{0,4},{4,0},{8,12},{12,8},{16,20},{20,16},{24,28},{28,24},{1,5},{5... | collective-permute-start | bytes 1572872 | tf_op jit(solution)/shard_map/ppermute | solution.py:735
  371.8 12.8 %collective-permute-start.56 = (bf16[128,2048]{1,0:T(8,128)(2,1)}, bf16[128,2048]{1,0:T(8,128)(2,1)}, u32[]{:S(2)}, u32[]{:S(2)}) collective-permute-start(bf16[128,2048]{1,0:T(8,128)(2,1)} %add_convert_fusion.5), channel_id=1, source_target_pairs={{0,2},{1,3},{2,0},{3,1},{4,6},{5,7},{6,4},{7,5},{8,10},{9,11},{10,... | collective-permute-start | bytes 1572872 | tf_op jit(solution)/shard_map/ppermute | solution.py:738
  373.0 197.6 %reduce-scatter.14.cloned.1.call-start = ((), (), s32[]{:S(2)}) async-start(), calls=%async_computation.9 | async-start | bytes 1310720 | tf_op jit(solution)/shard_map/reduce_scatter | solution.py:1072
  382.1 12.8 %collective-permute-start.55 = (bf16[256,2048]{1,0:T(8,128)(2,1)S(1)}, bf16[256,2048]{1,0:T(8,128)(2,1)S(1)}, u32[]{:S(2)}, u32[]{:S(2)}) collective-permute-start(bf16[256,2048]{1,0:T(8,128)(2,1)S(1)} %get-tuple-element.434), channel_id=1, source_target_pairs={{0,1},{1,0},{2,3},{3,2},{4,5},{5,4},{6,7},{7,6},{8,9},{9,8},{10,11... | collective-permute-start | bytes 3145736 | tf_op jit(solution)/shard_map/ppermute | solution.py:741
  382.6 12.3 %collective-permute-start.54 = (bf16[256,2048]{1,0:T(8,128)(2,1)S(1)}, bf16[256,2048]{1,0:T(8,128)(2,1)S(1)}, u32[]{:S(2)}, u32[]{:S(2)}) collective-permute-start(bf16[256,2048]{1,0:T(8,128)(2,1)S(1)} %get-tuple-element.432), channel_id=1, source_target_pairs={{0,1},{1,0},{2,3},{3,2},{4,5},{5,4},{6,7},{7,6},{8,9},{9,8},{10,11... | collective-permute-start | bytes 3145736 | tf_op jit(solution)/shard_map/ppermute | solution.py:741
  392.3 13.8 %collective-permute-start.59 = (bf16[128,2048]{1,0:T(8,128)(2,1)S(1)}, bf16[128,2048]{1,0:T(8,128)(2,1)S(1)}, u32[]{:S(2)}, u32[]{:S(2)}) collective-permute-start(bf16[128,2048]{1,0:T(8,128)(2,1)S(1)} %get-tuple-element.596), channel_id=1, source_target_pairs={{0,2},{1,3},{2,0},{3,1},{4,6},{5,7},{6,4},{7,5},{8,10},{9,11},{10,... | collective-permute-start | bytes 1572872 | tf_op jit(solution)/shard_map/ppermute | solution.py:738
  393.6 13.7 %collective-permute-start.58 = (bf16[128,2048]{1,0:T(8,128)(2,1)S(1)}, bf16[128,2048]{1,0:T(8,128)(2,1)}, u32[]{:S(2)}, u32[]{:S(2)}) collective-permute-start(bf16[128,2048]{1,0:T(8,128)(2,1)S(1)} %get-tuple-element.597), channel_id=1, source_target_pairs={{0,4},{4,0},{8,12},{12,8},{16,20},{20,16},{24,28},{28,24},{1,5},{5... | collective-permute-start | bytes 1572872 | tf_op jit(solution)/shard_map/ppermute | solution.py:735
  410.8 24.3 %collective-permute-start.61 = (bf16[256,2048]{1,0:T(8,128)(2,1)}, bf16[256,2048]{1,0:T(8,128)(2,1)}, u32[]{:S(2)}, u32[]{:S(2)}) collective-permute-start(bf16[256,2048]{1,0:T(8,128)(2,1)} %pad_maximum_fusion.10.refs_3_), channel_id=1, source_target_pairs={{0,4},{4,0},{8,12},{12,8},{16,20},{20,16},{24,28},{28,24},{1,5},{5... | collective-permute-start | bytes 3145736 | tf_op jit(solution)/shard_map/ppermute | solution.py:735
  411.5 23.7 %collective-permute-start.60 = (bf16[256,2048]{1,0:T(8,128)(2,1)}, bf16[256,2048]{1,0:T(8,128)(2,1)}, u32[]{:S(2)}, u32[]{:S(2)}) collective-permute-start(bf16[256,2048]{1,0:T(8,128)(2,1)} %pad_maximum_fusion.9.refs_1_), channel_id=1, source_target_pairs={{0,2},{1,3},{2,0},{3,1},{4,6},{5,7},{6,4},{7,5},{8,10},{9,11},{10,... | collective-permute-start | bytes 3145736 | tf_op jit(solution)/shard_map/ppermute | solution.py:738
  412.5 24.8 %collective-permute-start.67 = (bf16[256,2048]{1,0:T(8,128)(2,1)}, bf16[256,2048]{1,0:T(8,128)(2,1)}, u32[]{:S(2)}, u32[]{:S(2)}) collective-permute-start(bf16[256,2048]{1,0:T(8,128)(2,1)} %pad_maximum_fusion.10.refs_3_), channel_id=1, source_target_pairs={{0,1},{1,0},{2,3},{3,2},{4,5},{5,4},{6,7},{7,6},{8,9},{9,8},{10,11... | collective-permute-start | bytes 3145736 | tf_op jit(solution)/shard_map/ppermute | solution.py:741
  412.5 29.4 %collective-permute-start.66 = (bf16[256,2048]{1,0:T(8,128)(2,1)}, bf16[256,2048]{1,0:T(8,128)(2,1)}, u32[]{:S(2)}, u32[]{:S(2)}) collective-permute-start(bf16[256,2048]{1,0:T(8,128)(2,1)} %pad_maximum_fusion.9.refs_1_), channel_id=1, source_target_pairs={{0,1},{1,0},{2,3},{3,2},{4,5},{5,4},{6,7},{7,6},{8,9},{9,8},{10,11... | collective-permute-start | bytes 3145736 | tf_op jit(solution)/shard_map/ppermute | solution.py:741
  435.7 62.7 %collective-permute-start.62 = (bf16[256,2048]{1,0:T(8,128)(2,1)}, bf16[256,2048]{1,0:T(8,128)(2,1)}, u32[]{:S(2)}, u32[]{:S(2)}) collective-permute-start(bf16[256,2048]{1,0:T(8,128)(2,1)} %copy-done.116), channel_id=1, source_target_pairs={{0,4},{4,0},{8,12},{12,8},{16,20},{20,16},{24,28},{28,24},{1,5},{5... | collective-permute-start | bytes 3145736 | tf_op jit(solution)/shard_map/ppermute | solution.py:735
  437.3 61.0 %collective-permute-start.63 = (bf16[256,2048]{1,0:T(8,128)(2,1)}, bf16[256,2048]{1,0:T(8,128)(2,1)}, u32[]{:S(2)}, u32[]{:S(2)}) collective-permute-start(bf16[256,2048]{1,0:T(8,128)(2,1)} %copy-done.115), channel_id=1, source_target_pairs={{0,2},{1,3},{2,0},{3,1},{4,6},{5,7},{6,4},{7,5},{8,10},{9,11},{10,... | collective-permute-start | bytes 3145736 | tf_op jit(solution)/shard_map/ppermute | solution.py:738
  455.6 120.3 %reduce-scatter.12.cloned.1.call-start = ((), (), s32[]{:S(2)}) async-start(), calls=%async_computation.8 | async-start | bytes 3932160 | tf_op jit(solution)/shard_map/reduce_scatter | solution.py:1072
  455.9 41.0 %collective-permute-start.64 = (bf16[704,256]{1,0:T(8,128)(2,1)}, bf16[704,256]{1,0:T(8,128)(2,1)S(1)}, u32[]{:S(2)}, u32[]{:S(2)}) collective-permute-start(bf16[704,256]{1,0:T(8,128)(2,1)} %copy-done.118), channel_id=1, source_target_pairs={{0,4},{4,0},{8,12},{12,8},{16,20},{20,16},{24,28},{28,24},{1,5},{5... | collective-permute-start | bytes 1081352 | tf_op jit(solution)/shard_map/ppermute | solution.py:735
  456.2 41.5 %collective-permute-start.65 = (bf16[704,256]{1,0:T(8,128)(2,1)}, bf16[704,256]{1,0:T(8,128)(2,1)S(1)}, u32[]{:S(2)}, u32[]{:S(2)}) collective-permute-start(bf16[704,256]{1,0:T(8,128)(2,1)} %copy-done.119), channel_id=1, source_target_pairs={{0,4},{4,0},{8,12},{12,8},{16,20},{20,16},{24,28},{28,24},{1,5},{5... | collective-permute-start | bytes 1081352 | tf_op jit(solution)/shard_map/ppermute | solution.py:735
  521.4 25.4 %collective-permute-start.75 = (bf16[256,2048]{1,0:T(8,128)(2,1)}, bf16[256,2048]{1,0:T(8,128)(2,1)}, u32[]{:S(2)}, u32[]{:S(2)}) collective-permute-start(bf16[256,2048]{1,0:T(8,128)(2,1)} %get-tuple-element.494), channel_id=1, source_target_pairs={{0,2},{1,3},{2,0},{3,1},{4,6},{5,7},{6,4},{7,5},{8,10},{9,11},{10,... | collective-permute-start | bytes 3145736 | tf_op jit(solution)/shard_map/ppermute | solution.py:738
  522.0 25.2 %collective-permute-start.74 = (bf16[256,2048]{1,0:T(8,128)(2,1)}, bf16[256,2048]{1,0:T(8,128)(2,1)}, u32[]{:S(2)}, u32[]{:S(2)}) collective-permute-start(bf16[256,2048]{1,0:T(8,128)(2,1)} %get-tuple-element.492), channel_id=1, source_target_pairs={{0,4},{4,0},{8,12},{12,8},{16,20},{20,16},{24,28},{28,24},{1,5},{5... | collective-permute-start | bytes 3145736 | tf_op jit(solution)/shard_map/ppermute | solution.py:735
  549.3 16.3 %collective-permute-start.80 = (bf16[128,2048]{1,0:T(8,128)(2,1)}, bf16[128,2048]{1,0:T(8,128)(2,1)}, u32[]{:S(2)}, u32[]{:S(2)}) collective-permute-start(bf16[128,2048]{1,0:T(8,128)(2,1)} %add_convert_fusion.2), channel_id=1, source_target_pairs={{0,4},{4,0},{8,12},{12,8},{16,20},{20,16},{24,28},{28,24},{1,5},{5... | collective-permute-start | bytes 1572872 | tf_op jit(solution)/shard_map/ppermute | solution.py:735
  551.6 14.0 %collective-permute-start.79 = (bf16[128,2048]{1,0:T(8,128)(2,1)}, bf16[128,2048]{1,0:T(8,128)(2,1)}, u32[]{:S(2)}, u32[]{:S(2)}) collective-permute-start(bf16[128,2048]{1,0:T(8,128)(2,1)} %add_convert_fusion.3), channel_id=1, source_target_pairs={{0,2},{1,3},{2,0},{3,1},{4,6},{5,7},{6,4},{7,5},{8,10},{9,11},{10,... | collective-permute-start | bytes 1572872 | tf_op jit(solution)/shard_map/ppermute | solution.py:738
  560.8 44.5 %collective-permute-start.78 = (bf16[128,2048]{1,0:T(8,128)(2,1)}, bf16[128,2048]{1,0:T(8,128)(2,1)}, u32[]{:S(2)}, u32[]{:S(2)}) collective-permute-start(bf16[128,2048]{1,0:T(8,128)(2,1)} %add_convert_fusion), channel_id=1, source_target_pairs={{0,4},{4,0},{8,12},{12,8},{16,20},{20,16},{24,28},{28,24},{1,5},{5... | collective-permute-start | bytes 1572872 | tf_op jit(solution)/shard_map/ppermute | solution.py:735
  562.6 42.7 %collective-permute-start.77 = (bf16[128,2048]{1,0:T(8,128)(2,1)}, bf16[128,2048]{1,0:T(8,128)(2,1)}, u32[]{:S(2)}, u32[]{:S(2)}) collective-permute-start(bf16[128,2048]{1,0:T(8,128)(2,1)} %add_convert_fusion.1), channel_id=1, source_target_pairs={{0,2},{1,3},{2,0},{3,1},{4,6},{5,7},{6,4},{7,5},{8,10},{9,11},{10,... | collective-permute-start | bytes 1572872 | tf_op jit(solution)/shard_map/ppermute | solution.py:738
  564.1 29.8 %collective-permute-start.90 = (bf16[704,256]{1,0:T(8,128)(2,1)}, bf16[704,256]{1,0:T(8,128)(2,1)}, u32[]{:S(2)}, u32[]{:S(2)}) collective-permute-start(bf16[704,256]{1,0:T(8,128)(2,1)} %get-tuple-element.538), channel_id=1, source_target_pairs={{0,4},{4,0},{8,12},{12,8},{16,20},{20,16},{24,28},{28,24},{1,5},{5... | collective-permute-start | bytes 1081352 | tf_op jit(solution)/shard_map/ppermute | solution.py:735
  (208 other events, 1329.0 us)
Sparse Core Ops, SparseCore 0:
  101.4 62.3 all-gather.6
  167.5 56.4 all-gather.8
  235.4 56.1 all-gather.10
  295.2 53.4 reduce-scatter.5
  370.6 53.7 reduce-scatter.7
  426.6 56.0 reduce-scatter.9
  485.5 26.9 reduce-scatter.13
  514.9 60.9 reduce-scatter.11
